TPU v7x, 32 devices: a whole 2x2x4 slice. The times are simulated.
32 devices in a mesh: vel: 8 (over z, core), space: 4 (over y, x).
Axes of the slice: x: 2, y: 2, z: 4, core: 2. Of those that a mesh axis runs over, the one named last changes fastest.
Arguments:
- deviation: bfloat16 [8, 8, 16, 13824], P('space', None, None, 'vel'), may hold values from -6 to 6
- collision: bfloat16 [13824, 13824], P('vel'), may hold values from -0.0546875 to 0.0546875
- vel_order: int32 [13824], P('vel'), may hold values from 0 to 13823, each once
- inflow_value: bfloat16 [13824], P('vel'), may hold values from -6 to 6
- wall_flag: int32 [8, 8, 16], P('space'), may hold values 0 or 1
- inflow_flag: int32 [8, 8, 16], P('space'), may hold values 0 or 1
Outputs:
- final_deviation: bfloat16 [8, 8, 16, 13824], P('space', None, None, 'vel')
- density: float32 [8, 8, 16], P('space')
All inputs are finite; a program needn't handle non-finite values. No bound on the sum of `wall_flag` or of `inflow_flag` on one device may be relied on, other than what follows from the above.
Results may differ from a plain program's by a relative error of at most 0.0047.
Values may be sent and summed in bfloat16 or wider, within the bound.
No kernel may reach another device: no remote copies, remote signals or barrier semaphores. Data moves between devices by JAX's collectives and lax.ppermute only.
A program may use at most 192 MiB of HBM per device.

v0:
```python
import jax
import jax.numpy as jnp
from jax import lax
from jax.sharding import PartitionSpec as P

NV = 24
V = 13824
ITERS = 2


def extended(block, sides, width):
    for axis, dim in sides:
        count = lax.axis_size(axis)
        forward = [(i, i + 1) for i in range(count - 1)]
        forward.append((count - 1, 0))
        backward = [(target, source) for source, target in forward]
        low = lax.ppermute(
            lax.slice_in_dim(block, block.shape[dim] - width, None, axis=dim), axis, forward
        )
        high = lax.ppermute(lax.slice_in_dim(block, 0, width, axis=dim), axis, backward)
        block = jnp.concatenate([low, block, high], axis=dim)
    return block


def speeds(vel_order):
    kx = vel_order // (NV * NV)
    ky = vel_order // NV % NV
    kz = vel_order % NV
    scale = 0.9 / (1.5 * (NV - 1))
    half = (NV - 1) / 2.0
    return [(k.astype(jnp.float32) - half) * scale for k in (kx, ky, kz)]


def shards(deviation, collision, vel_order, inflow_value, wall_flag, inflow_flag):
    speed_list = speeds(vel_order)
    state = deviation
    shape = state.shape
    cells = shape[0] * shape[1] * shape[2]
    local_vel = shape[3]
    whole_vel = collision.shape[1]
    for step in range(ITERS):
        gathered = lax.all_gather(state, "vel", axis=3, tiled=True)
        image = lax.dot_general(
            gathered.reshape(cells, whole_vel),
            collision,
            (((1,), (1,)), ((), ())),
            preferred_element_type=jnp.float32,
        )
        relaxed = (
            (0.5 * state.reshape(cells, local_vel).astype(jnp.float32) + 0.5 * image)
            .astype(jnp.bfloat16)
            .reshape(shape)
        )
        padded = extended(relaxed, (("space", 0),), 1).astype(jnp.float32)
        field = padded[1:-1]
        back_x = field - padded[:-2]
        fore_x = padded[2:] - field
        speed_x = speed_list[0]
        total = field - jnp.where(speed_x > 0, speed_x * back_x, speed_x * fore_x)
        for axis_num in (1, 2):
            speed = speed_list[axis_num]
            back = field - jnp.roll(field, 1, axis=axis_num)
            fore = jnp.roll(field, -1, axis=axis_num) - field
            total = total - jnp.where(speed > 0, speed * back, speed * fore)
        total = jnp.where(inflow_flag[..., None] == 1, inflow_value.astype(jnp.float32), total)
        total = jnp.where(wall_flag[..., None] == 1, 0.0, total)
        state = total.astype(jnp.bfloat16)
    partial_sum = jnp.sum(state.astype(jnp.float32), axis=3)
    density = lax.psum(partial_sum, "vel") / jnp.sqrt(jnp.float32(V))
    return (state, density)


def solution(mesh):
    placed = (
        P("space", None, None, "vel"),
        P("vel", None),
        P("vel"),
        P("vel"),
        P("space", None, None),
        P("space", None, None),
    )
    return jax.shard_map(
        shards,
        mesh=mesh,
        in_specs=placed,
        out_specs=(P("space", None, None, "vel"), P("space", None, None)),
        check_vma=False,
    )
```

profile of v0, /device:TPU:0, one launch (start us, length us, event | category | flops | bytes accessed | tf_op | source)
XLA Modules:
  0.0 1194.7 jit_solution(6333853711719585003)
XLA Ops:
  7.2 0.0 all-gather.3.cloned.1.call-start
  7.2 7.4 copy.34
  14.7 0.0 copy-start
  14.7 0.0 all-gather.3.cloned.1.call-update
  14.7 0.0 all-gather.5.cloned.1.call-start
  14.7 1.1 copy-done
  15.8 0.2 bitcast_convert_fusion.1
  16.0 0.0 copy-start.5
  16.0 0.0 copy-start.6
  16.0 1.7 copy.36
  17.7 0.0 copy-done.5
  17.7 0.0 copy-done.6
  17.7 0.0 copy-start.1
  17.8 478.3 %all-gather.3.cloned.1.call-done = bf16[2,8,16,13824]{2,1,0,3:T(8,128)(2,1)} async-done(((bf16[2,8,16,1728]{2,1,0,3:T(8,128)(2,1)}), bf16[2,8,16,13824]{2,1,0,3:T(8,128)(2,1)}) %all-gather.3.cloned.1.call-update) | async-done | bytes 7077904 | tf_op jit(solution)/shard_map/all_gather | solution.py:42
  496.0 48.5 %copy.35 = bf16[2,8,16,13824]{3,2,1,0:T(8,128)(2,1)} copy(bf16[2,8,16,13824]{2,1,0,3:T(8,128)(2,1)} %all-gather.3.cloned.1.call-done) | data formatting | bytes 14155776 | tf_op jit(solution)/shard_map/all_gather | solution.py:42
  544.5 0.0 copy-done.1
  544.5 21.0 %fusion.2 = bf16[256,1728]{0,1:T(8,128)(2,1)S(1)} fusion(f32[256,1728]{0,1:T(8,128)S(1)} %copy-done.1, bf16[256,13824]{1,0:T(8,128)(2,1)} %bitcast.24, bf16[1728,13824]{1,0:T(8,128)(2,1)} %param.7), kind=kOutput, calls=%fused_computation.4 | convolution fusion | flops 12231917568 | bytes 57507840 | tf_op jit(solution)/shard_map/dot_general | solution.py:43
  565.6 0.0 copy-start.3
  565.6 0.1 fusion.53
  565.7 0.2 copy.37
  565.9 1.5 collective-permute-start
  567.4 1.0 copy.39
  568.4 1.5 collective-permute-start.1
  569.8 0.0 copy-done.3
  569.9 0.6 copy.38
  570.5 9.7 collective-permute-done
  580.2 9.2 collective-permute-done.1
  589.3 0.3 maximum_convert_fusion
  589.6 0.3 fusion.50
  590.0 0.4 fusion.51
  590.3 0.0 copy-start.4
  590.3 0.1 maximum_convert_fusion.6
  590.5 0.5 copy-done.4
  591.0 2.0 fusion.20
  593.1 6.4 copy.40
  599.5 0.0 all-gather.5.cloned.1.call-update
  599.5 0.2 bitcast_convert_fusion
  599.7 1.7 copy.42
  601.4 0.0 copy-start.2
  601.4 474.1 %all-gather.5.cloned.1.call-done = bf16[2,8,16,13824]{2,1,0,3:T(8,128)(2,1)} async-done(((bf16[2,8,16,1728]{2,1,0,3:T(8,128)(2,1)}), bf16[2,8,16,13824]{2,1,0,3:T(8,128)(2,1)}) %all-gather.5.cloned.1.call-update) | async-done | bytes 7077904 | tf_op jit(solution)/shard_map/all_gather | solution.py:42
  1075.4 48.5 %copy.41 = bf16[2,8,16,13824]{3,2,1,0:T(8,128)(2,1)} copy(bf16[2,8,16,13824]{2,1,0,3:T(8,128)(2,1)} %all-gather.5.cloned.1.call-done) | data formatting | bytes 14155776 | tf_op jit(solution)/shard_map/all_gather | solution.py:42
  1123.9 0.0 copy-done.2
  1123.9 21.0 %fusion.3 = bf16[256,1728]{0,1:T(8,128)(2,1)S(1)} fusion(f32[256,1728]{0,1:T(8,128)S(1)} %copy-done.2, bf16[256,13824]{1,0:T(8,128)(2,1)} %bitcast.25, bf16[1728,13824]{1,0:T(8,128)(2,1)} %param.7), kind=kOutput, calls=%fused_computation.5 | convolution fusion | flops 12231917568 | bytes 57507840 | tf_op jit(solution)/shard_map/dot_general | solution.py:43
  1145.0 0.1 fusion.52
  1145.0 0.2 copy.43
  1145.2 1.5 collective-permute-start.2
  1146.8 1.0 copy.45
  1147.7 1.5 collective-permute-start.3
  1149.2 0.6 copy.44
  1149.8 9.7 collective-permute-done.2
  1159.5 9.2 collective-permute-done.3
  1168.7 0.3 maximum_convert_fusion.1
  1169.0 0.3 fusion.49
  1169.3 0.4 fusion.48
  1169.8 0.1 maximum_convert_fusion.3
  1169.9 3.4 convert_reduce_fusion
  1173.3 13.9 %psum.7 = f32[2,8,16]{2,1,0:T(8,128)S(1)} all-reduce(f32[2,8,16]{2,1,0:T(8,128)S(1)} %get-tuple-element.2), channel_id=1, replica_groups=mesh['vel'=8,'space'=4] {'vel'}, use_global_device_ids=true, to_apply=%region_1.2 | all-reduce | flops 256 | bytes 2048 | tf_op jit(solution)/shard_map/psum | solution.py:69
  1187.2 0.6 broadcast_multiply_fusion
  (5 shorter events, 0.1 us)
Async XLA Ops:
  7.2 488.9 %all-gather.3.cloned.1.call-start = ((), (), s32[]{:S(2)}) async-start(), calls=%async_computation | async-start | bytes 63700992 | tf_op jit(solution)/shard_map/all_gather | solution.py:42
  14.7 1.2 copy-start
  14.7 1060.7 %all-gather.5.cloned.1.call-start = ((), (), s32[]{:S(2)}) async-start(), calls=%async_computation.1 | async-start | bytes 63700992 | tf_op jit(solution)/shard_map/all_gather | solution.py:42
  16.0 1.7 copy-start.5
  16.0 1.7 copy-start.6
  17.7 526.8 %copy-start.1 = (f32[256,1728]{0,1:T(8,128)S(1)}, f32[256,1728]{0,1:T(8,128)}, u32[]{:S(2)}) copy-start(f32[256,1728]{0,1:T(8,128)} %copy.36) | copy-start | bytes 5308420
  565.6 4.3 copy-start.3
  565.9 14.3 %collective-permute-start = (bf16[1,8,16,1728]{3,2,1,0:T(8,128)(2,1)S(1)}, bf16[1,8,16,1728]{3,2,1,0:T(8,128)(2,1)S(1)}, u32[]{:S(2)}, u32[]{:S(2)}) collective-permute-start(bf16[1,8,16,1728]{3,2,1,0:T(8,128)(2,1)S(1)} %bitcast.26), channel_id=1, source_target_pairs={{0,1},{1,2},{2,3},{3,0},{4,5},{5,6},{6,7},{7,4},{8,9},{9,10},{10,1... | collective-permute-start | bytes 1327112 | tf_op jit(solution)/shard_map/ppermute | solution.py:17
  568.4 21.0 %collective-permute-start.1 = (bf16[1,8,16,1728]{3,2,1,0:T(8,128)(2,1)}, bf16[1,8,16,1728]{3,2,1,0:T(8,128)(2,1)S(1)}, u32[]{:S(2)}, u32[]{:S(2)}) collective-permute-start(bf16[1,8,16,1728]{3,2,1,0:T(8,128)(2,1)} %bitcast.4), channel_id=1, source_target_pairs={{1,0},{2,1},{3,2},{0,3},{5,4},{6,5},{7,6},{4,7},{9,8},{10,9},{11,1... | collective-permute-start | bytes 1327112 | tf_op jit(solution)/shard_map/ppermute | solution.py:20
  590.3 0.7 copy-start.4
  601.4 522.6 %copy-start.2 = (f32[256,1728]{0,1:T(8,128)S(1)}, f32[256,1728]{0,1:T(8,128)}, u32[]{:S(2)}) copy-start(f32[256,1728]{0,1:T(8,128)} %copy.42) | copy-start | bytes 5308420
  1145.2 14.3 %collective-permute-start.2 = (bf16[1,8,16,1728]{3,2,1,0:T(8,128)(2,1)S(1)}, bf16[1,8,16,1728]{3,2,1,0:T(8,128)(2,1)S(1)}, u32[]{:S(2)}, u32[]{:S(2)}) collective-permute-start(bf16[1,8,16,1728]{3,2,1,0:T(8,128)(2,1)S(1)} %bitcast.27), channel_id=1, source_target_pairs={{0,1},{1,2},{2,3},{3,0},{4,5},{5,6},{6,7},{7,4},{8,9},{9,10},{10,1... | collective-permute-start | bytes 1327112 | tf_op jit(solution)/shard_map/ppermute | solution.py:17
  1147.7 21.0 %collective-permute-start.3 = (bf16[1,8,16,1728]{3,2,1,0:T(8,128)(2,1)}, bf16[1,8,16,1728]{3,2,1,0:T(8,128)(2,1)S(1)}, u32[]{:S(2)}, u32[]{:S(2)}) collective-permute-start(bf16[1,8,16,1728]{3,2,1,0:T(8,128)(2,1)} %bitcast.9), channel_id=1, source_target_pairs={{1,0},{2,1},{3,2},{0,3},{5,4},{6,5},{7,6},{4,7},{9,8},{10,9},{11,1... | collective-permute-start | bytes 1327112 | tf_op jit(solution)/shard_map/ppermute | solution.py:20
Sparse Core Ops, SparseCore 0:
  14.8 481.1 all-gather.2
  599.6 475.7 all-gather.4
where the time goes:
time: 1200 us; the launch traced here: 1190 us
  waiting for transfers between devices  990 us (82%)
  local copies, waits for them, and re-layouts  121 us (10%)
  matrix products  42 us (4%)
  between operations  14.2 us (1%)
  blocking collectives  13.9 us (1%)
    all_gather x2, waiting for transfers between devices, shards(): gathered = lax.all_gather(state, 'vel', axis=3, tiled=True)  952 us
    all_gather x2, local copies, waits for them, and re-layouts, shards(): gathered = lax.all_gather(state, 'vel', axis=3, tiled=True)  97 us
    dot_general x2, matrix products, shards(): lax.dot_general(gathered.reshape(cells, whole_vel), collision, (((1,), (1...  42 us
  transfers between devices with their start and end apart: 6, of which 6 were waited for; matrix products, arithmetic and copies ran while one was open for 1% of the time, Pallas kernels for 0%

commit v1 on v0

v1 whole, which is shorter than its diff:
```python
import functools

import jax
import jax.numpy as jnp
from jax import lax
from jax.experimental import pallas as pl
from jax.experimental.pallas import tpu as pltpu
from jax.sharding import PartitionSpec as P

NV = 24
V = 13824
ITERS = 2
LANES = 128
HALF = LANES // 2
VMEM_LIMIT = 40 * 1024 * 1024


def speeds(vel_order):
    kx = vel_order // (NV * NV)
    ky = vel_order // NV % NV
    kz = vel_order % NV
    scale = 0.9 / (1.5 * (NV - 1))
    half = (NV - 1) / 2.0
    return [(k.astype(jnp.float32) - half) * scale for k in (kx, ky, kz)]


def ring(axis):
    count = lax.axis_size(axis)
    forward = [(i, (i + 1) % count) for i in range(count)]
    return forward, [(target, source) for source, target in forward]


def plain_step(state, collision, speed_list, inflow_value, wall_flag, inflow_flag):
    shape = state.shape
    cells = shape[0] * shape[1] * shape[2]
    local_vel = shape[3]
    flat = state.reshape(cells, local_vel)
    gathered = lax.all_gather(flat, "vel")
    gathered = gathered.transpose(1, 0, 2).reshape(cells, collision.shape[1])
    image = lax.dot_general(
        gathered, collision, (((1,), (1,)), ((), ())), preferred_element_type=jnp.float32
    )
    relaxed = (0.5 * flat.astype(jnp.float32) + 0.5 * image).astype(jnp.bfloat16).reshape(shape)
    forward, backward = ring("space")
    low = lax.ppermute(relaxed[-1:], "space", forward)
    high = lax.ppermute(relaxed[:1], "space", backward)
    padded = jnp.concatenate([low, relaxed, high], axis=0).astype(jnp.float32)
    field = padded[1:-1]
    total = field
    for axis, speed in enumerate(speed_list):
        if axis == 0:
            lower, upper = padded[:-2], padded[2:]
        else:
            lower, upper = jnp.roll(field, 1, axis=axis), jnp.roll(field, -1, axis=axis)
        total = total - jnp.where(speed > 0, speed * (field - lower), speed * (upper - field))
    total = jnp.where(inflow_flag[..., None] == 1, inflow_value.astype(jnp.float32), total)
    total = jnp.where(wall_flag[..., None] == 1, 0.0, total)
    return total.astype(jnp.bfloat16)


def plain(deviation, collision, vel_order, inflow_value, wall_flag, inflow_flag):
    state = deviation
    for _ in range(ITERS):
        state = plain_step(
            state, collision, speeds(vel_order), inflow_value, wall_flag, inflow_flag
        )
    partial_sum = jnp.sum(state.astype(jnp.float32), axis=3)
    return state, lax.psum(partial_sum, "vel") / jnp.sqrt(jnp.float32(V))


def vmem(count):
    return [pl.BlockSpec(memory_space=pltpu.VMEM)] * count


def params():
    return pltpu.CompilerParams(vmem_limit_bytes=VMEM_LIMIT)


def packed_rows(cells, local):
    return cells * local // LANES


def rows_at(start, size):
    return pl.ds(pl.multiple_of(start, 16), size)


def pack_kernel(runs, deviation_ref, *outs):
    planes, _, depth, local = deviation_ref.shape
    full = local // LANES
    for ys, out_ref in zip(runs, outs):
        cells = planes * len(ys) * depth
        half = cells // 2
        for x in range(planes):
            for i, y in enumerate(ys):
                at = (x * len(ys) + i) * depth
                for t in range(full):
                    out_ref[t * cells + at : t * cells + at + depth, :] = deviation_ref[
                        x, y, :, t * LANES : (t + 1) * LANES
                    ]
                side = 0 if at < half else 1
                at = full * cells + at - side * half
                out_ref[at : at + depth, side * HALF : (side + 1) * HALF] = deviation_ref[
                    x, y, :, full * LANES : local
                ]


def pack(deviation, runs):
    planes, _, depth, local = deviation.shape
    return pl.pallas_call(
        functools.partial(pack_kernel, runs),
        out_shape=[
            jax.ShapeDtypeStruct(
                (packed_rows(planes * len(ys) * depth, local), LANES), jnp.bfloat16
            )
            for ys in runs
        ],
        in_specs=vmem(1),
        out_specs=vmem(len(runs)),
        compiler_params=params(),
        name="pack",
    )(deviation)


def row_block(rows):
    return max(b for b in range(16, 577, 16) if rows % b == 0)


def matmul_kernel(count, cells, local, planes, has_acc, last, buffers, chips_ref, core_ref, *refs):
    refs = list(refs)
    pairs = [(refs.pop(0), refs.pop(0)) for _ in range(count)]
    collision_ref = refs.pop(0)
    acc_ref = refs.pop(0) if has_acc else None
    state_ref = refs.pop(0) if last else None
    outs = [refs.pop(0) for _ in range(planes if last else 1)]
    buffer_ref, sems, whole_ref, total_ref = refs
    total_ref = total_ref if last else outs[0]
    rows = buffer_ref.shape[1]
    blocks = local // rows
    steps = blocks * count
    full = local // LANES
    half = cells // 2
    width = 2 * local

    def copy(n):
        columns = pl.ds(pl.multiple_of(chips_ref[n // blocks] * width, LANES), width)
        return pltpu.make_async_copy(
            collision_ref.at[rows_at(n % blocks * rows, rows), columns],
            buffer_ref.at[n % buffers],
            sems.at[n % buffers],
        )

    for n in range(min(buffers - 1, steps)):
        copy(n).start()

    first_core = core_ref[0] == 0
    for k, (own_ref, other_ref) in enumerate(pairs):

        def tile(t, size=cells):
            own, other = own_ref[t * cells : t * cells + size], other_ref[t * cells : t * cells + size]
            return jnp.where(first_core, own, other), jnp.where(first_core, other, own)

        tiles = [tile(t) for t in range(full)]
        ends = tile(full, half)
        ends = [jnp.concatenate([e[:, :HALF], e[:, HALF:]], axis=0) for e in ends]
        for t in range(full):
            whole_ref[k, 0:cells, t * LANES : (t + 1) * LANES] = tiles[t][0]
        middle = jnp.concatenate([ends[0], tiles[0][1][:, :HALF]], axis=1)
        whole_ref[k, 0:cells, full * LANES : (full + 1) * LANES] = middle
        for t in range(full):
            right = tiles[t + 1][1][:, :HALF] if t + 1 < full else ends[1]
            both = jnp.concatenate([tiles[t][1][:, HALF:], right], axis=1)
            at = (full + 1 + t) * LANES
            whole_ref[k, 0:cells, at : at + LANES] = both

    total_ref[...] = acc_ref[...] if has_acc else jnp.zeros_like(total_ref)

    def step(n, carry):
        @pl.when(n + buffers - 1 < steps)
        def _():
            copy(n + buffers - 1).start()

        copy(n).wait()
        total_ref[rows_at(n % blocks * rows, rows), :] += lax.dot_general(
            buffer_ref[n % buffers],
            whole_ref[n // blocks],
            (((1,), (1,)), ((), ())),
            preferred_element_type=jnp.float32,
        )
        return carry

    lax.fori_loop(0, steps, step, 0)

    if last:
        size = cells // planes

        def relax(state, image):
            return (0.5 * state.astype(jnp.float32) + 0.5 * image).astype(jnp.bfloat16)

        def relax_tile(t, carry):
            image = total_ref[pl.ds(pl.multiple_of(t * LANES, LANES), LANES), :].T[0:cells, :]
            relaxed = relax(state_ref[rows_at(t * cells, cells), :], image)
            for x in range(planes):
                outs[x][rows_at(t * size, size), :] = relaxed[x * size : (x + 1) * size, :]
            return carry

        lax.fori_loop(0, full, relax_tile, 0)
        image = total_ref[full * LANES : local, :].T[0:cells, :]
        end = state_ref[full * cells : full * cells + half, :]
        relaxed = relax(jnp.concatenate([end[:, :HALF], end[:, HALF:]], axis=0), image)
        for x in range(planes):
            outs[x][full * size : (full + 1) * size, 0:HALF] = relaxed[x * size : (x + 1) * size, :]
            outs[x][full * size : (full + 1) * size, HALF:LANES] = jnp.zeros((size, HALF), jnp.bfloat16)


def matmul(pairs, chips, core, collision, cells, acc=None, state=None, planes=0):
    local = collision.shape[0]
    rows = row_block(local)
    buffers = 3
    count = len(pairs)
    padded = -(-cells // LANES) * LANES
    last = state is not None
    operands = [a for pair in pairs for a in pair] + [collision]
    in_specs = vmem(2 * count) + [pl.BlockSpec(memory_space=pl.ANY)]
    for extra in (acc, state):
        if extra is not None:
            operands.append(extra)
            in_specs += vmem(1)
    if last:
        tiles = local // LANES + 1
        out_shape = [
            jax.ShapeDtypeStruct((tiles * cells // planes, LANES), jnp.bfloat16)
        ] * planes
    else:
        out_shape = [jax.ShapeDtypeStruct((local, padded), jnp.float32)]
    scalar = pl.BlockSpec(memory_space=pltpu.SMEM)
    return pl.pallas_call(
        functools.partial(
            matmul_kernel, count, cells, local, planes, acc is not None, last, buffers
        ),
        out_shape=out_shape,
        in_specs=[scalar, scalar] + in_specs,
        out_specs=vmem(len(out_shape)),
        scratch_shapes=[
            pltpu.VMEM((buffers, rows, 2 * local), jnp.bfloat16),
            pltpu.SemaphoreType.DMA((buffers,)),
            pltpu.VMEM((count, padded, 2 * local), jnp.bfloat16),
            pltpu.VMEM((local, padded) if last else (8, LANES), jnp.float32),
        ],
        compiler_params=params(),
        cost_estimate=pl.CostEstimate(
            flops=4 * count * local * local * 256,
            bytes_accessed=4 * count * local * local,
            transcendentals=0,
        ),
        name="collide",
    )(jnp.stack(chips).astype(jnp.int32), core.astype(jnp.int32)[None], *operands)


def stream_kernel(ys, where_is, planes, depth, final, sizes, speed_ref, inflow_ref, code_ref, *refs):
    refs = list(refs)
    chunks = [[refs.pop(0) for _ in range(planes + 2)] for _ in sizes]
    out_ref = refs.pop(0)
    height = len(where_is)
    full = speed_ref.shape[0] - 1
    cells = planes * len(ys) * depth
    half = cells // 2

    def tile(t, tail):
        def plane(x, y):
            chunk, at = where_is[y % height]
            ref = chunks[chunk][x + 1]
            return ref[rows_at(t * sizes[chunk] + at * depth, depth), :].astype(jnp.float32)

        speed = [speed_ref[t, d : d + 1, :] for d in range(3)]
        size = [jnp.abs(s) for s in speed]
        up = [s > 0 for s in speed]
        inflow = inflow_ref[t, 0:1, :].astype(jnp.float32)
        for x in range(planes):
            for i, y in enumerate(ys):
                field = plane(x, y)
                total = field
                for d in range(3):
                    if d == 0:
                        lower, upper = plane(x - 1, y), plane(x + 1, y)
                    elif d == 1:
                        lower, upper = plane(x, y - 1), plane(x, y + 1)
                    else:
                        lower = pltpu.roll(field, 1, 0)
                        upper = pltpu.roll(field, depth - 1, 0)
                    near = jnp.where(up[d], lower, upper)
                    total = total - size[d] * (field - near)
                at = (x * height + y) * depth
                code = code_ref[at : at + depth, :]
                total = jnp.where(code == 0, total, jnp.where(code == 1, inflow, 0.0))
                total = total.astype(jnp.bfloat16)
                at = (x * len(ys) + i) * depth
                if final:
                    wide = total.astype(jnp.float32)
                    if tail:
                        out_ref[at : at + depth, full * LANES : full * LANES + HALF] = total[:, :HALF]
                        lane = lax.broadcasted_iota(jnp.int32, wide.shape, 1)
                        wide = jnp.where(lane < HALF, wide, 0.0)
                        summed = refs[1][at : at + depth, :] + wide
                        refs[0][at : at + depth, :] = jnp.sum(summed, axis=1, keepdims=True)
                    else:
                        lanes = pl.ds(pl.multiple_of(t * LANES, LANES), LANES)
                        out_ref[at : at + depth, lanes] = total
                        refs[1][at : at + depth, :] += wide
                elif tail:
                    side = 0 if at < half else 1
                    at = full * cells + at - side * half
                    out_ref[at : at + depth, side * HALF : (side + 1) * HALF] = total[:, :HALF]
                else:
                    out_ref[rows_at(t * cells + at, depth), :] = total

    if final:
        refs[1][...] = jnp.zeros_like(refs[1])

    def body(t, carry):
        tile(t, False)
        return carry

    lax.fori_loop(0, full, body, 0)
    tile(full, True)


def stream(ys, chunks, where_is, speed, inflow, code, planes, depth, local, final):
    used = sorted({where_is[(y + d) % len(where_is)][0] for y in ys for d in (-1, 0, 1)})
    where_is = [(used.index(c) if c in used else None, at) for c, at in where_is]
    operands = [a for c in used for a in chunks[c]]
    tiles = local // LANES + 1
    sizes = tuple(chunks[c][0].shape[0] // tiles for c in used)
    cells = planes * len(ys) * depth
    scratch = []
    if final:
        out_shape = [
            jax.ShapeDtypeStruct((cells, local), jnp.bfloat16),
            jax.ShapeDtypeStruct((cells, 1), jnp.float32),
        ]
        scratch = [pltpu.VMEM((cells, LANES), jnp.float32)]
    else:
        out_shape = [jax.ShapeDtypeStruct((packed_rows(cells, local), LANES), jnp.bfloat16)]
    return pl.pallas_call(
        functools.partial(stream_kernel, tuple(ys), tuple(where_is), planes, depth, final, sizes),
        out_shape=out_shape,
        in_specs=vmem(3 + len(operands)),
        out_specs=vmem(len(out_shape)),
        scratch_shapes=scratch,
        compiler_params=params(),
        cost_estimate=pl.CostEstimate(
            flops=40 * cells * local, bytes_accessed=12 * cells * local, transcendentals=0
        ),
        name="stream",
    )(speed, inflow, code, *operands)


def line_perm(pairs):
    return [(2 * a + c, 2 * b + c) for a, b in pairs for c in range(2)]


def other_core(block):
    return lax.ppermute(block, "vel", [(i, i ^ 1) for i in range(8)])


def line_sum(part):
    part = part + other_core(part)
    for mask in (1, 2):
        perm = line_perm([(a, a ^ mask) for a in range(4)])
        part = part + lax.ppermute(part, "vel", perm)
    return part


def line_gather(own, chip):
    far = lax.ppermute(own, "vel", line_perm([(a, a ^ 3) for a in range(4)]))
    near = lax.ppermute(own, "vel", line_perm([(a, a ^ 1) for a in range(4)]))
    middle = (chip == 1) | (chip == 2)
    relayed = jnp.where(middle, far, own)
    rest = lax.ppermute(relayed, "vel", line_perm([(0, 2), (3, 1), (2, 3), (1, 0)]))
    return [(block, other_core(block)) for block in (own, near, far, rest)]


def split_rows(height, sizes, turn):
    assert sum(sizes) == height
    runs, at = [], turn
    for size in sizes:
        runs.append(tuple((at + i) % height for i in range(size)))
        at += size
    return runs


PLANS = (((8,), 0), ((8,), 0), ((8,), 0))


def line(deviation, collision, vel_order, inflow_value, wall_flag, inflow_flag):
    planes, height, depth, local = deviation.shape
    index = lax.axis_index("vel")
    chip, core = index // 2, index % 2
    order = [chip, chip ^ 1, chip ^ 3, chip ^ 2]
    tiles = local // LANES + 1

    def by_tile(rows):
        rows = jnp.pad(rows, ((0, 0), (0, tiles * LANES - local)))
        return rows.reshape(-1, tiles, LANES).transpose(1, 0, 2)

    speed = by_tile(jnp.stack(speeds(vel_order)))
    inflow = by_tile(inflow_value[None, :].astype(jnp.float32))
    code = jnp.where(wall_flag == 1, 2, inflow_flag).reshape(-1, 1)
    forward, backward = ring("space")

    runs = split_rows(height, *PLANS[0])
    states = pack(deviation, runs)
    for step in range(ITERS):
        chunks, where_is = [], [None] * height
        for number, (ys, own) in enumerate(zip(runs, states)):
            cells = planes * len(ys) * depth
            blocks = line_gather(own, chip)
            acc = matmul(blocks[:3], order[:3], core, collision, cells)[0]
            relaxed = matmul(
                blocks[3:], order[3:], core, collision, cells, acc=acc, state=own, planes=planes
            )
            low = lax.ppermute(relaxed[-1], "space", forward)
            high = lax.ppermute(relaxed[0], "space", backward)
            chunks.append([low, *relaxed, high])
            for at, y in enumerate(ys):
                where_is[y] = (number, at)
        final = step == ITERS - 1
        runs = split_rows(height, *PLANS[step + 1])
        results = [
            stream(ys, chunks, where_is, speed, inflow, code, planes, depth, local, final)
            for ys in runs
        ]
        states = [r[0] for r in results]
    position = {y: (k, i) for k, ys in enumerate(runs) for i, y in enumerate(ys)}

    def assemble(arrays, width):
        arrays = [a.reshape(planes, -1, depth, width) for a in arrays]
        if len(arrays) == 1:
            return arrays[0]
        parts = [arrays[k][:, i : i + 1] for k, i in map(position.get, range(height))]
        return jnp.concatenate(parts, axis=1)

    state = assemble(states, local)
    partial_sum = assemble([r[1] for r in results], 1)[..., 0]
    return state, line_sum(partial_sum) / jnp.sqrt(jnp.float32(V))


def shards(deviation, collision, *rest):
    planes, _, depth, local = deviation.shape
    fits = local % LANES == HALF and planes % 2 == 0 and depth % 16 == 0
    body = line if lax.axis_size("vel") == 8 and fits else plain
    return body(deviation, collision, *rest)


def solution(mesh):
    placed = (
        P("space", None, None, "vel"),
        P("vel", None),
        P("vel"),
        P("vel"),
        P("space", None, None),
        P("space", None, None),
    )
    return jax.shard_map(
        shards,
        mesh=mesh,
        in_specs=placed,
        out_specs=(P("space", None, None, "vel"), P("space", None, None)),
        check_vma=False,
    )
```

time: 1200 us -> 240 us (0.20)
  waiting for transfers between devices: 990 us -> 123 us
  local copies, waits for them, and re-layouts: 121 us -> 1.4 us
  Pallas kernels: 0 us -> 54.3 us
  starting transfers between devices: 6.03 us -> 59 us
  matrix products: 42 us -> 0 us
  blocking collectives: 13.9 us -> 0 us
  between operations: 14.2 us -> 0.86 us
    all_gather x2 -> x0, waiting for transfers between devices: 952 us -> none  [shards(): gathered = lax.all_gather(state, 'vel', axis=3, tiled=True)]
    all_gather x2 -> x0, local copies, waits for them, and re-layouts: 97 us -> none  [shards(): gathered = lax.all_gather(state, 'vel', axis=3, tiled=True)]
    ppermute x4 -> x21, waiting for transfers between devices: 37.7 us -> 123 us  [the longest x2 41.1 us: line_gather(): far = lax.ppermute(own, 'vel', line_perm([(a, a ^ 3) for a in range(4)]))]
    pallas_call x0 -> x7, Pallas kernels: none -> 54.3 us  [the longest x4 48.4 us: matmul(): pl.pallas_call(functools.partial(matmul_kernel, count, cells, local, plan...]
    ppermute x4 -> x21, starting transfers between devices: 5.95 us -> 59 us  [the longest x2 37.7 us: line_gather(): lax.ppermute(relayed, 'vel', line_perm([(0, 2), (3, 1), (2, 3), (1, 0)]))]
    dot_general x2 -> x0, matrix products: 42 us -> none  [shards(): lax.dot_general(gathered.reshape(cells, whole_vel), collision, (((1,), (1...]
    psum x1 -> x0, blocking collectives: 13.9 us -> none  [shards(): density = lax.psum(partial_sum, 'vel') / jnp.sqrt(jnp.float32(V))]
  transfers between devices with their start and end apart: 6 -> 21, of which waited for: 6 -> 11; matrix products, arithmetic and copies ran while one was open for 1% -> 1% of each run, Pallas kernels for 0% -> 13%
where the time goes in v1:
time: 240 us
  waiting for transfers between devices  123 us (51%)
  starting transfers between devices  59 us (25%)
  Pallas kernels  54.3 us (23%)
    pallas_call x4, Pallas kernels, matmul(): pl.pallas_call(functools.partial(matmul_kernel, count, cells, local, plan...  48.4 us
    ppermute x2, waiting for transfers between devices, line_gather(): far = lax.ppermute(own, 'vel', line_perm([(a, a ^ 3) for a in range(4)]))  41.1 us
    ppermute x2, starting transfers between devices, line_gather(): lax.ppermute(relayed, 'vel', line_perm([(0, 2), (3, 1), (2, 3), (1, 0)]))  37.7 us
    ppermute x2, waiting for transfers between devices, line_gather(): lax.ppermute(relayed, 'vel', line_perm([(0, 2), (3, 1), (2, 3), (1, 0)]))  36.5 us
    ppermute x2, waiting for transfers between devices, line(): low = lax.ppermute(relaxed[-1], 'space', forward)  22.3 us
    ppermute x2, waiting for transfers between devices, line(): high = lax.ppermute(relaxed[0], 'space', backward)  18 us
    ppermute x2, starting transfers between devices, line_gather(): far = lax.ppermute(own, 'vel', line_perm([(a, a ^ 3) for a in range(4)]))  7.28 us
    pallas_call x2, Pallas kernels, stream(): pl.pallas_call(functools.partial(stream_kernel, tuple(ys), tuple(where_is...  5.82 us
  transfers between devices with their start and end apart: 21, of which 11 were waited for; matrix products, arithmetic and copies ran while one was open for 1% of the time, Pallas kernels for 13%

profile of v1, /device:TPU:0, one launch (start us, length us, event | category | flops | bytes accessed | tf_op | source)
XLA Modules:
  0.0 240.2 jit_solution(3826319791023446207)
XLA Ops:
  0.6 0.0 copy-start
  0.6 1.2 copy-done
  1.8 0.2 pack.1.refs_0_.refs_4_
  2.0 5.1 %collective-permute-start = (bf16[3456,128]{1,0:T(8,128)(2,1)S(1)}, bf16[3456,128]{1,0:T(8,128)(2,1)S(1)}, u32[]{:S(2)}, u32[]{:S(2)}) collective-permute-start(bf16[3456,128]{1,0:T(8,128)(2,1)S(1)} %pack.1.refs_0_.refs_4_), channel_id=1, source_target_pairs={{0,24},{4,28},{8,16},{12,20},{16,8},{20,12},{24,0},{28,4},{1,25},{... | collective-permute-start | bytes 2654216 | tf_op jit(solution)/shard_map/ppermute | solution.py:374
  7.1 0.0 collective-permute-start.4
  7.1 20.6 %collective-permute-done.refs_4_ = bf16[3456,128]{1,0:T(8,128)(2,1)S(1)} collective-permute-done((bf16[3456,128]{1,0:T(8,128)(2,1)S(1)}, bf16[3456,128]{1,0:T(8,128)(2,1)S(1)}, u32[]{:S(2)}, u32[]{:S(2)}) %collective-permute-start) | collective-permute-done | bytes 884768 | tf_op jit(solution)/shard_map/ppermute | solution.py:374
  27.7 1.0 broadcast_select_fusion.1
  28.7 18.8 %collective-permute-start.1 = (bf16[3456,128]{1,0:T(8,128)(2,1)}, bf16[3456,128]{1,0:T(8,128)(2,1)S(1)}, u32[]{:S(2)}, u32[]{:S(2)}) collective-permute-start(bf16[3456,128]{1,0:T(8,128)(2,1)} %broadcast_select_fusion.1), channel_id=1, source_target_pairs={{0,16},{4,20},{24,8},{28,12},{16,24},{20,28},{8,0},{12,4},{1,17},{... | collective-permute-start | bytes 2654216 | tf_op jit(solution)/shard_map/ppermute | solution.py:378
  47.4 0.0 collective-permute-start.3
  47.4 0.5 collective-permute-start.6
  47.9 0.0 collective-permute-done.4.refs_2_
  47.9 0.0 collective-permute-start.5
  47.9 17.8 %collective-permute-done.1.refs_0_ = bf16[3456,128]{1,0:T(8,128)(2,1)S(1)} collective-permute-done((bf16[3456,128]{1,0:T(8,128)(2,1)}, bf16[3456,128]{1,0:T(8,128)(2,1)S(1)}, u32[]{:S(2)}, u32[]{:S(2)}) %collective-permute-start.1) | collective-permute-done | bytes 884768 | tf_op jit(solution)/shard_map/ppermute | solution.py:378
  65.8 0.0 collective-permute-start.2
  65.8 0.1 pad_add_fusion.chips_ref
  65.9 0.0 collective-permute-done.3.refs_1_
  65.9 0.0 collective-permute-done.6.refs_5_
  65.9 0.0 collective-permute-done.5.refs_3_
  65.9 16.4 %collide.4.refs_3_ = f32[1728,256]{1,0:T(8,128)S(1)} custom-call(s32[3]{0:T(128)S(1)} %pad_add_fusion.chips_ref, s32[1]{0:T(128)} %bitcast.4.core_ref, bf16[3456,128]{1,0:T(8,128)(2,1)S(1)} %pack.1.refs_0_.refs_4_, bf16[3456,128]{1,0:T(8,128)(2,1)} %collective-permute-done.3.refs_1_, bf16[3456,128]{1,0:T(8,128)(2,1)S(1)} %collective-permute-done.4.refs_2_, ...), custom_call_target="tpu_custom_call" | custom-call | flops 9172942848 | bytes 35831808 | tf_op jit(solution)/shard_map/collide/pallas_call | solution.py:236
  82.3 0.0 collective-permute-done.2.refs_1_
  82.3 0.0 copy-start.3
  82.3 0.0 copy-start.1
  82.3 0.0 copy-start.2
  82.3 0.0 copy-start.4
  82.3 9.0 %collide.5 = (bf16[1792,128]{1,0:T(8,128)(2,1)S(1)}, bf16[1792,128]{1,0:T(8,128)(2,1)S(1)}) custom-call(s32[1]{0:T(128)} %bitcast.3.chips_ref, s32[1]{0:T(128)} %bitcast.4.core_ref, bf16[3456,128]{1,0:T(8,128)(2,1)S(1)} %collective-permute-done.1.refs_0_, bf16[3456,128]{1,0:T(8,128)(2,1)} %collective-permute-done.2.refs_1_, bf16[1728,13824]{1,0:T(8,128)(2,1)} %refs_2_.3, ...), custom_call_target="tpu_custom_call" | custom-call | flops 3057647616 | bytes 11943936 | tf_op jit(solution)/shard_map/collide/pallas_call | solution.py:236
  91.3 1.6 collective-permute-start.7
  92.9 1.4 collective-permute-start.8
  94.3 0.0 copy-done.3
  94.4 0.0 copy-done.1
  94.4 0.1 reshape.19.code_ref
  94.6 11.0 %collective-permute-done.7.refs_0_ = bf16[1792,128]{1,0:T(8,128)(2,1)S(1)} collective-permute-done((bf16[1792,128]{1,0:T(8,128)(2,1)S(1)}, bf16[1792,128]{1,0:T(8,128)(2,1)S(1)}, u32[]{:S(2)}, u32[]{:S(2)}) %collective-permute-start.7) | collective-permute-done | bytes 458784 | tf_op jit(solution)/shard_map/ppermute | solution.py:421
  105.6 9.5 %collective-permute-done.8.refs_3_ = bf16[1792,128]{1,0:T(8,128)(2,1)S(1)} collective-permute-done((bf16[1792,128]{1,0:T(8,128)(2,1)S(1)}, bf16[1792,128]{1,0:T(8,128)(2,1)S(1)}, u32[]{:S(2)}, u32[]{:S(2)}) %collective-permute-start.8) | collective-permute-done | bytes 458784 | tf_op jit(solution)/shard_map/ppermute | solution.py:422
  115.1 2.0 stream.2.refs_0_.refs_4_
  117.1 2.2 collective-permute-start.9
  119.3 1.7 collective-permute-start.13
  121.0 20.6 %collective-permute-done.9.refs_4_ = bf16[3456,128]{1,0:T(8,128)(2,1)S(1)} collective-permute-done((bf16[3456,128]{1,0:T(8,128)(2,1)S(1)}, bf16[3456,128]{1,0:T(8,128)(2,1)S(1)}, u32[]{:S(2)}, u32[]{:S(2)}) %collective-permute-start.9) | collective-permute-done | bytes 884768 | tf_op jit(solution)/shard_map/ppermute | solution.py:374
  141.6 0.1 broadcast_select_fusion
  141.7 18.9 %collective-permute-start.10 = (bf16[3456,128]{1,0:T(8,128)(2,1)S(1)}, bf16[3456,128]{1,0:T(8,128)(2,1)S(1)}, u32[]{:S(2)}, u32[]{:S(2)}) collective-permute-start(bf16[3456,128]{1,0:T(8,128)(2,1)S(1)} %broadcast_select_fusion), channel_id=1, source_target_pairs={{0,16},{4,20},{24,8},{28,12},{16,24},{20,28},{8,0},{12,4},{1,17},{... | collective-permute-start | bytes 2654216 | tf_op jit(solution)/shard_map/ppermute | solution.py:378
  160.6 0.0 collective-permute-start.12
  160.6 0.0 collective-permute-done.13.refs_2_
  160.6 0.5 collective-permute-start.14
  161.1 0.0 collective-permute-start.15
  161.1 18.6 %collective-permute-done.10.refs_0_ = bf16[3456,128]{1,0:T(8,128)(2,1)S(1)} collective-permute-done((bf16[3456,128]{1,0:T(8,128)(2,1)S(1)}, bf16[3456,128]{1,0:T(8,128)(2,1)S(1)}, u32[]{:S(2)}, u32[]{:S(2)}) %collective-permute-start.10) | collective-permute-done | bytes 884768 | tf_op jit(solution)/shard_map/ppermute | solution.py:378
  179.7 0.0 collective-permute-start.11
  179.7 0.0 collective-permute-done.12.refs_1_
  179.8 0.0 collective-permute-done.14.refs_3_
  179.8 0.0 collective-permute-done.15.refs_5_
  179.8 15.2 %collide.6.refs_3_ = f32[1728,256]{1,0:T(8,128)S(1)} custom-call(s32[3]{0:T(128)S(1)} %pad_add_fusion.chips_ref, s32[1]{0:T(128)} %bitcast.4.core_ref, bf16[3456,128]{1,0:T(8,128)(2,1)S(1)} %stream.2.refs_0_.refs_4_, bf16[3456,128]{1,0:T(8,128)(2,1)S(1)} %collective-permute-done.12.refs_1_, bf16[3456,128]{1,0:T(8,128)(2,1)S(1)} %collective-permute-done.13.refs_2_, ...), custom_call_target="tpu_custom_call" | custom-call | flops 9172942848 | bytes 35831808 | tf_op jit(solution)/shard_map/collide/pallas_call | solution.py:236
  195.0 0.0 collective-permute-done.11.refs_1_
  195.0 7.8 %collide.7 = (bf16[1792,128]{1,0:T(8,128)(2,1)S(1)}, bf16[1792,128]{1,0:T(8,128)(2,1)S(1)}) custom-call(s32[1]{0:T(128)} %bitcast.3.chips_ref, s32[1]{0:T(128)} %bitcast.4.core_ref, bf16[3456,128]{1,0:T(8,128)(2,1)S(1)} %collective-permute-done.10.refs_0_, bf16[3456,128]{1,0:T(8,128)(2,1)S(1)} %collective-permute-done.11.refs_1_, ...), custom_call_target="tpu_custom_call" | custom-call | flops 3057647616 | bytes 11943936 | tf_op jit(solution)/shard_map/collide/pallas_call | solution.py:236
  202.8 1.5 collective-permute-start.16
  204.3 1.5 collective-permute-start.17
  205.7 11.3 %collective-permute-done.16.refs_0_ = bf16[1792,128]{1,0:T(8,128)(2,1)S(1)} collective-permute-done((bf16[1792,128]{1,0:T(8,128)(2,1)S(1)}, bf16[1792,128]{1,0:T(8,128)(2,1)S(1)}, u32[]{:S(2)}, u32[]{:S(2)}) %collective-permute-start.16) | collective-permute-done | bytes 458784 | tf_op jit(solution)/shard_map/ppermute | solution.py:421
  217.0 8.5 %collective-permute-done.17.refs_3_ = bf16[1792,128]{1,0:T(8,128)(2,1)S(1)} collective-permute-done((bf16[1792,128]{1,0:T(8,128)(2,1)S(1)}, bf16[1792,128]{1,0:T(8,128)(2,1)S(1)}, u32[]{:S(2)}, u32[]{:S(2)}) %collective-permute-start.17) | collective-permute-done | bytes 458784 | tf_op jit(solution)/shard_map/ppermute | solution.py:422
  225.5 3.8 %stream.3 = (bf16[256,1728]{1,0:T(8,128)(2,1)}, f32[256,1]{1,0:T(8,128)S(1)}) custom-call(f32[14,3,128]{2,1,0:T(4,128)S(1)} %fusion.speed_ref, f32[14,1,128]{2,1,0:T(1,128)S(1)} %bitcast_convert_fusion.inflow_ref, s32[256,1]{1,0:T(8,128)S(1)} %reshape.19.code_ref, bf16[1792,128]{1,0:T(8,128)(2,1)S(1)} %collective-permute-done.16.refs_0_, ...), custom_call_target="tpu_custom_call" | custom-call | flops 17694720 | bytes 5308416 | tf_op jit(solution)/shard_map/stream/pallas_call | solution.py:343
  229.4 0.1 reduce
  229.5 0.1 squeeze_reshape.3
  229.5 0.0 collective-permute-start.18
  229.6 1.2 collective-permute-done.18
  230.7 2.6 %collective-permute-start.19 = (f32[2,8,16]{2,1,0:T(8,128)S(1)}, f32[2,8,16]{2,1,0:T(8,128)S(1)}, u32[]{:S(2)}, u32[]{:S(2)}) collective-permute-start(f32[2,8,16]{2,1,0:T(8,128)S(1)} %add.36), channel_id=1, source_target_pairs={{0,8},{4,12},{8,0},{12,4},{16,24},{20,28},{24,16},{28,20},{1,9},{5... | collective-permute-start | bytes 3080 | tf_op jit(solution)/shard_map/ppermute | solution.py:369
  233.4 1.6 collective-permute-done.19
  235.0 2.6 %collective-permute-start.20 = (f32[2,8,16]{2,1,0:T(8,128)S(1)}, f32[2,8,16]{2,1,0:T(8,128)S(1)}, u32[]{:S(2)}, u32[]{:S(2)}) collective-permute-start(f32[2,8,16]{2,1,0:T(8,128)S(1)} %add.37), channel_id=1, source_target_pairs={{0,16},{4,20},{8,24},{12,28},{16,0},{20,4},{24,8},{28,12},{1,17},{... | collective-permute-start | bytes 3080 | tf_op jit(solution)/shard_map/ppermute | solution.py:369
  237.7 1.9 collective-permute-done.20
  239.6 0.6 add_multiply_fusion
  (12 shorter events, 0.1 us)
Async XLA Ops:
  0.6 1.2 copy-start
  2.0 25.7 %collective-permute-start = (bf16[3456,128]{1,0:T(8,128)(2,1)S(1)}, bf16[3456,128]{1,0:T(8,128)(2,1)S(1)}, u32[]{:S(2)}, u32[]{:S(2)}) collective-permute-start(bf16[3456,128]{1,0:T(8,128)(2,1)S(1)} %pack.1.refs_0_.refs_4_), channel_id=1, source_target_pairs={{0,24},{4,28},{8,16},{12,20},{16,8},{20,12},{24,0},{28,4},{1,25},{... | collective-permute-start | bytes 2654216 | tf_op jit(solution)/shard_map/ppermute | solution.py:374
  7.1 40.9 %collective-permute-start.4 = (bf16[3456,128]{1,0:T(8,128)(2,1)S(1)}, bf16[3456,128]{1,0:T(8,128)(2,1)S(1)}, u32[]{:S(2)}, u32[]{:S(2)}) collective-permute-start(bf16[3456,128]{1,0:T(8,128)(2,1)S(1)} %pack.1.refs_0_.refs_4_), channel_id=1, source_target_pairs={{0,8},{4,12},{8,0},{12,4},{16,24},{20,28},{24,16},{28,20},{1,9},{5... | collective-permute-start | bytes 2654216 | tf_op jit(solution)/shard_map/ppermute | solution.py:375
  28.7 37.1 %collective-permute-start.1 = (bf16[3456,128]{1,0:T(8,128)(2,1)}, bf16[3456,128]{1,0:T(8,128)(2,1)S(1)}, u32[]{:S(2)}, u32[]{:S(2)}) collective-permute-start(bf16[3456,128]{1,0:T(8,128)(2,1)} %broadcast_select_fusion.1), channel_id=1, source_target_pairs={{0,16},{4,20},{24,8},{28,12},{16,24},{20,28},{8,0},{12,4},{1,17},{... | collective-permute-start | bytes 2654216 | tf_op jit(solution)/shard_map/ppermute | solution.py:378
  47.4 18.4 %collective-permute-start.3 = (bf16[3456,128]{1,0:T(8,128)(2,1)S(1)}, bf16[3456,128]{1,0:T(8,128)(2,1)}, u32[]{:S(2)}, u32[]{:S(2)}) collective-permute-start(bf16[3456,128]{1,0:T(8,128)(2,1)S(1)} %pack.1.refs_0_.refs_4_), channel_id=1, source_target_pairs={{0,4},{4,0},{8,12},{12,8},{16,20},{20,16},{24,28},{28,24},{1,5},{5... | collective-permute-start | bytes 2654216 | tf_op jit(solution)/shard_map/ppermute | solution.py:362
  47.4 18.4 %collective-permute-start.6 = (bf16[3456,128]{1,0:T(8,128)(2,1)S(1)}, bf16[3456,128]{1,0:T(8,128)(2,1)}, u32[]{:S(2)}, u32[]{:S(2)}) collective-permute-start(bf16[3456,128]{1,0:T(8,128)(2,1)S(1)} %collective-permute-done.refs_4_), channel_id=1, source_target_pairs={{0,4},{4,0},{8,12},{12,8},{16,20},{20,16},{24,28},{28,24},{1,5},{5... | collective-permute-start | bytes 2654216 | tf_op jit(solution)/shard_map/ppermute | solution.py:362
  47.9 17.9 %collective-permute-start.5 = (bf16[3456,128]{1,0:T(8,128)(2,1)S(1)}, bf16[3456,128]{1,0:T(8,128)(2,1)}, u32[]{:S(2)}, u32[]{:S(2)}) collective-permute-start(bf16[3456,128]{1,0:T(8,128)(2,1)S(1)} %collective-permute-done.4.refs_2_), channel_id=1, source_target_pairs={{0,4},{4,0},{8,12},{12,8},{16,20},{20,16},{24,28},{28,24},{1,5},{5... | collective-permute-start | bytes 2654216 | tf_op jit(solution)/shard_map/ppermute | solution.py:362
  65.8 16.5 %collective-permute-start.2 = (bf16[3456,128]{1,0:T(8,128)(2,1)S(1)}, bf16[3456,128]{1,0:T(8,128)(2,1)}, u32[]{:S(2)}, u32[]{:S(2)}) collective-permute-start(bf16[3456,128]{1,0:T(8,128)(2,1)S(1)} %collective-permute-done.1.refs_0_), channel_id=1, source_target_pairs={{0,4},{4,0},{8,12},{12,8},{16,20},{20,16},{24,28},{28,24},{1,5},{5... | collective-permute-start | bytes 2654216 | tf_op jit(solution)/shard_map/ppermute | solution.py:362
  82.3 12.0 %copy-start.3 = (s32[1728]{0:T(1024)S(1)}, s32[1728]{0:T(1024)}, u32[]{:S(2)}) copy-start(s32[1728]{0:T(1024)} %param.8) | copy-start | bytes 20740
  82.3 12.1 %copy-start.1 = (s32[2,8,16]{2,1,0:T(8,128)S(1)}, s32[2,8,16]{2,1,0:T(8,128)}, u32[]{:S(2)}) copy-start(s32[2,8,16]{2,1,0:T(8,128)} %param.11) | copy-start | bytes 3076
  82.3 12.1 %copy-start.2 = (s32[2,8,16]{2,1,0:T(8,128)S(1)}, s32[2,8,16]{2,1,0:T(8,128)}, u32[]{:S(2)}) copy-start(s32[2,8,16]{2,1,0:T(8,128)} %param.10) | copy-start | bytes 3076
  82.3 12.2 %copy-start.4 = (bf16[1728]{0:T(1024)(128)(2,1)S(1)}, bf16[1728]{0:T(1024)(128)(2,1)}, u32[]{:S(2)}) copy-start(bf16[1728]{0:T(1024)(128)(2,1)} %param.9) | copy-start | bytes 10372
  91.3 14.3 %collective-permute-start.7 = (bf16[1792,128]{1,0:T(8,128)(2,1)S(1)}, bf16[1792,128]{1,0:T(8,128)(2,1)S(1)}, u32[]{:S(2)}, u32[]{:S(2)}) collective-permute-start(bf16[1792,128]{1,0:T(8,128)(2,1)S(1)} %get-tuple-element.8.refs_2_), channel_id=1, source_target_pairs={{0,1},{1,2},{2,3},{3,0},{4,5},{5,6},{6,7},{7,4},{8,9},{9,10},{10,1... | collective-permute-start | bytes 1376264 | tf_op jit(solution)/shard_map/ppermute | solution.py:421
  92.9 22.2 %collective-permute-start.8 = (bf16[1792,128]{1,0:T(8,128)(2,1)S(1)}, bf16[1792,128]{1,0:T(8,128)(2,1)S(1)}, u32[]{:S(2)}, u32[]{:S(2)}) collective-permute-start(bf16[1792,128]{1,0:T(8,128)(2,1)S(1)} %get-tuple-element.9.refs_1_), channel_id=1, source_target_pairs={{1,0},{2,1},{3,2},{0,3},{5,4},{6,5},{7,6},{4,7},{9,8},{10,9},{11,1... | collective-permute-start | bytes 1376264 | tf_op jit(solution)/shard_map/ppermute | solution.py:422
  117.1 24.5 %collective-permute-start.9 = (bf16[3456,128]{1,0:T(8,128)(2,1)S(1)}, bf16[3456,128]{1,0:T(8,128)(2,1)S(1)}, u32[]{:S(2)}, u32[]{:S(2)}) collective-permute-start(bf16[3456,128]{1,0:T(8,128)(2,1)S(1)} %stream.2.refs_0_.refs_4_), channel_id=1, source_target_pairs={{0,24},{4,28},{8,16},{12,20},{16,8},{20,12},{24,0},{28,4},{1,25},{... | collective-permute-start | bytes 2654216 | tf_op jit(solution)/shard_map/ppermute | solution.py:374
  119.3 41.3 %collective-permute-start.13 = (bf16[3456,128]{1,0:T(8,128)(2,1)S(1)}, bf16[3456,128]{1,0:T(8,128)(2,1)S(1)}, u32[]{:S(2)}, u32[]{:S(2)}) collective-permute-start(bf16[3456,128]{1,0:T(8,128)(2,1)S(1)} %stream.2.refs_0_.refs_4_), channel_id=1, source_target_pairs={{0,8},{4,12},{8,0},{12,4},{16,24},{20,28},{24,16},{28,20},{1,9},{5... | collective-permute-start | bytes 2654216 | tf_op jit(solution)/shard_map/ppermute | solution.py:375
  141.7 38.1 %collective-permute-start.10 = (bf16[3456,128]{1,0:T(8,128)(2,1)S(1)}, bf16[3456,128]{1,0:T(8,128)(2,1)S(1)}, u32[]{:S(2)}, u32[]{:S(2)}) collective-permute-start(bf16[3456,128]{1,0:T(8,128)(2,1)S(1)} %broadcast_select_fusion), channel_id=1, source_target_pairs={{0,16},{4,20},{24,8},{28,12},{16,24},{20,28},{8,0},{12,4},{1,17},{... | collective-permute-start | bytes 2654216 | tf_op jit(solution)/shard_map/ppermute | solution.py:378
  160.6 19.2 %collective-permute-start.12 = (bf16[3456,128]{1,0:T(8,128)(2,1)S(1)}, bf16[3456,128]{1,0:T(8,128)(2,1)S(1)}, u32[]{:S(2)}, u32[]{:S(2)}) collective-permute-start(bf16[3456,128]{1,0:T(8,128)(2,1)S(1)} %stream.2.refs_0_.refs_4_), channel_id=1, source_target_pairs={{0,4},{4,0},{8,12},{12,8},{16,20},{20,16},{24,28},{28,24},{1,5},{5... | collective-permute-start | bytes 2654216 | tf_op jit(solution)/shard_map/ppermute | solution.py:362
  160.6 19.2 %collective-permute-start.14 = (bf16[3456,128]{1,0:T(8,128)(2,1)S(1)}, bf16[3456,128]{1,0:T(8,128)(2,1)S(1)}, u32[]{:S(2)}, u32[]{:S(2)}) collective-permute-start(bf16[3456,128]{1,0:T(8,128)(2,1)S(1)} %collective-permute-done.13.refs_2_), channel_id=1, source_target_pairs={{0,4},{4,0},{8,12},{12,8},{16,20},{20,16},{24,28},{28,24},{1,5},{5... | collective-permute-start | bytes 2654216 | tf_op jit(solution)/shard_map/ppermute | solution.py:362
  161.1 18.6 %collective-permute-start.15 = (bf16[3456,128]{1,0:T(8,128)(2,1)S(1)}, bf16[3456,128]{1,0:T(8,128)(2,1)S(1)}, u32[]{:S(2)}, u32[]{:S(2)}) collective-permute-start(bf16[3456,128]{1,0:T(8,128)(2,1)S(1)} %collective-permute-done.9.refs_4_), channel_id=1, source_target_pairs={{0,4},{4,0},{8,12},{12,8},{16,20},{20,16},{24,28},{28,24},{1,5},{5... | collective-permute-start | bytes 2654216 | tf_op jit(solution)/shard_map/ppermute | solution.py:362
  179.7 15.3 %collective-permute-start.11 = (bf16[3456,128]{1,0:T(8,128)(2,1)S(1)}, bf16[3456,128]{1,0:T(8,128)(2,1)S(1)}, u32[]{:S(2)}, u32[]{:S(2)}) collective-permute-start(bf16[3456,128]{1,0:T(8,128)(2,1)S(1)} %collective-permute-done.10.refs_0_), channel_id=1, source_target_pairs={{0,4},{4,0},{8,12},{12,8},{16,20},{20,16},{24,28},{28,24},{1,5},{5... | collective-permute-start | bytes 2654216 | tf_op jit(solution)/shard_map/ppermute | solution.py:362
  202.8 14.3 %collective-permute-start.16 = (bf16[1792,128]{1,0:T(8,128)(2,1)S(1)}, bf16[1792,128]{1,0:T(8,128)(2,1)S(1)}, u32[]{:S(2)}, u32[]{:S(2)}) collective-permute-start(bf16[1792,128]{1,0:T(8,128)(2,1)S(1)} %get-tuple-element.10.refs_2_), channel_id=1, source_target_pairs={{0,1},{1,2},{2,3},{3,0},{4,5},{5,6},{6,7},{7,4},{8,9},{9,10},{10,1... | collective-permute-start | bytes 1376264 | tf_op jit(solution)/shard_map/ppermute | solution.py:421
  204.3 21.2 %collective-permute-start.17 = (bf16[1792,128]{1,0:T(8,128)(2,1)S(1)}, bf16[1792,128]{1,0:T(8,128)(2,1)S(1)}, u32[]{:S(2)}, u32[]{:S(2)}) collective-permute-start(bf16[1792,128]{1,0:T(8,128)(2,1)S(1)} %get-tuple-element.11.refs_1_), channel_id=1, source_target_pairs={{1,0},{2,1},{3,2},{0,3},{5,4},{6,5},{7,6},{4,7},{9,8},{10,9},{11,1... | collective-permute-start | bytes 1376264 | tf_op jit(solution)/shard_map/ppermute | solution.py:422
  229.5 1.2 collective-permute-start.18
  230.7 4.3 %collective-permute-start.19 = (f32[2,8,16]{2,1,0:T(8,128)S(1)}, f32[2,8,16]{2,1,0:T(8,128)S(1)}, u32[]{:S(2)}, u32[]{:S(2)}) collective-permute-start(f32[2,8,16]{2,1,0:T(8,128)S(1)} %add.36), channel_id=1, source_target_pairs={{0,8},{4,12},{8,0},{12,4},{16,24},{20,28},{24,16},{28,20},{1,9},{5... | collective-permute-start | bytes 3080 | tf_op jit(solution)/shard_map/ppermute | solution.py:369
  235.0 4.5 %collective-permute-start.20 = (f32[2,8,16]{2,1,0:T(8,128)S(1)}, f32[2,8,16]{2,1,0:T(8,128)S(1)}, u32[]{:S(2)}, u32[]{:S(2)}) collective-permute-start(f32[2,8,16]{2,1,0:T(8,128)S(1)} %add.37), channel_id=1, source_target_pairs={{0,16},{4,20},{8,24},{12,28},{16,0},{20,4},{24,8},{28,12},{1,17},{... | collective-permute-start | bytes 3080 | tf_op jit(solution)/shard_map/ppermute | solution.py:369

commit v2 on v1

v2 whole, which is shorter than its diff:
```python
import functools

import jax
import jax.numpy as jnp
from jax import lax
from jax.experimental import pallas as pl
from jax.experimental.pallas import tpu as pltpu
from jax.sharding import PartitionSpec as P

NV = 24
V = 13824
ITERS = 2
LANES = 128
HALF = LANES // 2
COST = 1024
STREAM_COST = 1024
VMEM_LIMIT = 36 * 1024 * 1024
BUFFERS = 3


def speeds(vel_order):
    kx = vel_order // (NV * NV)
    ky = vel_order // NV % NV
    kz = vel_order % NV
    scale = 0.9 / (1.5 * (NV - 1))
    half = (NV - 1) / 2.0
    return [(k.astype(jnp.float32) - half) * scale for k in (kx, ky, kz)]


def ring(axis):
    count = lax.axis_size(axis)
    forward = [(i, (i + 1) % count) for i in range(count)]
    return forward, [(target, source) for source, target in forward]


def plain_step(state, collision, speed_list, inflow_value, wall_flag, inflow_flag):
    shape = state.shape
    cells = shape[0] * shape[1] * shape[2]
    local_vel = shape[3]
    flat = state.reshape(cells, local_vel)
    gathered = lax.all_gather(flat, "vel")
    gathered = gathered.transpose(1, 0, 2).reshape(cells, collision.shape[1])
    image = lax.dot_general(
        gathered, collision, (((1,), (1,)), ((), ())), preferred_element_type=jnp.float32
    )
    relaxed = (0.5 * flat.astype(jnp.float32) + 0.5 * image).astype(jnp.bfloat16).reshape(shape)
    forward, backward = ring("space")
    low = lax.ppermute(relaxed[-1:], "space", forward)
    high = lax.ppermute(relaxed[:1], "space", backward)
    padded = jnp.concatenate([low, relaxed, high], axis=0).astype(jnp.float32)
    field = padded[1:-1]
    total = field
    for axis, speed in enumerate(speed_list):
        if axis == 0:
            lower, upper = padded[:-2], padded[2:]
        else:
            lower, upper = jnp.roll(field, 1, axis=axis), jnp.roll(field, -1, axis=axis)
        total = total - jnp.where(speed > 0, speed * (field - lower), speed * (upper - field))
    total = jnp.where(inflow_flag[..., None] == 1, inflow_value.astype(jnp.float32), total)
    total = jnp.where(wall_flag[..., None] == 1, 0.0, total)
    return total.astype(jnp.bfloat16)


def plain(deviation, collision, vel_order, inflow_value, wall_flag, inflow_flag):
    state = deviation
    for _ in range(ITERS):
        state = plain_step(
            state, collision, speeds(vel_order), inflow_value, wall_flag, inflow_flag
        )
    partial_sum = jnp.sum(state.astype(jnp.float32), axis=3)
    return state, lax.psum(partial_sum, "vel") / jnp.sqrt(jnp.float32(V))


PARTS = (7,)


def vmem(count):
    return [pl.BlockSpec(memory_space=pltpu.VMEM)] * count


def params():
    return pltpu.CompilerParams(vmem_limit_bytes=VMEM_LIMIT)


def cost(size=COST):
    return pl.CostEstimate(flops=size, bytes_accessed=size, transcendentals=0)


def rows_at(start, size):
    return pl.ds(pl.multiple_of(start, 16), size)


def part_tiles(local):
    cuts = (0, *PARTS, local // LANES + 1)
    return list(zip(cuts[:-1], cuts[1:]))


def packed_rows(first, end, cells, local):
    return (end - first) * cells - (cells // 2 if end * LANES > local else 0)


def pack_kernel(deviation_ref, *outs):
    planes, height, depth, local = deviation_ref.shape
    cells = planes * height * depth
    half = cells // 2
    full = local // LANES
    for (first, end), out_ref in zip(part_tiles(local), outs):
        for x in range(planes):
            for y in range(height):
                at = (x * height + y) * depth
                for t in range(first, min(end, full)):
                    to = (t - first) * cells + at
                    out_ref[to : to + depth, :] = deviation_ref[
                        x, y, :, t * LANES : (t + 1) * LANES
                    ]
                if end > full:
                    side = 0 if at < half else 1
                    to = (full - first) * cells + at - side * half
                    out_ref[to : to + depth, side * HALF : (side + 1) * HALF] = deviation_ref[
                        x, y, :, full * LANES : local
                    ]


def pack(deviation):
    planes, height, depth, local = deviation.shape
    cells = planes * height * depth
    out_shape = [
        jax.ShapeDtypeStruct((packed_rows(*part, cells, local), LANES), jnp.bfloat16)
        for part in part_tiles(local)
    ]
    return pl.pallas_call(
        pack_kernel,
        out_shape=out_shape,
        in_specs=vmem(1),
        out_specs=vmem(len(out_shape)),
        compiler_params=params(),
        cost_estimate=cost(),
        name="pack",
    )(deviation)


def row_block(rows):
    return max(b for b in range(16, 577, 16) if rows % b == 0)


def unpack(own_ref, other_ref, first_core, whole_ref, k, cells, local):
    full = local // LANES
    half = cells // 2

    def tile(t, size=cells):
        own, other = own_ref[t * cells : t * cells + size], other_ref[t * cells : t * cells + size]
        return jnp.where(first_core, own, other), jnp.where(first_core, other, own)

    tiles = [tile(t) for t in range(full)]
    ends = tile(full, half)
    ends = [jnp.concatenate([e[:, :HALF], e[:, HALF:]], axis=0) for e in ends]
    for t in range(full):
        whole_ref[k, 0:cells, t * LANES : (t + 1) * LANES] = tiles[t][0]
    middle = jnp.concatenate([ends[0], tiles[0][1][:, :HALF]], axis=1)
    whole_ref[k, 0:cells, full * LANES : (full + 1) * LANES] = middle
    for t in range(full):
        right = tiles[t + 1][1][:, :HALF] if t + 1 < full else ends[1]
        both = jnp.concatenate([tiles[t][1][:, HALF:], right], axis=1)
        at = (full + 1 + t) * LANES
        whole_ref[k, 0:cells, at : at + LANES] = both


def matmul_kernel(
    count, pieces, cells, local, part, planes, has_acc, has_token, buffers, chips_ref, core_ref, *refs
):
    refs = list(refs)
    given = [[refs.pop(0) for _ in range(pieces)] for _ in range(2 * count)]
    collision_ref = refs.pop(0)
    acc_ref = refs.pop(0) if has_acc else None
    state_ref = refs.pop(0) if part else None
    if has_token:
        refs.pop(0)
    outs = [refs.pop(0) for _ in range(planes if part else 1)]
    if part:
        token_ref = refs.pop(0)
        token_ref[...] = jnp.zeros_like(token_ref)
    buffer_ref, sems, whole_ref, total_ref, load_sems, state_there = refs[:6]
    blocks_ref = refs[6:]
    total_ref = total_ref if part else outs[0]
    first, end = part or (0, local // LANES + 1)
    height = total_ref.shape[0]
    rows = buffer_ref.shape[1]
    blocks = height // rows
    steps = blocks * count
    width = 2 * local

    def copy(n):
        columns = pl.ds(pl.multiple_of(chips_ref[n // blocks] * width, LANES), width)
        return pltpu.make_async_copy(
            collision_ref.at[rows_at(first * LANES + n % blocks * rows, rows), columns],
            buffer_ref.at[n % buffers],
            sems.at[n % buffers],
        )

    def load(sources, target, number):
        copies, start = [], 0
        for i, source in enumerate(sources):
            here = pl.ds(start, source.shape[0])
            copies.append(
                pltpu.make_async_copy(source, target.at[here], load_sems.at[number * pieces + i])
            )
            start += source.shape[0]
        for one in copies:
            one.start()
        return copies

    def wait(copies):
        for one in copies:
            one.wait()

    loads = [load(sources, blocks_ref[i], i) for i, sources in enumerate(given)]
    for n in range(min(buffers - 1, steps)):
        copy(n).start()
    if has_acc:
        old = acc_ref.at[first * LANES : first * LANES + height, :]
        loads.append(load([old], total_ref, len(given)))
    if part:
        state_copy = load([state_ref], state_there, len(given) + 1)

    first_core = core_ref[0] == 0
    if not has_acc:
        total_ref[...] = jnp.zeros_like(total_ref)
    for k in range(count):
        wait(loads[2 * k] + loads[2 * k + 1])
        unpack(blocks_ref[2 * k], blocks_ref[2 * k + 1], first_core, whole_ref, k, cells, local)
    if has_acc:
        wait(loads[-1])

    def step(n, carry):
        @pl.when(n + buffers - 1 < steps)
        def _():
            copy(n + buffers - 1).start()

        copy(n).wait()
        total_ref[rows_at(n % blocks * rows, rows), :] += lax.dot_general(
            buffer_ref[n % buffers],
            whole_ref[n // blocks],
            (((1,), (1,)), ((), ())),
            preferred_element_type=jnp.float32,
        )
        return carry

    lax.fori_loop(0, steps, step, 0)

    if part:
        wait(state_copy)
        size = cells // planes
        whole_tiles = height // LANES

        def relax(t, state, image, lanes):
            relaxed = 0.5 * state.astype(jnp.float32) + 0.5 * image.T[0:cells, :]
            relaxed = relaxed.astype(jnp.bfloat16)
            for x in range(planes):
                outs[x][rows_at(t * size, size), 0:lanes] = relaxed[x * size : (x + 1) * size, :]

        def relax_tile(t, carry):
            image = total_ref[rows_at(t * LANES, LANES), :]
            relax(t, state_there[rows_at(t * cells, cells), :], image, LANES)
            return carry

        lax.fori_loop(0, whole_tiles, relax_tile, 0)
        if height % LANES:
            last = state_there[whole_tiles * cells :, :]
            state = jnp.concatenate([last[:, :HALF], last[:, HALF:]], axis=0)
            relax(whole_tiles, state, total_ref[whole_tiles * LANES :, :], HALF)
            for out_ref in outs:
                out_ref[whole_tiles * size :, HALF:LANES] = jnp.zeros((size, HALF), jnp.bfloat16)


def matmul(
    pairs,
    chips,
    core,
    collision,
    cells,
    acc=None,
    part=None,
    state=None,
    planes=0,
    token=None,
    size=COST,
):
    local = collision.shape[0]
    height = local
    if part:
        height = min(part[1] * LANES, local) - part[0] * LANES
    rows = row_block(height)
    buffers = BUFFERS
    count, pieces = len(pairs), len(pairs[0][0])
    padded = -(-cells // LANES) * LANES
    given = [a for pair in pairs for block in pair for a in block]
    operands = given + [collision] + [a for a in (acc, state, token) if a is not None]
    if part:
        shape = ((part[1] - part[0]) * cells // planes, LANES)
        out_shape = [jax.ShapeDtypeStruct(shape, jnp.bfloat16)] * planes
        out_shape.append(jax.ShapeDtypeStruct((8, LANES), jnp.float32))
    else:
        out_shape = [jax.ShapeDtypeStruct((local, padded), jnp.float32)]
    scalar = pl.BlockSpec(memory_space=pltpu.SMEM)
    small = (16, LANES)
    block = (packed_rows(0, local // LANES + 1, cells, local), LANES)
    return pl.pallas_call(
        functools.partial(
            matmul_kernel,
            count,
            pieces,
            cells,
            local,
            part,
            planes,
            acc is not None,
            token is not None,
            buffers,
        ),
        out_shape=out_shape,
        in_specs=[scalar, scalar] + [pl.BlockSpec(memory_space=pl.ANY)] * len(operands),
        out_specs=vmem(len(out_shape)),
        scratch_shapes=[
            pltpu.VMEM((buffers, rows, 2 * local), jnp.bfloat16),
            pltpu.SemaphoreType.DMA((buffers,)),
            pltpu.VMEM((count, padded, 2 * local), jnp.bfloat16),
            pltpu.VMEM((height, padded) if part else small, jnp.float32),
            pltpu.SemaphoreType.DMA(((2 * count + 2) * pieces,)),
            pltpu.VMEM(state.shape if part else small, jnp.bfloat16),
        ]
        + [pltpu.VMEM(block, jnp.bfloat16)] * (2 * count),
        compiler_params=params(),
        cost_estimate=cost(size),
        name="collide",
    )(jnp.stack(chips).astype(jnp.int32), core.astype(jnp.int32)[None], *operands)


def stream_kernel(part, shape, final, _, speed_ref, inflow_ref, code_ref, *refs):
    planes, height, depth, local = shape
    refs = list(refs)
    plane_refs = [refs.pop(0) for _ in range(planes + 2)]
    done = [refs.pop(0) for _ in range(2 if final else 1)] if part[0] > 0 else None
    out_ref = refs.pop(0)
    first, end = part
    full = local // LANES
    size = height * depth
    cells = planes * size
    half = cells // 2

    def tile(t, tail):
        def plane(x, y):
            at = t * size + y % height * depth
            return plane_refs[x + 1][rows_at(at, depth), :].astype(jnp.float32)

        speed = [speed_ref[first + t, d : d + 1, :] for d in range(3)]
        fast = [jnp.abs(s) for s in speed]
        up = [s > 0 for s in speed]
        inflow = inflow_ref[first + t, 0:1, :]
        for x in range(planes):
            for y in range(height):
                field = plane(x, y)
                total = field
                for d in range(3):
                    if d == 0:
                        lower, upper = plane(x - 1, y), plane(x + 1, y)
                    elif d == 1:
                        lower, upper = plane(x, y - 1), plane(x, y + 1)
                    else:
                        lower = pltpu.roll(field, 1, 0)
                        upper = pltpu.roll(field, depth - 1, 0)
                    near = jnp.where(up[d], lower, upper)
                    total = total - fast[d] * (field - near)
                at = (x * height + y) * depth
                here = slice(at, at + depth)
                code = code_ref[here, :]
                total = jnp.where(code == 0, total, jnp.where(code == 1, inflow, 0.0))
                total = total.astype(jnp.bfloat16)
                if final:
                    wide = total.astype(jnp.float32)
                    if tail:
                        out_ref[here, full * LANES : local] = total[:, :HALF]
                        lane = lax.broadcasted_iota(jnp.int32, wide.shape, 1)
                        wide = jnp.where(lane < HALF, wide, 0.0)
                    else:
                        lanes = pl.ds(pl.multiple_of((place + t) * LANES, LANES), LANES)
                        out_ref[here, lanes] = total
                    refs[0][here, :] += wide
                elif tail:
                    side = 0 if at < half else 1
                    to = t * cells + at - side * half
                    out_ref[to : to + depth, side * HALF : (side + 1) * HALF] = total[:, :HALF]
                else:
                    out_ref[rows_at(t * cells + at, depth), :] = total

    place = 0
    if not final:
        refs[0][...] = jnp.zeros_like(refs[0])
    if final:
        if done is None:
            refs[0][...] = jnp.zeros_like(refs[0])
        else:
            place = first
            out_ref[:, 0 : first * LANES] = done[0][...]
            refs[0][...] = done[1][...]

    def body(t, carry):
        tile(t, False)
        return carry

    lax.fori_loop(0, min(end, full) - first, body, 0)
    if end > full:
        tile(full - first, True)
        if final:
            refs[0][:, 0:1] = jnp.sum(refs[0][...], axis=1, keepdims=True)


def stream(part, planes, speed, inflow, code, shape, final, done, token):
    cells, local = shape[0] * shape[1] * shape[2], shape[3]
    operands = [token, speed, inflow, code, *planes, *done]
    if final:
        width = min(part[1] * LANES, local)
        out_shape = [
            jax.ShapeDtypeStruct((cells, width), jnp.bfloat16),
            jax.ShapeDtypeStruct((cells, LANES), jnp.float32),
        ]
    else:
        rows = packed_rows(*part, cells, local)
        out_shape = [
            jax.ShapeDtypeStruct((rows, LANES), jnp.bfloat16),
            jax.ShapeDtypeStruct((8, LANES), jnp.float32),
        ]
    return pl.pallas_call(
        functools.partial(stream_kernel, part, shape, final),
        out_shape=out_shape,
        in_specs=vmem(len(operands)),
        out_specs=vmem(len(out_shape)),
        compiler_params=params(),
        cost_estimate=cost(STREAM_COST),
        name="stream",
    )(*operands)


NEAR = ((0, 1), (1, 0), (2, 3), (3, 2))
FAR = ((0, 3), (3, 0), (1, 2), (2, 1))
RELAY = ((0, 2), (3, 1), (2, 3), (1, 0))
TWO = ((0, 2), (2, 0), (1, 3), (3, 1))


def along(block, pairs):
    perm = [(2 * a + c, 2 * b + c) for a, b in pairs for c in range(2)]
    return lax.ppermute(block, "vel", perm)


def other_core(block):
    return lax.ppermute(block, "vel", [(i, i ^ 1) for i in range(8)])


def line_sum(part):
    part = part + other_core(part)
    others = [along(part, pairs) for pairs in (NEAR, TWO, FAR)]
    return part + (others[0] + (others[1] + others[2]))


def tied(*values):
    return lax.optimization_barrier(values)


def line(deviation, collision, vel_order, inflow_value, wall_flag, inflow_flag):
    shape = deviation.shape
    planes, height, depth, local = shape
    cells = planes * height * depth
    parts = part_tiles(local)
    index = lax.axis_index("vel")
    chip, core = index // 2, index % 2
    middle = (chip == 1) | (chip == 2)
    tiles = local // LANES + 1

    def by_tile(rows):
        rows = jnp.pad(rows, ((0, 0), (0, tiles * LANES - local)))
        return rows.reshape(-1, tiles, LANES).transpose(1, 0, 2)

    speed = by_tile(jnp.stack(speeds(vel_order)))
    inflow = by_tile(inflow_value[None, :].astype(jnp.float32))
    code = jnp.where(wall_flag == 1, 2, inflow_flag).reshape(-1, 1)
    forward, backward = ring("space")

    def halo(relaxed):
        low = lax.ppermute(relaxed[-1], "space", forward)
        high = lax.ppermute(relaxed[0], "space", backward)
        return [low, *relaxed, high]

    def pair(blocks):
        return blocks, [other_core(block) for block in blocks]

    start, speed, inflow, code = tied(chip, speed, inflow, code)
    state = pack(deviation)
    for step in range(ITERS):
        final = step == ITERS - 1
        sent = [(along(block, FAR), along(block, NEAR)) for block in state]
        far, near = [f for f, _ in sent], [n for _, n in sent]
        far[0], near[0], start = tied(far[0], near[0], start)
        acc = matmul([pair(state)], [start], core, collision, cells, size=4 * collision.size)[0]
        *both, acc = tied(*far[1:], *near[1:], acc)
        far, near = far[:1] + both[: len(far) - 1], near[:1] + both[len(far) - 1 :]
        rest = jnp.where(middle, jnp.concatenate(far), jnp.concatenate(state))
        rest = along(rest, RELAY)
        acc = matmul([pair(near), pair(far)], [chip ^ 1, chip ^ 3], core, collision, cells, acc)[0]
        rest, acc = tied(rest, acc)
        rest = pair([rest])
        chunks, token = [], None
        for part, block in zip(parts, state):
            *relaxed, token = matmul(
                [rest], [chip ^ 2], core, collision, cells, acc, part, block, planes, token
            )
            chunks.append(halo(relaxed))
        state, done = [], ()
        for part, chunk in zip(parts, chunks):
            result = stream(part, chunk, speed, inflow, code, shape, final, done, token)
            state.append(result[0])
            done = tuple(result) if final else (result[1],)
    partial_sum = done[1][:, 0].reshape(planes, height, depth)
    return state[-1].reshape(shape), line_sum(partial_sum) / jnp.sqrt(jnp.float32(V))


def shards(deviation, collision, *rest):
    planes, _, depth, local = deviation.shape
    fits = local % LANES == HALF and planes % 2 == 0 and depth % 16 == 0 and local > PARTS[-1] * LANES
    body = line if lax.axis_size("vel") == 8 and fits else plain
    return body(deviation, collision, *rest)


def solution(mesh):
    placed = (
        P("space", None, None, "vel"),
        P("vel", None),
        P("vel"),
        P("vel"),
        P("space", None, None),
        P("space", None, None),
    )
    return jax.shard_map(
        shards,
        mesh=mesh,
        in_specs=placed,
        out_specs=(P("space", None, None, "vel"), P("space", None, None)),
        check_vma=False,
    )
```

time: 240 us -> 202 us (0.84)
  waiting for transfers between devices: 123 us -> 67.5 us
  Pallas kernels: 54.3 us -> 65.8 us
  local copies, waits for them, and re-layouts: 1.4 us -> 12.5 us
  starting transfers between devices: 59 us -> 50.4 us
    ppermute x12 -> x21, waiting for transfers between devices: 121 us -> 56 us  [the longest x13 31.2 us: along(): return lax.ppermute(block, 'vel', perm)]
    pallas_call x7 -> x13, Pallas kernels: 54.3 us -> 65.8 us  [the longest x8 59.1 us: matmul(): pl.pallas_call(functools.partial(matmul_kernel, count, pieces, cells, loc...]
    ppermute x9 -> x15, waiting for transfers between devices: 1.19 us -> 11.5 us  [other_core(): return lax.ppermute(block, 'vel', [(i, i ^ 1) for i in range(8)])]
    unnamed x10 -> x36, local copies, waits for them, and re-layouts: 1.2 us -> 11.4 us
    ppermute x12 -> x21, starting transfers between devices: 58 us -> 47.8 us  [the longest x13 36 us: along(): return lax.ppermute(block, 'vel', perm)]
  transfers between devices with their start and end apart: 21 -> 36, of which waited for: 11 -> 21; matrix products, arithmetic and copies ran while one was open for 1% -> 2% of each run, Pallas kernels for 13% -> 25%
where the time goes in v2:
time: 202 us; the launch traced here: 201 us
  waiting for transfers between devices  67.5 us (33%)
  Pallas kernels  65.8 us (33%)
  starting transfers between devices  50.4 us (25%)
  local copies, waits for them, and re-layouts  12.5 us (6%)
  other arithmetic  4.14 us (2%)
    pallas_call x8, Pallas kernels, matmul(): pl.pallas_call(functools.partial(matmul_kernel, count, pieces, cells, loc...  59.1 us
    ppermute x13, starting transfers between devices, along(): return lax.ppermute(block, 'vel', perm)  36 us
    ppermute x13, waiting for transfers between devices, along(): return lax.ppermute(block, 'vel', perm)  31.2 us
    ppermute x4, waiting for transfers between devices, halo(): low = lax.ppermute(relaxed[-1], 'space', forward)  13 us
    ppermute x4, waiting for transfers between devices, halo(): high = lax.ppermute(relaxed[0], 'space', backward)  11.8 us
    ppermute x15, waiting for transfers between devices, other_core(): return lax.ppermute(block, 'vel', [(i, i ^ 1) for i in range(8)])  11.5 us
    unnamed x36, local copies, waits for them, and re-layouts  11.4 us
    ppermute x4, starting transfers between devices, halo(): high = lax.ppermute(relaxed[0], 'space', backward)  6.74 us
  transfers between devices with their start and end apart: 36, of which 21 were waited for; matrix products, arithmetic and copies ran while one was open for 2% of the time, Pallas kernels for 25%

profile of v2, /device:TPU:0, one launch (start us, length us, event | category | flops | bytes accessed | tf_op | source)
XLA Modules:
  0.0 201.2 jit_solution(11423846451314000742)
XLA Ops:
  0.6 1.2 copy-done.8
  2.0 5.1 %collective-permute-start = (bf16[1792,128]{1,0:T(8,128)(2,1)S(1)}, bf16[1792,128]{1,0:T(8,128)(2,1)S(1)}, u32[]{:S(2)}, u32[]{:S(2)}) collective-permute-start(bf16[1792,128]{1,0:T(8,128)(2,1)S(1)} %get-tuple-element.43.refs_0_.refs_4_), channel_id=1, source_target_pairs={{0,24},{4,28},{24,0},{28,4},{8,16},{12,20},{16,8},{20,12},{1,25},{... | collective-permute-start | bytes 1376264 | tf_op jit(solution)/shard_map/ppermute | solution.py:451
  7.6 0.9 collective-permute-start.2
  8.5 0.7 fusion.3
  9.3 0.7 convert_element_type.20
  10.0 8.5 %collective-permute-done.refs_4_ = bf16[1792,128]{1,0:T(8,128)(2,1)S(1)} collective-permute-done((bf16[1792,128]{1,0:T(8,128)(2,1)S(1)}, bf16[1792,128]{1,0:T(8,128)(2,1)S(1)}, u32[]{:S(2)}, u32[]{:S(2)}) %collective-permute-start) | collective-permute-done | bytes 458784 | tf_op jit(solution)/shard_map/ppermute | solution.py:451
  18.5 10.4 %collective-permute-start.3 = (bf16[1664,128]{1,0:T(8,128)(2,1)S(1)}, bf16[1664,128]{1,0:T(8,128)(2,1)}, u32[]{:S(2)}, u32[]{:S(2)}) collective-permute-start(bf16[1664,128]{1,0:T(8,128)(2,1)S(1)} %get-tuple-element.46.refs_1_.refs_4_), channel_id=1, source_target_pairs={{0,8},{4,12},{8,0},{12,4},{16,24},{20,28},{24,16},{28,20},{1,9},{5... | collective-permute-start | bytes 1277960 | tf_op jit(solution)/shard_map/ppermute | solution.py:451
  29.0 0.7 compare_select_fusion
  29.8 0.6 fusion.speed_ref
  30.4 0.8 copy-done.16
  31.2 0.8 copy-done.10
  32.0 1.0 copy-done.11
  33.0 1.0 copy-done.17
  34.0 7.1 %collide.8.refs_9_ = f32[1728,256]{1,0:T(8,128)S(1)} custom-call(s32[1]{0:T(128)} %bitcast.5.chips_ref, s32[1]{0:T(128)} %bitcast.1.core_ref, bf16[1792,128]{1,0:T(8,128)(2,1)S(1)} %get-tuple-element.43.refs_0_.refs_4_, bf16[1664,128]{1,0:T(8,128)(2,1)S(1)} %get-tuple-element.46.refs_1_.refs_4_, bf16[1792,128]{1,0:T(8,128)(2,1)S(1)} %copy-done.11, ...), custom_call_target="tpu_custom_call" | custom-call | flops 95551488 | bytes 95551488 | tf_op jit(solution)/shard_map/collide/pallas_call | solution.py:307
  41.2 4.8 %collective-permute-done.3.refs_1_ = bf16[1664,128]{1,0:T(8,128)(2,1)} collective-permute-done((bf16[1664,128]{1,0:T(8,128)(2,1)S(1)}, bf16[1664,128]{1,0:T(8,128)(2,1)}, u32[]{:S(2)}, u32[]{:S(2)}) %collective-permute-start.3) | collective-permute-done | bytes 426016 | tf_op jit(solution)/shard_map/ppermute | solution.py:451
  45.9 1.1 maximum_select_fusion
  48.8 2.6 %collective-permute-done.10.refs_7_ = bf16[1664,128]{1,0:T(8,128)(2,1)S(1)} collective-permute-done((bf16[1664,128]{1,0:T(8,128)(2,1)S(1)}, bf16[1664,128]{1,0:T(8,128)(2,1)S(1)}, u32[]{:S(2)}, u32[]{:S(2)}) %collective-permute-start.10) | collective-permute-done | bytes 426016 | tf_op jit(solution)/shard_map/ppermute | solution.py:455
  51.3 0.8 copy-done.14
  52.1 0.8 copy-done.12
  52.9 1.0 copy-done.5
  53.9 1.0 copy-done.7
  54.9 1.0 copy-done.13
  55.9 1.0 copy-done.15
  56.9 11.6 %collide.9.refs_3_ = f32[1728,256]{1,0:T(8,128)S(1)} custom-call(s32[2]{0:T(128)S(1)} %pad_add_fusion.chips_ref, s32[1]{0:T(128)} %bitcast.1.core_ref, bf16[1792,128]{1,0:T(8,128)(2,1)} %collective-permute-done.1.refs_0_, bf16[1664,128]{1,0:T(8,128)(2,1)} %collective-permute-done.3.refs_1_, bf16[1792,128]{1,0:T(8,128)(2,1)} %collective-permute-done.7.refs_2_, ...), custom_call_target="tpu_custom_call" | custom-call | flops 1024 | bytes 1024 | tf_op jit(solution)/shard_map/collide/pallas_call | solution.py:307
  68.8 2.6 %collective-permute-done.11.refs_1_ = bf16[3456,128]{1,0:T(8,128)(2,1)S(1)} collective-permute-done((bf16[3456,128]{1,0:T(8,128)(2,1)}, bf16[3456,128]{1,0:T(8,128)(2,1)S(1)}, u32[]{:S(2)}, u32[]{:S(2)}) %collective-permute-start.11) | collective-permute-done | bytes 884768 | tf_op jit(solution)/shard_map/ppermute | solution.py:455
  71.5 1.0 copy-done.1
  72.5 5.8 %collide.10 = (bf16[896,128]{1,0:T(8,128)(2,1)S(1)}, bf16[896,128]{1,0:T(8,128)(2,1)}, f32[8,128]{1,0:T(8,128)S(1)}) custom-call(s32[1]{0:T(128)} %bitcast.chips_ref, s32[1]{0:T(128)} %bitcast.1.core_ref, bf16[3456,128]{1,0:T(8,128)(2,1)} %collective-permute-done.6.refs_0_, bf16[3456,128]{1,0:T(8,128)(2,1)S(1)} %collective-permute-done.11.refs_1_, ...), custom_call_target="tpu_custom_call" | custom-call | flops 1024 | bytes 1024 | tf_op jit(solution)/shard_map/collide/pallas_call | solution.py:307
  78.3 1.5 collective-permute-start.12
  79.8 1.4 collective-permute-start.13
  81.4 4.9 %collide.11 = (bf16[896,128]{1,0:T(8,128)(2,1)S(1)}, bf16[896,128]{1,0:T(8,128)(2,1)S(1)}, f32[8,128]{1,0:T(8,128)S(1)}) custom-call(s32[1]{0:T(128)} %bitcast.chips_ref, s32[1]{0:T(128)} %bitcast.1.core_ref, bf16[3456,128]{1,0:T(8,128)(2,1)} %collective-permute-done.6.refs_0_, bf16[3456,128]{1,0:T(8,128)(2,1)S(1)} %collective-permute-done.11.refs_1_, ...), custom_call_target="tpu_custom_call" | custom-call | flops 1024 | bytes 1024 | tf_op jit(solution)/shard_map/collide/pallas_call | solution.py:307
  86.3 1.7 collective-permute-done.12.refs_0_
  88.0 4.2 %collective-permute-done.13.refs_3_ = bf16[896,128]{1,0:T(8,128)(2,1)} collective-permute-done((bf16[896,128]{1,0:T(8,128)(2,1)S(1)}, bf16[896,128]{1,0:T(8,128)(2,1)}, u32[]{:S(2)}, u32[]{:S(2)}) %collective-permute-start.13) | collective-permute-done | bytes 229408 | tf_op jit(solution)/shard_map/ppermute | solution.py:489
  92.2 2.1 %stream.4 = (bf16[1792,128]{1,0:T(8,128)(2,1)S(1)}, f32[8,128]{1,0:T(8,128)S(1)}) custom-call(f32[8,128]{1,0:T(8,128)S(1)} %get-tuple-element.55._, f32[14,3,128]{2,1,0:T(4,128)S(1)} %copy-done.9, f32[14,1,128]{2,1,0:T(1,128)S(1)} %bitcast_convert_fusion.inflow_ref, s32[256,1]{1,0:T(8,128)S(1)} %copy.8.code_ref, ...), custom_call_target="tpu_custom_call" | custom-call | flops 1024 | bytes 1024 | tf_op jit(solution)/shard_map/stream/pallas_call | solution.py:432
  94.3 3.3 %collective-permute-start.14 = (bf16[1792,128]{1,0:T(8,128)(2,1)S(1)}, bf16[1792,128]{1,0:T(8,128)(2,1)S(1)}, u32[]{:S(2)}, u32[]{:S(2)}) collective-permute-start(bf16[1792,128]{1,0:T(8,128)(2,1)S(1)} %get-tuple-element.61.refs_0_.refs_4_), channel_id=1, source_target_pairs={{0,24},{4,28},{24,0},{28,4},{8,16},{12,20},{16,8},{20,12},{1,25},{... | collective-permute-start | bytes 1376264 | tf_op jit(solution)/shard_map/ppermute | solution.py:451
  97.6 1.5 collective-permute-start.16
  99.1 1.4 collective-permute-start.17
  100.5 6.5 %collective-permute-done.16.refs_0_ = bf16[896,128]{1,0:T(8,128)(2,1)S(1)} collective-permute-done((bf16[896,128]{1,0:T(8,128)(2,1)S(1)}, bf16[896,128]{1,0:T(8,128)(2,1)S(1)}, u32[]{:S(2)}, u32[]{:S(2)}) %collective-permute-start.16) | collective-permute-done | bytes 229408 | tf_op jit(solution)/shard_map/ppermute | solution.py:488
  107.1 2.0 collective-permute-done.17.refs_3_
  109.0 1.5 stream.5
  111.1 9.1 %collective-permute-start.19 = (bf16[1664,128]{1,0:T(8,128)(2,1)S(1)}, bf16[1664,128]{1,0:T(8,128)(2,1)S(1)}, u32[]{:S(2)}, u32[]{:S(2)}) collective-permute-start(bf16[1664,128]{1,0:T(8,128)(2,1)S(1)} %get-tuple-element.66.refs_1_.refs_4_), channel_id=1, source_target_pairs={{0,8},{4,12},{8,0},{12,4},{16,24},{20,28},{24,16},{28,20},{1,9},{5... | collective-permute-start | bytes 1277960 | tf_op jit(solution)/shard_map/ppermute | solution.py:451
  120.2 7.2 %collide.12.refs_9_ = f32[1728,256]{1,0:T(8,128)S(1)} custom-call(s32[1]{0:T(128)} %bitcast.8.chips_ref, s32[1]{0:T(128)} %bitcast.1.core_ref, bf16[1792,128]{1,0:T(8,128)(2,1)S(1)} %get-tuple-element.61.refs_0_.refs_4_, bf16[1664,128]{1,0:T(8,128)(2,1)S(1)} %get-tuple-element.66.refs_1_.refs_4_, bf16[1792,128]{1,0:T(8,128)(2,1)S(1)} %collective-permute-done.20.refs_2_, ...), custom_call_target="tpu_custom_call" | custom-call | flops 95551488 | bytes 95551488 | tf_op jit(solution)/shard_map/collide/pallas_call | solution.py:307
  127.4 1.3 collective-permute-done.18.refs_5_
  128.7 7.4 %collective-permute-done.19.refs_1_ = bf16[1664,128]{1,0:T(8,128)(2,1)S(1)} collective-permute-done((bf16[1664,128]{1,0:T(8,128)(2,1)S(1)}, bf16[1664,128]{1,0:T(8,128)(2,1)S(1)}, u32[]{:S(2)}, u32[]{:S(2)}) %collective-permute-start.19) | collective-permute-done | bytes 426016 | tf_op jit(solution)/shard_map/ppermute | solution.py:451
  136.4 1.5 collective-permute-start.22
  138.9 2.1 %collective-permute-done.24.refs_3_ = bf16[1664,128]{1,0:T(8,128)(2,1)S(1)} collective-permute-done((bf16[1664,128]{1,0:T(8,128)(2,1)S(1)}, bf16[1664,128]{1,0:T(8,128)(2,1)S(1)}, u32[]{:S(2)}, u32[]{:S(2)}) %collective-permute-start.24) | collective-permute-done | bytes 426016 | tf_op jit(solution)/shard_map/ppermute | solution.py:455
  141.6 12.5 %collide.13.refs_3_ = f32[1728,256]{1,0:T(8,128)S(1)} custom-call(s32[2]{0:T(128)S(1)} %pad_add_fusion.chips_ref, s32[1]{0:T(128)} %bitcast.1.core_ref, bf16[1792,128]{1,0:T(8,128)(2,1)S(1)} %collective-permute-done.15.refs_0_, bf16[1664,128]{1,0:T(8,128)(2,1)S(1)} %collective-permute-done.19.refs_1_, bf16[1792,128]{1,0:T(8,128)(2,1)S(1)} %collective-permute-done.23.refs_2_, ...), custom_call_target="tpu_custom_call" | custom-call | flops 1024 | bytes 1024 | tf_op jit(solution)/shard_map/collide/pallas_call | solution.py:307
  154.1 4.0 %collective-permute-done.22.refs_0_ = bf16[3456,128]{1,0:T(8,128)(2,1)S(1)} collective-permute-done((bf16[3456,128]{1,0:T(8,128)(2,1)S(1)}, bf16[3456,128]{1,0:T(8,128)(2,1)S(1)}, u32[]{:S(2)}, u32[]{:S(2)}) %collective-permute-start.22) | collective-permute-done | bytes 884768 | tf_op jit(solution)/shard_map/ppermute | solution.py:451
  158.1 2.4 %collective-permute-done.27.refs_1_ = bf16[3456,128]{1,0:T(8,128)(2,1)S(1)} collective-permute-done((bf16[3456,128]{1,0:T(8,128)(2,1)S(1)}, bf16[3456,128]{1,0:T(8,128)(2,1)S(1)}, u32[]{:S(2)}, u32[]{:S(2)}) %collective-permute-start.27) | collective-permute-done | bytes 884768 | tf_op jit(solution)/shard_map/ppermute | solution.py:455
  160.5 5.1 %collide.14 = (bf16[896,128]{1,0:T(8,128)(2,1)S(1)}, bf16[896,128]{1,0:T(8,128)(2,1)S(1)}, f32[8,128]{1,0:T(8,128)S(1)}) custom-call(s32[1]{0:T(128)} %bitcast.chips_ref, s32[1]{0:T(128)} %bitcast.1.core_ref, bf16[3456,128]{1,0:T(8,128)(2,1)S(1)} %collective-permute-done.22.refs_0_, bf16[3456,128]{1,0:T(8,128)(2,1)S(1)} %collective-permute-done.27.refs_1_, ...), custom_call_target="tpu_custom_call" | custom-call | flops 1024 | bytes 1024 | tf_op jit(solution)/shard_map/collide/pallas_call | solution.py:307
  165.6 1.5 collective-permute-start.30
  167.1 1.5 collective-permute-start.31
  168.6 4.9 %collide.15 = (bf16[896,128]{1,0:T(8,128)(2,1)S(1)}, bf16[896,128]{1,0:T(8,128)(2,1)S(1)}, f32[8,128]{1,0:T(8,128)S(1)}) custom-call(s32[1]{0:T(128)} %bitcast.chips_ref, s32[1]{0:T(128)} %bitcast.1.core_ref, bf16[3456,128]{1,0:T(8,128)(2,1)S(1)} %collective-permute-done.22.refs_0_, bf16[3456,128]{1,0:T(8,128)(2,1)S(1)} %collective-permute-done.27.refs_1_, ...), custom_call_target="tpu_custom_call" | custom-call | flops 1024 | bytes 1024 | tf_op jit(solution)/shard_map/collide/pallas_call | solution.py:307
  174.1 2.4 %collective-permute-start.29 = (bf16[896,128]{1,0:T(8,128)(2,1)S(1)}, bf16[896,128]{1,0:T(8,128)(2,1)S(1)}, u32[]{:S(2)}, u32[]{:S(2)}) collective-permute-start(bf16[896,128]{1,0:T(8,128)(2,1)S(1)} %get-tuple-element.77.refs_1_), channel_id=1, source_target_pairs={{1,0},{2,1},{3,2},{0,3},{5,4},{6,5},{7,6},{4,7},{9,8},{10,9},{11,1... | collective-permute-start | bytes 688136 | tf_op jit(solution)/shard_map/ppermute | solution.py:489
  176.5 2.5 %collective-permute-done.31.refs_3_ = bf16[896,128]{1,0:T(8,128)(2,1)S(1)} collective-permute-done((bf16[896,128]{1,0:T(8,128)(2,1)S(1)}, bf16[896,128]{1,0:T(8,128)(2,1)S(1)}, u32[]{:S(2)}, u32[]{:S(2)}) %collective-permute-start.31) | collective-permute-done | bytes 229408 | tf_op jit(solution)/shard_map/ppermute | solution.py:489
  179.0 1.0 stream.6
  180.0 4.8 %collective-permute-done.28.refs_0_ = bf16[896,128]{1,0:T(8,128)(2,1)S(1)} collective-permute-done((bf16[896,128]{1,0:T(8,128)(2,1)S(1)}, bf16[896,128]{1,0:T(8,128)(2,1)S(1)}, u32[]{:S(2)}, u32[]{:S(2)}) %collective-permute-start.28) | collective-permute-done | bytes 229408 | tf_op jit(solution)/shard_map/ppermute | solution.py:488
  184.8 3.1 %collective-permute-done.29.refs_3_ = bf16[896,128]{1,0:T(8,128)(2,1)S(1)} collective-permute-done((bf16[896,128]{1,0:T(8,128)(2,1)S(1)}, bf16[896,128]{1,0:T(8,128)(2,1)S(1)}, u32[]{:S(2)}, u32[]{:S(2)}) %collective-permute-start.29) | collective-permute-done | bytes 229408 | tf_op jit(solution)/shard_map/ppermute | solution.py:489
  188.0 2.0 stream.7
  190.1 1.2 collective-permute-done.32
  191.3 2.1 %collective-permute-start.33 = (f32[2,8,16]{2,1,0:T(8,128)S(1)}, f32[2,8,16]{2,1,0:T(8,128)S(1)}, u32[]{:S(2)}, u32[]{:S(2)}) collective-permute-start(f32[2,8,16]{2,1,0:T(8,128)S(1)} %add.39), channel_id=1, source_target_pairs={{0,8},{4,12},{8,0},{12,4},{16,24},{20,28},{24,16},{28,20},{1,9},{5... | collective-permute-start | bytes 3080 | tf_op jit(solution)/shard_map/ppermute | solution.py:451
  193.4 1.7 collective-permute-start.34
  195.1 0.6 collective-permute-start.35
  195.7 2.2 %collective-permute-done.34 = f32[2,8,16]{2,1,0:T(8,128)S(1)} collective-permute-done((f32[2,8,16]{2,1,0:T(8,128)S(1)}, f32[2,8,16]{2,1,0:T(8,128)S(1)}, u32[]{:S(2)}, u32[]{:S(2)}) %collective-permute-start.34) | collective-permute-done | bytes 1056 | tf_op jit(solution)/shard_map/ppermute | solution.py:451
  197.9 2.6 %collective-permute-done.35 = f32[2,8,16]{2,1,0:T(8,128)S(1)} collective-permute-done((f32[2,8,16]{2,1,0:T(8,128)S(1)}, f32[2,8,16]{2,1,0:T(8,128)S(1)}, u32[]{:S(2)}, u32[]{:S(2)}) %collective-permute-start.35) | collective-permute-done | bytes 1056 | tf_op jit(solution)/shard_map/ppermute | solution.py:451
  (74 shorter events, 6.9 us)
Async XLA Ops:
  0.6 1.2 copy-start.8
  2.0 44.0 %copy-start = (bf16[1792,128]{1,0:T(8,128)(2,1)}, bf16[1792,128]{1,0:T(8,128)(2,1)S(1)}, u32[]{:S(2)}) copy-start(bf16[1792,128]{1,0:T(8,128)(2,1)S(1)} %get-tuple-element.43.refs_0_.refs_4_) | copy-start | bytes 1376260
  2.0 43.9 %copy-start.2 = (bf16[1664,128]{1,0:T(8,128)(2,1)}, bf16[1664,128]{1,0:T(8,128)(2,1)S(1)}, u32[]{:S(2)}) copy-start(bf16[1664,128]{1,0:T(8,128)(2,1)S(1)} %get-tuple-element.46.refs_1_.refs_4_) | copy-start | bytes 1277956
  2.0 16.6 %collective-permute-start = (bf16[1792,128]{1,0:T(8,128)(2,1)S(1)}, bf16[1792,128]{1,0:T(8,128)(2,1)S(1)}, u32[]{:S(2)}, u32[]{:S(2)}) collective-permute-start(bf16[1792,128]{1,0:T(8,128)(2,1)S(1)} %get-tuple-element.43.refs_0_.refs_4_), channel_id=1, source_target_pairs={{0,24},{4,28},{24,0},{28,4},{8,16},{12,20},{16,8},{20,12},{1,25},{... | collective-permute-start | bytes 1376264 | tf_op jit(solution)/shard_map/ppermute | solution.py:451
  7.1 23.3 %collective-permute-start.1 = (bf16[1792,128]{1,0:T(8,128)(2,1)S(1)}, bf16[1792,128]{1,0:T(8,128)(2,1)}, u32[]{:S(2)}, u32[]{:S(2)}) collective-permute-start(bf16[1792,128]{1,0:T(8,128)(2,1)S(1)} %get-tuple-element.43.refs_0_.refs_4_), channel_id=1, source_target_pairs={{0,8},{4,12},{8,0},{12,4},{16,24},{20,28},{24,16},{28,20},{1,9},{5... | collective-permute-start | bytes 1376264 | tf_op jit(solution)/shard_map/ppermute | solution.py:451
  7.1 24.1 %collective-permute-start.4 = (bf16[1792,128]{1,0:T(8,128)(2,1)S(1)}, bf16[1792,128]{1,0:T(8,128)(2,1)S(1)}, u32[]{:S(2)}, u32[]{:S(2)}) collective-permute-start(bf16[1792,128]{1,0:T(8,128)(2,1)S(1)} %get-tuple-element.43.refs_0_.refs_4_), channel_id=1, source_target_pairs={{0,4},{4,0},{8,12},{12,8},{16,20},{20,16},{24,28},{28,24},{1,5},{5... | collective-permute-start | bytes 1376264 | tf_op jit(solution)/shard_map/ppermute | solution.py:455
  7.1 23.3 %collective-permute-start.5 = (bf16[1664,128]{1,0:T(8,128)(2,1)S(1)}, bf16[1664,128]{1,0:T(8,128)(2,1)S(1)}, u32[]{:S(2)}, u32[]{:S(2)}) collective-permute-start(bf16[1664,128]{1,0:T(8,128)(2,1)S(1)} %get-tuple-element.46.refs_1_.refs_4_), channel_id=1, source_target_pairs={{0,4},{4,0},{8,12},{12,8},{16,20},{20,16},{24,28},{28,24},{1,5},{5... | collective-permute-start | bytes 1277960 | tf_op jit(solution)/shard_map/ppermute | solution.py:455
  7.6 33.5 %collective-permute-start.2 = (bf16[1664,128]{1,0:T(8,128)(2,1)S(1)}, bf16[1664,128]{1,0:T(8,128)(2,1)S(1)}, u32[]{:S(2)}, u32[]{:S(2)}) collective-permute-start(bf16[1664,128]{1,0:T(8,128)(2,1)S(1)} %get-tuple-element.46.refs_1_.refs_4_), channel_id=1, source_target_pairs={{0,24},{4,28},{24,0},{28,4},{8,16},{12,20},{16,8},{20,12},{1,25},{... | collective-permute-start | bytes 1277960 | tf_op jit(solution)/shard_map/ppermute | solution.py:451
  18.5 29.1 %copy-start.4 = (bf16[1792,128]{1,0:T(8,128)(2,1)}, bf16[1792,128]{1,0:T(8,128)(2,1)S(1)}, u32[]{:S(2)}) copy-start(bf16[1792,128]{1,0:T(8,128)(2,1)S(1)} %collective-permute-done.refs_4_) | copy-start | bytes 1376260
  18.5 27.4 %collective-permute-start.3 = (bf16[1664,128]{1,0:T(8,128)(2,1)S(1)}, bf16[1664,128]{1,0:T(8,128)(2,1)}, u32[]{:S(2)}, u32[]{:S(2)}) collective-permute-start(bf16[1664,128]{1,0:T(8,128)(2,1)S(1)} %get-tuple-element.46.refs_1_.refs_4_), channel_id=1, source_target_pairs={{0,8},{4,12},{8,0},{12,4},{16,24},{20,28},{24,16},{28,20},{1,9},{5... | collective-permute-start | bytes 1277960 | tf_op jit(solution)/shard_map/ppermute | solution.py:451
  30.4 0.8 copy-start.16
  31.2 0.8 copy-start.10
  32.0 1.0 copy-start.11
  33.0 1.0 copy-start.17
  41.1 11.0 %copy-start.6 = (bf16[1664,128]{1,0:T(8,128)(2,1)}, bf16[1664,128]{1,0:T(8,128)(2,1)S(1)}, u32[]{:S(2)}) copy-start(bf16[1664,128]{1,0:T(8,128)(2,1)S(1)} %collective-permute-done.2.refs_5_) | copy-start | bytes 1277956
  47.1 21.8 %collective-permute-start.6 = (bf16[3456,128]{1,0:T(8,128)(2,1)}, bf16[3456,128]{1,0:T(8,128)(2,1)}, u32[]{:S(2)}, u32[]{:S(2)}) collective-permute-start(bf16[3456,128]{1,0:T(8,128)(2,1)} %maximum_select_fusion), channel_id=1, source_target_pairs={{0,16},{4,20},{24,8},{28,12},{16,24},{20,28},{8,0},{12,4},{1,17},{... | collective-permute-start | bytes 2654216 | tf_op jit(solution)/shard_map/ppermute | solution.py:451
  47.7 4.4 %collective-permute-start.9 = (bf16[1792,128]{1,0:T(8,128)(2,1)S(1)}, bf16[1792,128]{1,0:T(8,128)(2,1)S(1)}, u32[]{:S(2)}, u32[]{:S(2)}) collective-permute-start(bf16[1792,128]{1,0:T(8,128)(2,1)S(1)} %collective-permute-done.refs_4_), channel_id=1, source_target_pairs={{0,4},{4,0},{8,12},{12,8},{16,20},{20,16},{24,28},{28,24},{1,5},{5... | collective-permute-start | bytes 1376264 | tf_op jit(solution)/shard_map/ppermute | solution.py:455
  47.7 5.2 %collective-permute-start.7 = (bf16[1792,128]{1,0:T(8,128)(2,1)}, bf16[1792,128]{1,0:T(8,128)(2,1)}, u32[]{:S(2)}, u32[]{:S(2)}) collective-permute-start(bf16[1792,128]{1,0:T(8,128)(2,1)} %collective-permute-done.1.refs_0_), channel_id=1, source_target_pairs={{0,4},{4,0},{8,12},{12,8},{16,20},{20,16},{24,28},{28,24},{1,5},{5... | collective-permute-start | bytes 1376264 | tf_op jit(solution)/shard_map/ppermute | solution.py:455
  48.2 3.1 %collective-permute-start.10 = (bf16[1664,128]{1,0:T(8,128)(2,1)S(1)}, bf16[1664,128]{1,0:T(8,128)(2,1)S(1)}, u32[]{:S(2)}, u32[]{:S(2)}) collective-permute-start(bf16[1664,128]{1,0:T(8,128)(2,1)S(1)} %collective-permute-done.2.refs_5_), channel_id=1, source_target_pairs={{0,4},{4,0},{8,12},{12,8},{16,20},{20,16},{24,28},{28,24},{1,5},{5... | collective-permute-start | bytes 1277960 | tf_op jit(solution)/shard_map/ppermute | solution.py:455
  48.2 3.9 %collective-permute-start.8 = (bf16[1664,128]{1,0:T(8,128)(2,1)}, bf16[1664,128]{1,0:T(8,128)(2,1)}, u32[]{:S(2)}, u32[]{:S(2)}) collective-permute-start(bf16[1664,128]{1,0:T(8,128)(2,1)} %collective-permute-done.3.refs_1_), channel_id=1, source_target_pairs={{0,4},{4,0},{8,12},{12,8},{16,20},{20,16},{24,28},{28,24},{1,5},{5... | collective-permute-start | bytes 1277960 | tf_op jit(solution)/shard_map/ppermute | solution.py:455
  51.3 0.8 copy-start.14
  52.1 0.8 copy-start.12
  52.9 1.0 copy-start.5
  53.9 1.0 copy-start.7
  54.9 1.0 copy-start.13
  55.9 1.0 copy-start.15
  68.8 2.6 %collective-permute-start.11 = (bf16[3456,128]{1,0:T(8,128)(2,1)}, bf16[3456,128]{1,0:T(8,128)(2,1)S(1)}, u32[]{:S(2)}, u32[]{:S(2)}) collective-permute-start(bf16[3456,128]{1,0:T(8,128)(2,1)} %collective-permute-done.6.refs_0_), channel_id=1, source_target_pairs={{0,4},{4,0},{8,12},{12,8},{16,20},{20,16},{24,28},{28,24},{1,5},{5... | collective-permute-start | bytes 2654216 | tf_op jit(solution)/shard_map/ppermute | solution.py:455
  71.5 1.0 copy-start.1
  72.5 8.9 %copy-start.3 = (bf16[1664,128]{1,0:T(8,128)(2,1)S(1)}, bf16[1664,128]{1,0:T(8,128)(2,1)}, u32[]{:S(2)}) copy-start(bf16[1664,128]{1,0:T(8,128)(2,1)} %copy-done.2) | copy-start | bytes 1277956
  78.3 9.7 %collective-permute-start.12 = (bf16[896,128]{1,0:T(8,128)(2,1)}, bf16[896,128]{1,0:T(8,128)(2,1)}, u32[]{:S(2)}, u32[]{:S(2)}) collective-permute-start(bf16[896,128]{1,0:T(8,128)(2,1)} %get-tuple-element.59.refs_2_), channel_id=1, source_target_pairs={{0,1},{1,2},{2,3},{3,0},{4,5},{5,6},{6,7},{7,4},{8,9},{9,10},{10,1... | collective-permute-start | bytes 688136 | tf_op jit(solution)/shard_map/ppermute | solution.py:488
  79.8 12.4 %collective-permute-start.13 = (bf16[896,128]{1,0:T(8,128)(2,1)S(1)}, bf16[896,128]{1,0:T(8,128)(2,1)}, u32[]{:S(2)}, u32[]{:S(2)}) collective-permute-start(bf16[896,128]{1,0:T(8,128)(2,1)S(1)} %get-tuple-element.60.refs_1_), channel_id=1, source_target_pairs={{1,0},{2,1},{3,2},{0,3},{5,4},{6,5},{7,6},{4,7},{9,8},{10,9},{11,1... | collective-permute-start | bytes 688136 | tf_op jit(solution)/shard_map/ppermute | solution.py:489
  81.4 10.8 %copy-start.9 = (f32[14,3,128]{2,1,0:T(4,128)S(1)}, f32[14,3,128]{2,1,0:T(4,128)}, u32[]{:S(2)}) copy-start(f32[14,3,128]{2,1,0:T(4,128)} %fusion.speed_ref) | copy-start | bytes 64516
  94.3 16.8 %collective-permute-start.14 = (bf16[1792,128]{1,0:T(8,128)(2,1)S(1)}, bf16[1792,128]{1,0:T(8,128)(2,1)S(1)}, u32[]{:S(2)}, u32[]{:S(2)}) collective-permute-start(bf16[1792,128]{1,0:T(8,128)(2,1)S(1)} %get-tuple-element.61.refs_0_.refs_4_), channel_id=1, source_target_pairs={{0,24},{4,28},{24,0},{28,4},{8,16},{12,20},{16,8},{20,12},{1,25},{... | collective-permute-start | bytes 1376264 | tf_op jit(solution)/shard_map/ppermute | solution.py:451
  97.6 9.4 %collective-permute-start.16 = (bf16[896,128]{1,0:T(8,128)(2,1)S(1)}, bf16[896,128]{1,0:T(8,128)(2,1)S(1)}, u32[]{:S(2)}, u32[]{:S(2)}) collective-permute-start(bf16[896,128]{1,0:T(8,128)(2,1)S(1)} %get-tuple-element.63.refs_2_), channel_id=1, source_target_pairs={{0,1},{1,2},{2,3},{3,0},{4,5},{5,6},{6,7},{7,4},{8,9},{9,10},{10,1... | collective-permute-start | bytes 688136 | tf_op jit(solution)/shard_map/ppermute | solution.py:488
  99.1 9.9 %collective-permute-start.17 = (bf16[896,128]{1,0:T(8,128)(2,1)S(1)}, bf16[896,128]{1,0:T(8,128)(2,1)S(1)}, u32[]{:S(2)}, u32[]{:S(2)}) collective-permute-start(bf16[896,128]{1,0:T(8,128)(2,1)S(1)} %get-tuple-element.64.refs_1_), channel_id=1, source_target_pairs={{1,0},{2,1},{3,2},{0,3},{5,4},{6,5},{7,6},{4,7},{9,8},{10,9},{11,1... | collective-permute-start | bytes 688136 | tf_op jit(solution)/shard_map/ppermute | solution.py:489
  100.5 19.6 %collective-permute-start.15 = (bf16[1792,128]{1,0:T(8,128)(2,1)S(1)}, bf16[1792,128]{1,0:T(8,128)(2,1)S(1)}, u32[]{:S(2)}, u32[]{:S(2)}) collective-permute-start(bf16[1792,128]{1,0:T(8,128)(2,1)S(1)} %get-tuple-element.61.refs_0_.refs_4_), channel_id=1, source_target_pairs={{0,8},{4,12},{8,0},{12,4},{16,24},{20,28},{24,16},{28,20},{1,9},{5... | collective-permute-start | bytes 1376264 | tf_op jit(solution)/shard_map/ppermute | solution.py:451
  100.5 19.6 %collective-permute-start.20 = (bf16[1792,128]{1,0:T(8,128)(2,1)S(1)}, bf16[1792,128]{1,0:T(8,128)(2,1)S(1)}, u32[]{:S(2)}, u32[]{:S(2)}) collective-permute-start(bf16[1792,128]{1,0:T(8,128)(2,1)S(1)} %get-tuple-element.61.refs_0_.refs_4_), channel_id=1, source_target_pairs={{0,4},{4,0},{8,12},{12,8},{16,20},{20,16},{24,28},{28,24},{1,5},{5... | collective-permute-start | bytes 1376264 | tf_op jit(solution)/shard_map/ppermute | solution.py:455
  110.5 9.7 %collective-permute-start.21 = (bf16[1664,128]{1,0:T(8,128)(2,1)S(1)}, bf16[1664,128]{1,0:T(8,128)(2,1)S(1)}, u32[]{:S(2)}, u32[]{:S(2)}) collective-permute-start(bf16[1664,128]{1,0:T(8,128)(2,1)S(1)} %get-tuple-element.66.refs_1_.refs_4_), channel_id=1, source_target_pairs={{0,4},{4,0},{8,12},{12,8},{16,20},{20,16},{24,28},{28,24},{1,5},{5... | collective-permute-start | bytes 1277960 | tf_op jit(solution)/shard_map/ppermute | solution.py:455
  110.5 18.2 %collective-permute-start.18 = (bf16[1664,128]{1,0:T(8,128)(2,1)S(1)}, bf16[1664,128]{1,0:T(8,128)(2,1)S(1)}, u32[]{:S(2)}, u32[]{:S(2)}) collective-permute-start(bf16[1664,128]{1,0:T(8,128)(2,1)S(1)} %get-tuple-element.66.refs_1_.refs_4_), channel_id=1, source_target_pairs={{0,24},{4,28},{24,0},{28,4},{8,16},{12,20},{16,8},{20,12},{1,25},{... | collective-permute-start | bytes 1277960 | tf_op jit(solution)/shard_map/ppermute | solution.py:451
  111.1 25.0 %collective-permute-start.19 = (bf16[1664,128]{1,0:T(8,128)(2,1)S(1)}, bf16[1664,128]{1,0:T(8,128)(2,1)S(1)}, u32[]{:S(2)}, u32[]{:S(2)}) collective-permute-start(bf16[1664,128]{1,0:T(8,128)(2,1)S(1)} %get-tuple-element.66.refs_1_.refs_4_), channel_id=1, source_target_pairs={{0,8},{4,12},{8,0},{12,4},{16,24},{20,28},{24,16},{28,20},{1,9},{5... | collective-permute-start | bytes 1277960 | tf_op jit(solution)/shard_map/ppermute | solution.py:451
  136.4 21.7 %collective-permute-start.22 = (bf16[3456,128]{1,0:T(8,128)(2,1)S(1)}, bf16[3456,128]{1,0:T(8,128)(2,1)S(1)}, u32[]{:S(2)}, u32[]{:S(2)}) collective-permute-start(bf16[3456,128]{1,0:T(8,128)(2,1)S(1)} %maximum_select_fusion.1), channel_id=1, source_target_pairs={{0,16},{4,20},{24,8},{28,12},{16,24},{20,28},{8,0},{12,4},{1,17},{... | collective-permute-start | bytes 2654216 | tf_op jit(solution)/shard_map/ppermute | solution.py:451
  137.9 3.7 %collective-permute-start.23 = (bf16[1792,128]{1,0:T(8,128)(2,1)S(1)}, bf16[1792,128]{1,0:T(8,128)(2,1)S(1)}, u32[]{:S(2)}, u32[]{:S(2)}) collective-permute-start(bf16[1792,128]{1,0:T(8,128)(2,1)S(1)} %collective-permute-done.15.refs_0_), channel_id=1, source_target_pairs={{0,4},{4,0},{8,12},{12,8},{16,20},{20,16},{24,28},{28,24},{1,5},{5... | collective-permute-start | bytes 1376264 | tf_op jit(solution)/shard_map/ppermute | solution.py:455
  137.9 3.7 %collective-permute-start.25 = (bf16[1792,128]{1,0:T(8,128)(2,1)S(1)}, bf16[1792,128]{1,0:T(8,128)(2,1)S(1)}, u32[]{:S(2)}, u32[]{:S(2)}) collective-permute-start(bf16[1792,128]{1,0:T(8,128)(2,1)S(1)} %collective-permute-done.14.refs_4_), channel_id=1, source_target_pairs={{0,4},{4,0},{8,12},{12,8},{16,20},{20,16},{24,28},{28,24},{1,5},{5... | collective-permute-start | bytes 1376264 | tf_op jit(solution)/shard_map/ppermute | solution.py:455
  138.4 2.6 %collective-permute-start.24 = (bf16[1664,128]{1,0:T(8,128)(2,1)S(1)}, bf16[1664,128]{1,0:T(8,128)(2,1)S(1)}, u32[]{:S(2)}, u32[]{:S(2)}) collective-permute-start(bf16[1664,128]{1,0:T(8,128)(2,1)S(1)} %collective-permute-done.19.refs_1_), channel_id=1, source_target_pairs={{0,4},{4,0},{8,12},{12,8},{16,20},{20,16},{24,28},{28,24},{1,5},{5... | collective-permute-start | bytes 1277960 | tf_op jit(solution)/shard_map/ppermute | solution.py:455
  138.4 3.2 %collective-permute-start.26 = (bf16[1664,128]{1,0:T(8,128)(2,1)S(1)}, bf16[1664,128]{1,0:T(8,128)(2,1)S(1)}, u32[]{:S(2)}, u32[]{:S(2)}) collective-permute-start(bf16[1664,128]{1,0:T(8,128)(2,1)S(1)} %collective-permute-done.18.refs_5_), channel_id=1, source_target_pairs={{0,4},{4,0},{8,12},{12,8},{16,20},{20,16},{24,28},{28,24},{1,5},{5... | collective-permute-start | bytes 1277960 | tf_op jit(solution)/shard_map/ppermute | solution.py:455
  158.1 2.4 %collective-permute-start.27 = (bf16[3456,128]{1,0:T(8,128)(2,1)S(1)}, bf16[3456,128]{1,0:T(8,128)(2,1)S(1)}, u32[]{:S(2)}, u32[]{:S(2)}) collective-permute-start(bf16[3456,128]{1,0:T(8,128)(2,1)S(1)} %collective-permute-done.22.refs_0_), channel_id=1, source_target_pairs={{0,4},{4,0},{8,12},{12,8},{16,20},{20,16},{24,28},{28,24},{1,5},{5... | collective-permute-start | bytes 2654216 | tf_op jit(solution)/shard_map/ppermute | solution.py:455
  165.6 10.9 %collective-permute-start.30 = (bf16[896,128]{1,0:T(8,128)(2,1)S(1)}, bf16[896,128]{1,0:T(8,128)(2,1)S(1)}, u32[]{:S(2)}, u32[]{:S(2)}) collective-permute-start(bf16[896,128]{1,0:T(8,128)(2,1)S(1)} %get-tuple-element.78.refs_2_), channel_id=1, source_target_pairs={{0,1},{1,2},{2,3},{3,0},{4,5},{5,6},{6,7},{7,4},{8,9},{9,10},{10,1... | collective-permute-start | bytes 688136 | tf_op jit(solution)/shard_map/ppermute | solution.py:488
  167.1 11.9 %collective-permute-start.31 = (bf16[896,128]{1,0:T(8,128)(2,1)S(1)}, bf16[896,128]{1,0:T(8,128)(2,1)S(1)}, u32[]{:S(2)}, u32[]{:S(2)}) collective-permute-start(bf16[896,128]{1,0:T(8,128)(2,1)S(1)} %get-tuple-element.79.refs_1_), channel_id=1, source_target_pairs={{1,0},{2,1},{3,2},{0,3},{5,4},{6,5},{7,6},{4,7},{9,8},{10,9},{11,1... | collective-permute-start | bytes 688136 | tf_op jit(solution)/shard_map/ppermute | solution.py:489
  173.5 11.3 %collective-permute-start.28 = (bf16[896,128]{1,0:T(8,128)(2,1)S(1)}, bf16[896,128]{1,0:T(8,128)(2,1)S(1)}, u32[]{:S(2)}, u32[]{:S(2)}) collective-permute-start(bf16[896,128]{1,0:T(8,128)(2,1)S(1)} %get-tuple-element.76.refs_2_), channel_id=1, source_target_pairs={{0,1},{1,2},{2,3},{3,0},{4,5},{5,6},{6,7},{7,4},{8,9},{9,10},{10,1... | collective-permute-start | bytes 688136 | tf_op jit(solution)/shard_map/ppermute | solution.py:488
  174.1 13.9 %collective-permute-start.29 = (bf16[896,128]{1,0:T(8,128)(2,1)S(1)}, bf16[896,128]{1,0:T(8,128)(2,1)S(1)}, u32[]{:S(2)}, u32[]{:S(2)}) collective-permute-start(bf16[896,128]{1,0:T(8,128)(2,1)S(1)} %get-tuple-element.77.refs_1_), channel_id=1, source_target_pairs={{1,0},{2,1},{3,2},{0,3},{5,4},{6,5},{7,6},{4,7},{9,8},{10,9},{11,1... | collective-permute-start | bytes 688136 | tf_op jit(solution)/shard_map/ppermute | solution.py:489
  190.1 1.2 collective-permute-start.32
  191.3 4.5 %collective-permute-start.33 = (f32[2,8,16]{2,1,0:T(8,128)S(1)}, f32[2,8,16]{2,1,0:T(8,128)S(1)}, u32[]{:S(2)}, u32[]{:S(2)}) collective-permute-start(f32[2,8,16]{2,1,0:T(8,128)S(1)} %add.39), channel_id=1, source_target_pairs={{0,8},{4,12},{8,0},{12,4},{16,24},{20,28},{24,16},{28,20},{1,9},{5... | collective-permute-start | bytes 3080 | tf_op jit(solution)/shard_map/ppermute | solution.py:451
  193.4 4.5 %collective-permute-start.34 = (f32[2,8,16]{2,1,0:T(8,128)S(1)}, f32[2,8,16]{2,1,0:T(8,128)S(1)}, u32[]{:S(2)}, u32[]{:S(2)}) collective-permute-start(f32[2,8,16]{2,1,0:T(8,128)S(1)} %add.39), channel_id=1, source_target_pairs={{0,16},{4,20},{16,0},{20,4},{8,24},{12,28},{24,8},{28,12},{1,17},{... | collective-permute-start | bytes 3080 | tf_op jit(solution)/shard_map/ppermute | solution.py:451
  195.1 5.4 %collective-permute-start.35 = (f32[2,8,16]{2,1,0:T(8,128)S(1)}, f32[2,8,16]{2,1,0:T(8,128)S(1)}, u32[]{:S(2)}, u32[]{:S(2)}) collective-permute-start(f32[2,8,16]{2,1,0:T(8,128)S(1)} %add.39), channel_id=1, source_target_pairs={{0,24},{4,28},{24,0},{28,4},{8,16},{12,20},{16,8},{20,12},{1,25},{... | collective-permute-start | bytes 3080 | tf_op jit(solution)/shard_map/ppermute | solution.py:451

commit v3 on v2

--- a/solution.py
+++ b/solution.py
@@ -71,7 +71,8 @@
     return state, lax.psum(partial_sum, "vel") / jnp.sqrt(jnp.float32(V))
 
 
-PARTS = (7,)
+PARTS = ((6,), (8,))
+BLOCKS = (3, 6)
 
 
 def vmem(count):
@@ -90,9 +91,13 @@
     return pl.ds(pl.multiple_of(start, 16), size)
 
 
-def part_tiles(local):
-    cuts = (0, *PARTS, local // LANES + 1)
+def spans(cuts, local):
+    cuts = (0, *cuts, local // LANES + 1)
     return list(zip(cuts[:-1], cuts[1:]))
+
+
+def blocks_of(part, local):
+    return [span for span in spans(BLOCKS, local) if part[0] <= span[0] < part[1]]
 
 
 def packed_rows(first, end, cells, local):
@@ -104,7 +109,7 @@
     cells = planes * height * depth
     half = cells // 2
     full = local // LANES
-    for (first, end), out_ref in zip(part_tiles(local), outs):
+    for (first, end), out_ref in zip(spans((), local), outs):
         for x in range(planes):
             for y in range(height):
                 at = (x * height + y) * depth
@@ -126,7 +131,7 @@
     cells = planes * height * depth
     out_shape = [
         jax.ShapeDtypeStruct((packed_rows(*part, cells, local), LANES), jnp.bfloat16)
-        for part in part_tiles(local)
+        for part in spans((), local)
     ]
     return pl.pallas_call(
         pack_kernel,
@@ -339,15 +344,16 @@
     planes, height, depth, local = shape
     refs = list(refs)
     plane_refs = [refs.pop(0) for _ in range(planes + 2)]
-    done = [refs.pop(0) for _ in range(2 if final else 1)] if part[0] > 0 else None
-    out_ref = refs.pop(0)
+    done_ref = refs.pop(0) if part[0] > 0 else None
     first, end = part
+    blocks = [part] if final else blocks_of(part, local)
+    out_refs = [refs.pop(0) for _ in blocks]
     full = local // LANES
     size = height * depth
     cells = planes * size
     half = cells // 2
 
-    def tile(t, tail):
+    def tile(t, tail, out_ref, begin):
         def plane(x, y):
             at = t * size + y % height * depth
             return plane_refs[x + 1][rows_at(at, depth), :].astype(jnp.float32)
@@ -375,43 +381,32 @@
                 code = code_ref[here, :]
                 total = jnp.where(code == 0, total, jnp.where(code == 1, inflow, 0.0))
                 total = total.astype(jnp.bfloat16)
-                if final:
-                    wide = total.astype(jnp.float32)
-                    if tail:
-                        out_ref[here, full * LANES : local] = total[:, :HALF]
-                        lane = lax.broadcasted_iota(jnp.int32, wide.shape, 1)
-                        wide = jnp.where(lane < HALF, wide, 0.0)
-                    else:
-                        lanes = pl.ds(pl.multiple_of((place + t) * LANES, LANES), LANES)
-                        out_ref[here, lanes] = total
-                    refs[0][here, :] += wide
+                if final and tail:
+                    out_ref[here, full * LANES : local] = total[:, :HALF]
+                elif final:
+                    lanes = pl.ds(pl.multiple_of((first + t) * LANES, LANES), LANES)
+                    out_ref[here, lanes] = total
                 elif tail:
                     side = 0 if at < half else 1
-                    to = t * cells + at - side * half
+                    to = (first + t - begin) * cells + at - side * half
                     out_ref[to : to + depth, side * HALF : (side + 1) * HALF] = total[:, :HALF]
                 else:
-                    out_ref[rows_at(t * cells + at, depth), :] = total
-
-    place = 0
+                    out_ref[rows_at((first + t - begin) * cells + at, depth), :] = total
+
     if not final:
         refs[0][...] = jnp.zeros_like(refs[0])
-    if final:
-        if done is None:
-            refs[0][...] = jnp.zeros_like(refs[0])
-        else:
-            place = first
-            out_ref[:, 0 : first * LANES] = done[0][...]
-            refs[0][...] = done[1][...]
-
-    def body(t, carry):
-        tile(t, False)
-        return carry
-
-    lax.fori_loop(0, min(end, full) - first, body, 0)
-    if end > full:
-        tile(full - first, True)
-        if final:
-            refs[0][:, 0:1] = jnp.sum(refs[0][...], axis=1, keepdims=True)
+    elif first > 0:
+        out_refs[0][:, 0 : first * LANES] = done_ref[...]
+
+    for (begin, stop), out_ref in zip(blocks, out_refs):
+
+        def body(t, carry):
+            tile(t, False, out_ref, begin)
+            return carry
+
+        lax.fori_loop(begin - first, min(stop, full) - first, body, 0)
+        if stop > full:
+            tile(full - first, True, out_ref, begin)
 
 
 def stream(part, planes, speed, inflow, code, shape, final, done, token):
@@ -419,16 +414,12 @@
     operands = [token, speed, inflow, code, *planes, *done]
     if final:
         width = min(part[1] * LANES, local)
+        out_shape = [jax.ShapeDtypeStruct((cells, width), jnp.bfloat16)]
+    else:
         out_shape = [
-            jax.ShapeDtypeStruct((cells, width), jnp.bfloat16),
-            jax.ShapeDtypeStruct((cells, LANES), jnp.float32),
-        ]
-    else:
-        rows = packed_rows(*part, cells, local)
-        out_shape = [
-            jax.ShapeDtypeStruct((rows, LANES), jnp.bfloat16),
-            jax.ShapeDtypeStruct((8, LANES), jnp.float32),
-        ]
+            jax.ShapeDtypeStruct((packed_rows(*span, cells, local), LANES), jnp.bfloat16)
+            for span in blocks_of(part, local)
+        ] + [jax.ShapeDtypeStruct((8, LANES), jnp.float32)]
     return pl.pallas_call(
         functools.partial(stream_kernel, part, shape, final),
         out_shape=out_shape,
@@ -455,10 +446,102 @@
     return lax.ppermute(block, "vel", [(i, i ^ 1) for i in range(8)])
 
 
-def line_sum(part):
+def totals_kernel(
+    parts, shape, speed_ref, inflow_ref, code_ref, *refs
+):
+    planes, height, depth, local = shape
+    refs = list(refs)
+    plane_refs = [[refs.pop(0) for _ in range(planes)] for _ in parts]
+    sum_ref, forward_ref, backward_ref, token_ref, wide_ref, ends_ref, inflow_sum_ref = refs
+    size = height * depth
+    token_ref[...] = jnp.zeros_like(token_ref)
+    wide_ref[...] = jnp.zeros_like(wide_ref)
+    ends_ref[...] = jnp.zeros_like(ends_ref)
+    inflow_sum_ref[...] = jnp.zeros_like(inflow_sum_ref)
+    for (first, end), mine in zip(parts, plane_refs):
+
+        def body(t, carry):
+            def plane(x, y):
+                at = t * size + y % height * depth
+                return mine[x][rows_at(at, depth), :].astype(jnp.float32)
+
+            speed = [speed_ref[first + t, d : d + 1, :] for d in range(3)]
+            fast = [jnp.abs(s) for s in speed]
+            up = [s > 0 for s in speed]
+            rise, fall = jnp.where(up[0], fast[0], 0.0), jnp.where(up[0], 0.0, fast[0])
+            stay = 1.0 - (fast[0] + fast[1] + fast[2])
+            inflow_sum_ref[0:1, :] += inflow_ref[first + t, 0:1, :]
+            for x in range(planes):
+                for y in range(height):
+                    field = plane(x, y)
+                    total = stay * field
+                    if x > 0:
+                        total = total + rise * plane(x - 1, y)
+                    if x < planes - 1:
+                        total = total + fall * plane(x + 1, y)
+                    near = jnp.where(up[1], plane(x, y - 1), plane(x, y + 1))
+                    total = total + fast[1] * near
+                    lower, upper = pltpu.roll(field, 1, 0), pltpu.roll(field, depth - 1, 0)
+                    total = total + fast[2] * jnp.where(up[2], lower, upper)
+                    at = (x * height + y) * depth
+                    wide_ref[at : at + depth, :] += total
+                    at = y * depth
+                    if x == planes - 1:
+                        ends_ref[0, at : at + depth, :] += rise * field
+                    if x == 0:
+                        ends_ref[1, at : at + depth, :] += fall * field
+            return carry
+
+        lax.fori_loop(0, end - first, body, 0)
+    flowing = jnp.sum(inflow_sum_ref[0:1, :], axis=1, keepdims=True)
+    total = jnp.sum(wide_ref[...], axis=1, keepdims=True)
+    code = code_ref[...]
+    sum_ref[...] = jnp.where(code == 0, total, jnp.where(code == 1, flowing, 0.0))
+    forward_ref[...] = jnp.sum(ends_ref[0], axis=1, keepdims=True)
+    backward_ref[...] = jnp.sum(ends_ref[1], axis=1, keepdims=True)
+
+
+def totals(chunks, speed, inflow, code, shape, parts):
+    planes, height, depth, _ = shape
+    size = height * depth
+    operands = [speed, inflow, code] + [a for chunk in chunks for a in chunk[1:-1]]
+    part, ahead, behind, token = pl.pallas_call(
+        functools.partial(totals_kernel, tuple(parts), shape),
+        out_shape=[
+            jax.ShapeDtypeStruct((planes * size, 1), jnp.float32),
+            jax.ShapeDtypeStruct((size, 1), jnp.float32),
+            jax.ShapeDtypeStruct((size, 1), jnp.float32),
+            jax.ShapeDtypeStruct((8, LANES), jnp.float32),
+        ],
+        in_specs=vmem(len(operands)),
+        out_specs=vmem(4),
+        scratch_shapes=[
+            pltpu.VMEM((planes * size, LANES), jnp.float32),
+            pltpu.VMEM((2, size, LANES), jnp.float32),
+            pltpu.VMEM((8, LANES), jnp.float32),
+        ],
+        compiler_params=params(),
+        cost_estimate=cost(),
+        name="totals",
+    )(*operands)
+    return token, part, ahead, behind
+
+
+def density_of(part, ahead, behind, code, shape, first, second):
+    planes, height, depth, _ = shape
+    ahead, behind, _ = tied(ahead, behind, first)
+    forward, backward = ring("space")
+    low = lax.ppermute(ahead.reshape(1, height, depth), "space", forward)
+    high = lax.ppermute(behind.reshape(1, height, depth), "space", backward)
+    none = jnp.zeros((planes - 1, height, depth), jnp.float32)
+    ends = jnp.concatenate([low, none]) + jnp.concatenate([none, high])
+    free = code.reshape(planes, height, depth) == 0
+    part = part.reshape(planes, height, depth) + jnp.where(free, ends, 0.0)
     part = part + other_core(part)
+    part, _ = tied(part, second)
     others = [along(part, pairs) for pairs in (NEAR, TWO, FAR)]
-    return part + (others[0] + (others[1] + others[2]))
+    part = part + (others[0] + (others[1] + others[2]))
+    return part / jnp.sqrt(jnp.float32(V))
 
 
 def tied(*values):
@@ -469,7 +552,6 @@
     shape = deviation.shape
     planes, height, depth, local = shape
     cells = planes * height * depth
-    parts = part_tiles(local)
     index = lax.axis_index("vel")
     chip, core = index // 2, index % 2
     middle = (chip == 1) | (chip == 2)
@@ -498,33 +580,41 @@
         final = step == ITERS - 1
         sent = [(along(block, FAR), along(block, NEAR)) for block in state]
         far, near = [f for f, _ in sent], [n for _, n in sent]
-        far[0], near[0], start = tied(far[0], near[0], start)
-        acc = matmul([pair(state)], [start], core, collision, cells, size=4 * collision.size)[0]
-        *both, acc = tied(*far[1:], *near[1:], acc)
-        far, near = far[:1] + both[: len(far) - 1], near[:1] + both[len(far) - 1 :]
-        rest = jnp.where(middle, jnp.concatenate(far), jnp.concatenate(state))
-        rest = along(rest, RELAY)
+        parts = spans(PARTS[step], local)
+        early = len(state) - 1
+        if early:
+            *far[:early], start = tied(*far[:early], start)
+        acc = matmul([pair(state)], [start], core, collision, cells)[0]
+        *both, acc = tied(*far[early:], *near, acc)
+        far[early:], near = both[:1], both[1:]
+        whole = jnp.concatenate(state)
+        rest = along(jnp.where(middle, jnp.concatenate(far), whole), RELAY)
         acc = matmul([pair(near), pair(far)], [chip ^ 1, chip ^ 3], core, collision, cells, acc)[0]
         rest, acc = tied(rest, acc)
         rest = pair([rest])
-        chunks, token = [], None
-        for part, block in zip(parts, state):
+        chunks, token, at = [], None, 0
+        for part in parts:
+            mine = whole[at : at + packed_rows(*part, cells, local)]
+            at += mine.shape[0]
             *relaxed, token = matmul(
-                [rest], [chip ^ 2], core, collision, cells, acc, part, block, planes, token
+                [rest], [chip ^ 2], core, collision, cells, acc, part, mine, planes, token
             )
             chunks.append(halo(relaxed))
-        state, done = [], ()
+        if final:
+            token, *sums = totals(chunks, speed, inflow, code, shape, parts)
+        state, done, firsts = [], (), []
         for part, chunk in zip(parts, chunks):
-            result = stream(part, chunk, speed, inflow, code, shape, final, done, token)
-            state.append(result[0])
-            done = tuple(result) if final else (result[1],)
-    partial_sum = done[1][:, 0].reshape(planes, height, depth)
-    return state[-1].reshape(shape), line_sum(partial_sum) / jnp.sqrt(jnp.float32(V))
+            *blocks, last = stream(part, chunk, speed, inflow, code, shape, final, done, token)
+            state += blocks
+            firsts.append(last)
+            done = (last,)
+    density = density_of(*sums, code, shape, chunks[0][0], firsts[0])
+    return last.reshape(shape), density
 
 
 def shards(deviation, collision, *rest):
     planes, _, depth, local = deviation.shape
-    fits = local % LANES == HALF and planes % 2 == 0 and depth % 16 == 0 and local > PARTS[-1] * LANES
+    fits = local % LANES == HALF and planes % 2 == 0 and depth % 16 == 0 and local > max(sum(PARTS, ())) * LANES
     body = line if lax.axis_size("vel") == 8 and fits else plain
     return body(deviation, collision, *rest)
 

time: 202 us -> 194 us (0.960)
  waiting for transfers between devices: 67.5 us -> 54.3 us
  starting transfers between devices: 50.4 us -> 54 us
  Pallas kernels: 65.8 us -> 68.6 us
    ppermute x4, waiting for transfers between devices: 13 us -> 0.76 us  [halo(): low = lax.ppermute(relaxed[-1], 'space', forward)]
    ppermute x13, waiting for transfers between devices: 31.2 us -> 36.8 us  [along(): return lax.ppermute(block, 'vel', perm)]
    ppermute x4, waiting for transfers between devices: 11.8 us -> 6.6 us  [halo(): high = lax.ppermute(relaxed[0], 'space', backward)]
    unnamed x36 -> x22, local copies, waits for them, and re-layouts: 11.4 us -> 7.21 us
    ppermute x0 -> x2, starting transfers between devices: none -> 2.96 us  [the longest x1 2.35 us: density_of(): high = lax.ppermute(behind.reshape(1, height, depth), 'space', backward)]
  transfers between devices with their start and end apart: 36 -> 38, of which waited for: 21 -> 18; matrix products, arithmetic and copies ran while one was open for 2% -> 4% of each run, Pallas kernels for 25% -> 30%
where the time goes in v3:
time: 194 us
  Pallas kernels  68.6 us (35%)
  waiting for transfers between devices  54.3 us (28%)
  starting transfers between devices  54 us (28%)
  local copies, waits for them, and re-layouts  11 us (6%)
  other arithmetic  5.09 us (3%)
    pallas_call x8, Pallas kernels, matmul(): pl.pallas_call(functools.partial(matmul_kernel, count, pieces, cells, loc...  60.5 us
    ppermute x13, waiting for transfers between devices, along(): return lax.ppermute(block, 'vel', perm)  36.8 us
    ppermute x13, starting transfers between devices, along(): return lax.ppermute(block, 'vel', perm)  36.1 us
    ppermute x15, waiting for transfers between devices, other_core(): return lax.ppermute(block, 'vel', [(i, i ^ 1) for i in range(8)])  10.1 us
    ppermute x4, starting transfers between devices, halo(): high = lax.ppermute(relaxed[0], 'space', backward)  8.16 us
    unnamed x22, local copies, waits for them, and re-layouts  7.21 us
    ppermute x4, waiting for transfers between devices, halo(): high = lax.ppermute(relaxed[0], 'space', backward)  6.6 us
    pallas_call x4, Pallas kernels, stream(): pl.pallas_call(functools.partial(stream_kernel, part, shape, final), out_...  6.57 us
  transfers between devices with their start and end apart: 38, of which 18 were waited for; matrix products, arithmetic and copies ran while one was open for 4% of the time, Pallas kernels for 30%

profile of v3, /device:TPU:0, one launch (start us, length us, event | category | flops | bytes accessed | tf_op | source)
XLA Modules:
  0.0 193.9 jit_solution(16176309010444243524)
XLA Ops:
  0.6 1.2 copy-done.3
  2.5 4.7 %collective-permute-start = (bf16[3456,128]{1,0:T(8,128)(2,1)S(1)}, bf16[3456,128]{1,0:T(8,128)(2,1)S(1)}, u32[]{:S(2)}, u32[]{:S(2)}) collective-permute-start(bf16[3456,128]{1,0:T(8,128)(2,1)S(1)} %pack.1.refs_0_), channel_id=1, source_target_pairs={{0,24},{4,28},{24,0},{28,4},{8,16},{12,20},{16,8},{20,12},{1,25},{... | collective-permute-start | bytes 2654216 | tf_op jit(solution)/shard_map/ppermute | solution.py:442
  7.2 0.6 stack.37
  7.8 0.6 stack.38
  8.4 1.3 convert_element_type.20
  9.7 0.7 compare_select_fusion
  10.4 0.7 reshape.28
  11.1 0.7 bitcast_convert_fusion.inflow_ref
  11.8 1.3 fusion.speed_ref
  13.2 6.5 %collide.8.refs_5_ = f32[1728,256]{1,0:T(8,128)S(1)} custom-call(s32[1]{0:T(128)} %bitcast.5.chips_ref, s32[1]{0:T(128)} %bitcast.4.core_ref, bf16[3456,128]{1,0:T(8,128)(2,1)S(1)} %pack.1.refs_0_, bf16[3456,128]{1,0:T(8,128)(2,1)S(1)} %collective-permute-done.2.refs_1_, bf16[1728,13824]{1,0:T(8,128)(2,1)} %refs_2_.9), custom_call_target="tpu_custom_call" | custom-call | flops 1024 | bytes 1024 | tf_op jit(solution)/shard_map/collide/pallas_call | solution.py:312
  19.7 1.2 copy-done
  20.9 6.9 %collective-permute-done.refs_2_ = bf16[3456,128]{1,0:T(8,128)(2,1)S(1)} collective-permute-done((bf16[3456,128]{1,0:T(8,128)(2,1)S(1)}, bf16[3456,128]{1,0:T(8,128)(2,1)S(1)}, u32[]{:S(2)}, u32[]{:S(2)}) %collective-permute-start) | collective-permute-done | bytes 884768 | tf_op jit(solution)/shard_map/ppermute | solution.py:442
  27.8 18.7 %collective-permute-done.1.refs_0_ = bf16[3456,128]{1,0:T(8,128)(2,1)S(1)} collective-permute-done((bf16[3456,128]{1,0:T(8,128)(2,1)S(1)}, bf16[3456,128]{1,0:T(8,128)(2,1)S(1)}, u32[]{:S(2)}, u32[]{:S(2)}) %collective-permute-start.1) | collective-permute-done | bytes 884768 | tf_op jit(solution)/shard_map/ppermute | solution.py:442
  47.0 1.0 broadcast_select_fusion
  48.0 0.6 collective-permute-start.3
  48.7 1.1 collective-permute-done.4.refs_1_
  49.8 0.9 copy-done.6
  50.7 1.5 copy-done.1
  52.2 1.2 copy-done.5
  53.4 1.2 copy-done.7
  54.5 11.2 %collide.9.refs_3_ = f32[1728,256]{1,0:T(8,128)S(1)} custom-call(s32[2]{0:T(128)S(1)} %pad_add_fusion.chips_ref, s32[1]{0:T(128)} %bitcast.4.core_ref, bf16[3456,128]{1,0:T(8,128)(2,1)S(1)} %copy-done.5, bf16[3456,128]{1,0:T(8,128)(2,1)S(1)} %copy-done.7, bf16[3456,128]{1,0:T(8,128)(2,1)S(1)} %collective-permute-done.refs_2_, ...), custom_call_target="tpu_custom_call" | custom-call | flops 1024 | bytes 1024 | tf_op jit(solution)/shard_map/collide/pallas_call | solution.py:312
  65.8 4.1 %collective-permute-done.3.refs_0_ = bf16[3456,128]{1,0:T(8,128)(2,1)} collective-permute-done((bf16[3456,128]{1,0:T(8,128)(2,1)}, bf16[3456,128]{1,0:T(8,128)(2,1)}, u32[]{:S(2)}, u32[]{:S(2)}) %collective-permute-start.3) | collective-permute-done | bytes 884768 | tf_op jit(solution)/shard_map/ppermute | solution.py:442
  69.9 2.6 %collective-permute-done.6.refs_1_ = bf16[3456,128]{1,0:T(8,128)(2,1)S(1)} collective-permute-done((bf16[3456,128]{1,0:T(8,128)(2,1)}, bf16[3456,128]{1,0:T(8,128)(2,1)S(1)}, u32[]{:S(2)}, u32[]{:S(2)}) %collective-permute-start.6) | collective-permute-done | bytes 884768 | tf_op jit(solution)/shard_map/ppermute | solution.py:446
  72.5 5.3 %collide.10 = (bf16[768,128]{1,0:T(8,128)(2,1)}, bf16[768,128]{1,0:T(8,128)(2,1)}, f32[8,128]{1,0:T(8,128)S(1)}) custom-call(s32[1]{0:T(128)} %bitcast.3.chips_ref, s32[1]{0:T(128)} %bitcast.4.core_ref, bf16[3456,128]{1,0:T(8,128)(2,1)} %collective-permute-done.3.refs_0_, bf16[3456,128]{1,0:T(8,128)(2,1)S(1)} %collective-permute-done.6.refs_1_, ...), custom_call_target="tpu_custom_call" | custom-call | flops 1024 | bytes 1024 | tf_op jit(solution)/shard_map/collide/pallas_call | solution.py:312
  77.9 1.5 collective-permute-start.7
  79.4 1.4 collective-permute-start.8
  80.9 5.4 %collide.11 = (bf16[1024,128]{1,0:T(8,128)(2,1)S(1)}, bf16[1024,128]{1,0:T(8,128)(2,1)S(1)}, f32[8,128]{1,0:T(8,128)S(1)}) custom-call(s32[1]{0:T(128)} %bitcast.3.chips_ref, s32[1]{0:T(128)} %bitcast.4.core_ref, bf16[3456,128]{1,0:T(8,128)(2,1)} %collective-permute-done.3.refs_0_, bf16[3456,128]{1,0:T(8,128)(2,1)S(1)} %collective-permute-done.6.refs_1_, ...), custom_call_target="tpu_custom_call" | custom-call | flops 1024 | bytes 1024 | tf_op jit(solution)/shard_map/collide/pallas_call | solution.py:312
  86.3 0.7 collective-permute-start.11
  86.9 2.3 %collective-permute-start.12 = (bf16[1024,128]{1,0:T(8,128)(2,1)S(1)}, bf16[1024,128]{1,0:T(8,128)(2,1)S(1)}, u32[]{:S(2)}, u32[]{:S(2)}) collective-permute-start(bf16[1024,128]{1,0:T(8,128)(2,1)S(1)} %get-tuple-element.61.refs_1_), channel_id=1, source_target_pairs={{1,0},{2,1},{3,2},{0,3},{5,4},{6,5},{7,6},{4,7},{9,8},{10,9},{11,1... | collective-permute-start | bytes 786440 | tf_op jit(solution)/shard_map/ppermute | solution.py:571
  89.4 1.7 collective-permute-done.8.refs_3_
  91.1 2.0 %stream.4 = (bf16[768,128]{1,0:T(8,128)(2,1)S(1)}, bf16[768,128]{1,0:T(8,128)(2,1)S(1)}, f32[8,128]{1,0:T(8,128)S(1)}) custom-call(f32[8,128]{1,0:T(8,128)S(1)} %get-tuple-element.53._, f32[14,3,128]{2,1,0:T(4,128)S(1)} %copy-done.2, f32[14,1,128]{2,1,0:T(1,128)S(1)} %bitcast_convert_fusion.inflow_ref, s32[256,1]{1,0:T(8,128)S(1)} %copy.10.code_ref, ...), custom_call_target="tpu_custom_call" | custom-call | flops 1024 | bytes 1024 | tf_op jit(solution)/shard_map/stream/pallas_call | solution.py:423
  93.1 1.7 collective-permute-start.10
  94.8 2.2 %collective-permute-start.9 = (bf16[768,128]{1,0:T(8,128)(2,1)S(1)}, bf16[768,128]{1,0:T(8,128)(2,1)S(1)}, u32[]{:S(2)}, u32[]{:S(2)}) collective-permute-start(bf16[768,128]{1,0:T(8,128)(2,1)S(1)} %get-tuple-element.56.refs_0_), channel_id=1, source_target_pairs={{0,24},{4,28},{24,0},{28,4},{8,16},{12,20},{16,8},{20,12},{1,25},{... | collective-permute-start | bytes 589832 | tf_op jit(solution)/shard_map/ppermute | solution.py:442
  97.0 4.5 %collective-permute-done.12.refs_3_ = bf16[1024,128]{1,0:T(8,128)(2,1)S(1)} collective-permute-done((bf16[1024,128]{1,0:T(8,128)(2,1)S(1)}, bf16[1024,128]{1,0:T(8,128)(2,1)S(1)}, u32[]{:S(2)}, u32[]{:S(2)}) %collective-permute-start.12) | collective-permute-done | bytes 262176 | tf_op jit(solution)/shard_map/ppermute | solution.py:571
  101.5 1.6 stream.5
  103.1 1.6 collective-permute-start.13
  104.7 1.0 collective-permute-start.16
  106.3 0.9 collective-permute-done.17.refs_3_
  107.1 17.2 %collective-permute-start.14 = (bf16[768,128]{1,0:T(8,128)(2,1)S(1)}, bf16[768,128]{1,0:T(8,128)(2,1)S(1)}, u32[]{:S(2)}, u32[]{:S(2)}) collective-permute-start(bf16[768,128]{1,0:T(8,128)(2,1)S(1)} %get-tuple-element.56.refs_0_), channel_id=1, source_target_pairs={{0,8},{4,12},{8,0},{12,4},{16,24},{20,28},{24,16},{28,20},{1,9},{5... | collective-permute-start | bytes 589832 | tf_op jit(solution)/shard_map/ppermute | solution.py:442
  124.4 1.3 collective-permute-start.15
  125.8 7.8 %collide.12.refs_13_ = f32[1728,256]{1,0:T(8,128)S(1)} custom-call(s32[1]{0:T(128)} %bitcast.8.chips_ref, s32[1]{0:T(128)} %bitcast.4.core_ref, bf16[768,128]{1,0:T(8,128)(2,1)S(1)} %get-tuple-element.56.refs_0_, bf16[768,128]{1,0:T(8,128)(2,1)S(1)} %get-tuple-element.57.refs_1_, bf16[1920,128]{1,0:T(8,128)(2,1)S(1)} %get-tuple-element.63.refs_2_, ...), custom_call_target="tpu_custom_call" | custom-call | flops 1024 | bytes 1024 | tf_op jit(solution)/shard_map/collide/pallas_call | solution.py:312
  133.6 3.4 %collective-permute-done.15.refs_1_ = bf16[768,128]{1,0:T(8,128)(2,1)S(1)} collective-permute-done((bf16[768,128]{1,0:T(8,128)(2,1)S(1)}, bf16[768,128]{1,0:T(8,128)(2,1)S(1)}, u32[]{:S(2)}, u32[]{:S(2)}) %collective-permute-start.15) | collective-permute-done | bytes 196640 | tf_op jit(solution)/shard_map/ppermute | solution.py:442
  137.3 1.3 collective-permute-start.20
  139.7 1.8 collective-permute-done.24.refs_9_
  142.0 0.9 collective-permute-done.21.refs_3_
  143.2 13.8 %collide.13.refs_3_ = f32[1728,256]{1,0:T(8,128)S(1)} custom-call(s32[2]{0:T(128)S(1)} %pad_add_fusion.chips_ref, s32[1]{0:T(128)} %bitcast.4.core_ref, bf16[768,128]{1,0:T(8,128)(2,1)S(1)} %collective-permute-done.14.refs_0_, bf16[768,128]{1,0:T(8,128)(2,1)S(1)} %collective-permute-done.15.refs_1_, bf16[1920,128]{1,0:T(8,128)(2,1)S(1)} %collective-permute-done.16.refs_2_, ...), custom_call_target="tpu_custom_call" | custom-call | flops 1024 | bytes 1024 | tf_op jit(solution)/shard_map/collide/pallas_call | solution.py:312
  157.0 1.6 collective-permute-done.20.refs_0_
  158.7 2.4 %collective-permute-done.27.refs_1_ = bf16[3456,128]{1,0:T(8,128)(2,1)S(1)} collective-permute-done((bf16[3456,128]{1,0:T(8,128)(2,1)S(1)}, bf16[3456,128]{1,0:T(8,128)(2,1)S(1)}, u32[]{:S(2)}, u32[]{:S(2)}) %collective-permute-start.27) | collective-permute-done | bytes 884768 | tf_op jit(solution)/shard_map/ppermute | solution.py:446
  161.1 5.6 %collide.14 = (bf16[1024,128]{1,0:T(8,128)(2,1)S(1)}, bf16[1024,128]{1,0:T(8,128)(2,1)S(1)}, f32[8,128]{1,0:T(8,128)S(1)}) custom-call(s32[1]{0:T(128)} %bitcast.3.chips_ref, s32[1]{0:T(128)} %bitcast.4.core_ref, bf16[3456,128]{1,0:T(8,128)(2,1)S(1)} %collective-permute-done.20.refs_0_, bf16[3456,128]{1,0:T(8,128)(2,1)S(1)} %collective-permute-done.27.refs_1_, ...), custom_call_target="tpu_custom_call" | custom-call | flops 1024 | bytes 1024 | tf_op jit(solution)/shard_map/collide/pallas_call | solution.py:312
  166.7 1.5 collective-permute-start.30
  168.2 1.5 collective-permute-start.31
  169.7 4.9 %collide.15 = (bf16[768,128]{1,0:T(8,128)(2,1)S(1)}, bf16[768,128]{1,0:T(8,128)(2,1)S(1)}, f32[8,128]{1,0:T(8,128)}) custom-call(s32[1]{0:T(128)} %bitcast.3.chips_ref, s32[1]{0:T(128)} %bitcast.4.core_ref, bf16[3456,128]{1,0:T(8,128)(2,1)S(1)} %collective-permute-done.20.refs_0_, bf16[3456,128]{1,0:T(8,128)(2,1)S(1)} %collective-permute-done.27.refs_1_, ...), custom_call_target="tpu_custom_call" | custom-call | flops 1024 | bytes 1024 | tf_op jit(solution)/shard_map/collide/pallas_call | solution.py:312
  174.7 1.3 totals.1
  176.0 0.7 collective-permute-done.30.refs_0_
  177.0 0.6 collective-permute-start.32
  177.8 2.4 %collective-permute-start.33 = (f32[1,8,16]{2,1,0:T(8,128)S(1)}, f32[1,8,16]{2,1,0:T(8,128)S(1)}, u32[]{:S(2)}, u32[]{:S(2)}) collective-permute-start(f32[1,8,16]{2,1,0:T(8,128)S(1)} %reshape.32), channel_id=1, source_target_pairs={{1,0},{2,1},{3,2},{0,3},{5,4},{6,5},{7,6},{4,7},{9,8},{10,9},{11,1... | collective-permute-start | bytes 1544 | tf_op jit(solution)/shard_map/ppermute | solution.py:535
  180.2 2.9 %collective-permute-start.29 = (bf16[768,128]{1,0:T(8,128)(2,1)S(1)}, bf16[768,128]{1,0:T(8,128)(2,1)S(1)}, u32[]{:S(2)}, u32[]{:S(2)}) collective-permute-start(bf16[768,128]{1,0:T(8,128)(2,1)S(1)} %get-tuple-element.75.refs_2_.refs_1_), channel_id=1, source_target_pairs={{1,0},{2,1},{3,2},{0,3},{5,4},{6,5},{7,6},{4,7},{9,8},{10,9},{11,1... | collective-permute-start | bytes 589832 | tf_op jit(solution)/shard_map/ppermute | solution.py:571
  183.5 1.1 stream.6.refs_4_
  184.6 1.5 collective-permute-start.35
  186.2 1.7 collective-permute-start.36
  187.9 1.2 collective-permute-start.37
  189.5 1.8 stream.7
  191.3 2.0 %collective-permute-done.37 = f32[2,8,16]{2,1,0:T(8,128)S(1)} collective-permute-done((f32[2,8,16]{2,1,0:T(8,128)S(1)}, f32[2,8,16]{2,1,0:T(8,128)S(1)}, u32[]{:S(2)}, u32[]{:S(2)}) %collective-permute-start.37) | collective-permute-done | bytes 1056 | tf_op jit(solution)/shard_map/ppermute | solution.py:442
  193.3 0.6 add_multiply_fusion
  (77 shorter events, 5.6 us)
Async XLA Ops:
  0.6 1.2 copy-start.3
  1.8 5.4 %copy-start.8 = (s32[1728]{0:T(1024)S(1)}, s32[1728]{0:T(1024)}, u32[]{:S(2)}) copy-start(s32[1728]{0:T(1024)} %param.8) | copy-start | bytes 20740
  2.0 11.2 %collective-permute-start.2 = (bf16[3456,128]{1,0:T(8,128)(2,1)S(1)}, bf16[3456,128]{1,0:T(8,128)(2,1)S(1)}, u32[]{:S(2)}, u32[]{:S(2)}) collective-permute-start(bf16[3456,128]{1,0:T(8,128)(2,1)S(1)} %pack.1.refs_0_), channel_id=1, source_target_pairs={{0,4},{4,0},{8,12},{12,8},{16,20},{20,16},{24,28},{28,24},{1,5},{5... | collective-permute-start | bytes 2654216 | tf_op jit(solution)/shard_map/ppermute | solution.py:446
  2.5 25.3 %collective-permute-start = (bf16[3456,128]{1,0:T(8,128)(2,1)S(1)}, bf16[3456,128]{1,0:T(8,128)(2,1)S(1)}, u32[]{:S(2)}, u32[]{:S(2)}) collective-permute-start(bf16[3456,128]{1,0:T(8,128)(2,1)S(1)} %pack.1.refs_0_), channel_id=1, source_target_pairs={{0,24},{4,28},{24,0},{28,4},{8,16},{12,20},{16,8},{20,12},{1,25},{... | collective-permute-start | bytes 2654216 | tf_op jit(solution)/shard_map/ppermute | solution.py:442
  7.2 39.3 %collective-permute-start.1 = (bf16[3456,128]{1,0:T(8,128)(2,1)S(1)}, bf16[3456,128]{1,0:T(8,128)(2,1)S(1)}, u32[]{:S(2)}, u32[]{:S(2)}) collective-permute-start(bf16[3456,128]{1,0:T(8,128)(2,1)S(1)} %pack.1.refs_0_), channel_id=1, source_target_pairs={{0,8},{4,12},{8,0},{12,4},{16,24},{20,28},{24,16},{28,20},{1,9},{5... | collective-permute-start | bytes 2654216 | tf_op jit(solution)/shard_map/ppermute | solution.py:442
  19.6 1.2 copy-start
  46.5 3.3 %copy-start.4 = (bf16[3456,128]{1,0:T(8,128)(2,1)}, bf16[3456,128]{1,0:T(8,128)(2,1)S(1)}, u32[]{:S(2)}) copy-start(bf16[3456,128]{1,0:T(8,128)(2,1)S(1)} %collective-permute-done.1.refs_0_) | copy-start | bytes 2654212
  46.5 3.3 %collective-permute-start.4 = (bf16[3456,128]{1,0:T(8,128)(2,1)S(1)}, bf16[3456,128]{1,0:T(8,128)(2,1)S(1)}, u32[]{:S(2)}, u32[]{:S(2)}) collective-permute-start(bf16[3456,128]{1,0:T(8,128)(2,1)S(1)} %collective-permute-done.1.refs_0_), channel_id=1, source_target_pairs={{0,4},{4,0},{8,12},{12,8},{16,20},{20,16},{24,28},{28,24},{1,5},{5... | collective-permute-start | bytes 2654216 | tf_op jit(solution)/shard_map/ppermute | solution.py:446
  46.5 4.2 %collective-permute-start.5 = (bf16[3456,128]{1,0:T(8,128)(2,1)S(1)}, bf16[3456,128]{1,0:T(8,128)(2,1)}, u32[]{:S(2)}, u32[]{:S(2)}) collective-permute-start(bf16[3456,128]{1,0:T(8,128)(2,1)S(1)} %collective-permute-done.refs_2_), channel_id=1, source_target_pairs={{0,4},{4,0},{8,12},{12,8},{16,20},{20,16},{24,28},{28,24},{1,5},{5... | collective-permute-start | bytes 2654216 | tf_op jit(solution)/shard_map/ppermute | solution.py:446
  48.0 21.9 %collective-permute-start.3 = (bf16[3456,128]{1,0:T(8,128)(2,1)}, bf16[3456,128]{1,0:T(8,128)(2,1)}, u32[]{:S(2)}, u32[]{:S(2)}) collective-permute-start(bf16[3456,128]{1,0:T(8,128)(2,1)} %broadcast_select_fusion), channel_id=1, source_target_pairs={{0,16},{4,20},{24,8},{28,12},{16,24},{20,28},{8,0},{12,4},{1,17},{... | collective-permute-start | bytes 2654216 | tf_op jit(solution)/shard_map/ppermute | solution.py:442
  49.8 0.9 copy-start.6
  50.7 1.5 copy-start.1
  52.2 1.2 copy-start.5
  53.4 1.2 copy-start.7
  69.9 2.6 %collective-permute-start.6 = (bf16[3456,128]{1,0:T(8,128)(2,1)}, bf16[3456,128]{1,0:T(8,128)(2,1)S(1)}, u32[]{:S(2)}, u32[]{:S(2)}) collective-permute-start(bf16[3456,128]{1,0:T(8,128)(2,1)} %collective-permute-done.3.refs_0_), channel_id=1, source_target_pairs={{0,4},{4,0},{8,12},{12,8},{16,20},{20,16},{24,28},{28,24},{1,5},{5... | collective-permute-start | bytes 2654216 | tf_op jit(solution)/shard_map/ppermute | solution.py:446
  77.9 11.5 %collective-permute-start.7 = (bf16[768,128]{1,0:T(8,128)(2,1)}, bf16[768,128]{1,0:T(8,128)(2,1)}, u32[]{:S(2)}, u32[]{:S(2)}) collective-permute-start(bf16[768,128]{1,0:T(8,128)(2,1)} %get-tuple-element.54.refs_2_), channel_id=1, source_target_pairs={{0,1},{1,2},{2,3},{3,0},{4,5},{5,6},{6,7},{7,4},{8,9},{9,10},{10,1... | collective-permute-start | bytes 589832 | tf_op jit(solution)/shard_map/ppermute | solution.py:570
  79.4 11.7 %collective-permute-start.8 = (bf16[768,128]{1,0:T(8,128)(2,1)}, bf16[768,128]{1,0:T(8,128)(2,1)}, u32[]{:S(2)}, u32[]{:S(2)}) collective-permute-start(bf16[768,128]{1,0:T(8,128)(2,1)} %get-tuple-element.55.refs_1_), channel_id=1, source_target_pairs={{1,0},{2,1},{3,2},{0,3},{5,4},{6,5},{7,6},{4,7},{9,8},{10,9},{11,1... | collective-permute-start | bytes 589832 | tf_op jit(solution)/shard_map/ppermute | solution.py:571
  80.9 8.4 %copy-start.9 = (s32[256,1]{0,1:T(1,128)S(1)}, s32[256,1]{0,1:T(1,128)}, u32[]{:S(2)}) copy-start(s32[256,1]{0,1:T(1,128)} %reshape.28) | copy-start | bytes 3076
  80.9 10.2 %copy-start.2 = (f32[14,3,128]{2,1,0:T(4,128)S(1)}, f32[14,3,128]{2,1,0:T(4,128)}, u32[]{:S(2)}) copy-start(f32[14,3,128]{2,1,0:T(4,128)} %fusion.speed_ref) | copy-start | bytes 64516
  86.3 10.8 %collective-permute-start.11 = (bf16[1024,128]{1,0:T(8,128)(2,1)S(1)}, bf16[1024,128]{1,0:T(8,128)(2,1)S(1)}, u32[]{:S(2)}, u32[]{:S(2)}) collective-permute-start(bf16[1024,128]{1,0:T(8,128)(2,1)S(1)} %get-tuple-element.60.refs_2_), channel_id=1, source_target_pairs={{0,1},{1,2},{2,3},{3,0},{4,5},{5,6},{6,7},{7,4},{8,9},{9,10},{10,1... | collective-permute-start | bytes 786440 | tf_op jit(solution)/shard_map/ppermute | solution.py:570
  86.9 14.6 %collective-permute-start.12 = (bf16[1024,128]{1,0:T(8,128)(2,1)S(1)}, bf16[1024,128]{1,0:T(8,128)(2,1)S(1)}, u32[]{:S(2)}, u32[]{:S(2)}) collective-permute-start(bf16[1024,128]{1,0:T(8,128)(2,1)S(1)} %get-tuple-element.61.refs_1_), channel_id=1, source_target_pairs={{1,0},{2,1},{3,2},{0,3},{5,4},{6,5},{7,6},{4,7},{9,8},{10,9},{11,1... | collective-permute-start | bytes 786440 | tf_op jit(solution)/shard_map/ppermute | solution.py:571
  93.1 12.6 %collective-permute-start.10 = (bf16[768,128]{1,0:T(8,128)(2,1)S(1)}, bf16[768,128]{1,0:T(8,128)(2,1)S(1)}, u32[]{:S(2)}, u32[]{:S(2)}) collective-permute-start(bf16[768,128]{1,0:T(8,128)(2,1)S(1)} %get-tuple-element.57.refs_1_), channel_id=1, source_target_pairs={{0,24},{4,28},{24,0},{28,4},{8,16},{12,20},{16,8},{20,12},{1,25},{... | collective-permute-start | bytes 589832 | tf_op jit(solution)/shard_map/ppermute | solution.py:442
  94.8 11.1 %collective-permute-start.9 = (bf16[768,128]{1,0:T(8,128)(2,1)S(1)}, bf16[768,128]{1,0:T(8,128)(2,1)S(1)}, u32[]{:S(2)}, u32[]{:S(2)}) collective-permute-start(bf16[768,128]{1,0:T(8,128)(2,1)S(1)} %get-tuple-element.56.refs_0_), channel_id=1, source_target_pairs={{0,24},{4,28},{24,0},{28,4},{8,16},{12,20},{16,8},{20,12},{1,25},{... | collective-permute-start | bytes 589832 | tf_op jit(solution)/shard_map/ppermute | solution.py:442
  103.1 22.6 %collective-permute-start.19 = (bf16[1920,128]{1,0:T(8,128)(2,1)S(1)}, bf16[1920,128]{1,0:T(8,128)(2,1)S(1)}, u32[]{:S(2)}, u32[]{:S(2)}) collective-permute-start(bf16[1920,128]{1,0:T(8,128)(2,1)S(1)} %get-tuple-element.63.refs_2_), channel_id=1, source_target_pairs={{0,4},{4,0},{8,12},{12,8},{16,20},{20,16},{24,28},{28,24},{1,5},{5... | collective-permute-start | bytes 1474568 | tf_op jit(solution)/shard_map/ppermute | solution.py:446
  103.1 33.9 %collective-permute-start.13 = (bf16[1920,128]{1,0:T(8,128)(2,1)S(1)}, bf16[1920,128]{1,0:T(8,128)(2,1)S(1)}, u32[]{:S(2)}, u32[]{:S(2)}) collective-permute-start(bf16[1920,128]{1,0:T(8,128)(2,1)S(1)} %get-tuple-element.63.refs_2_), channel_id=1, source_target_pairs={{0,24},{4,28},{24,0},{28,4},{8,16},{12,20},{16,8},{20,12},{1,25},{... | collective-permute-start | bytes 1474568 | tf_op jit(solution)/shard_map/ppermute | solution.py:442
  104.7 32.3 %collective-permute-start.16 = (bf16[1920,128]{1,0:T(8,128)(2,1)S(1)}, bf16[1920,128]{1,0:T(8,128)(2,1)S(1)}, u32[]{:S(2)}, u32[]{:S(2)}) collective-permute-start(bf16[1920,128]{1,0:T(8,128)(2,1)S(1)} %get-tuple-element.63.refs_2_), channel_id=1, source_target_pairs={{0,8},{4,12},{8,0},{12,4},{16,24},{20,28},{24,16},{28,20},{1,9},{5... | collective-permute-start | bytes 1474568 | tf_op jit(solution)/shard_map/ppermute | solution.py:442
  105.7 1.4 collective-permute-start.17
  105.9 18.5 %collective-permute-start.18 = (bf16[768,128]{1,0:T(8,128)(2,1)S(1)}, bf16[768,128]{1,0:T(8,128)(2,1)S(1)}, u32[]{:S(2)}, u32[]{:S(2)}) collective-permute-start(bf16[768,128]{1,0:T(8,128)(2,1)S(1)} %get-tuple-element.57.refs_1_), channel_id=1, source_target_pairs={{0,4},{4,0},{8,12},{12,8},{16,20},{20,16},{24,28},{28,24},{1,5},{5... | collective-permute-start | bytes 589832 | tf_op jit(solution)/shard_map/ppermute | solution.py:446
  107.1 26.5 %collective-permute-start.14 = (bf16[768,128]{1,0:T(8,128)(2,1)S(1)}, bf16[768,128]{1,0:T(8,128)(2,1)S(1)}, u32[]{:S(2)}, u32[]{:S(2)}) collective-permute-start(bf16[768,128]{1,0:T(8,128)(2,1)S(1)} %get-tuple-element.56.refs_0_), channel_id=1, source_target_pairs={{0,8},{4,12},{8,0},{12,4},{16,24},{20,28},{24,16},{28,20},{1,9},{5... | collective-permute-start | bytes 589832 | tf_op jit(solution)/shard_map/ppermute | solution.py:442
  124.4 12.7 %collective-permute-start.15 = (bf16[768,128]{1,0:T(8,128)(2,1)S(1)}, bf16[768,128]{1,0:T(8,128)(2,1)S(1)}, u32[]{:S(2)}, u32[]{:S(2)}) collective-permute-start(bf16[768,128]{1,0:T(8,128)(2,1)S(1)} %get-tuple-element.57.refs_1_), channel_id=1, source_target_pairs={{0,8},{4,12},{8,0},{12,4},{16,24},{20,28},{24,16},{28,20},{1,9},{5... | collective-permute-start | bytes 589832 | tf_op jit(solution)/shard_map/ppermute | solution.py:442
  137.3 21.3 %collective-permute-start.20 = (bf16[3456,128]{1,0:T(8,128)(2,1)S(1)}, bf16[3456,128]{1,0:T(8,128)(2,1)S(1)}, u32[]{:S(2)}, u32[]{:S(2)}) collective-permute-start(bf16[3456,128]{1,0:T(8,128)(2,1)S(1)} %maximum_select_fusion), channel_id=1, source_target_pairs={{0,16},{4,20},{24,8},{28,12},{16,24},{20,28},{8,0},{12,4},{1,17},{... | collective-permute-start | bytes 2654216 | tf_op jit(solution)/shard_map/ppermute | solution.py:442
  138.7 4.6 %collective-permute-start.23 = (bf16[1920,128]{1,0:T(8,128)(2,1)S(1)}, bf16[1920,128]{1,0:T(8,128)(2,1)S(1)}, u32[]{:S(2)}, u32[]{:S(2)}) collective-permute-start(bf16[1920,128]{1,0:T(8,128)(2,1)S(1)} %collective-permute-done.16.refs_2_), channel_id=1, source_target_pairs={{0,4},{4,0},{8,12},{12,8},{16,20},{20,16},{24,28},{28,24},{1,5},{5... | collective-permute-start | bytes 1474568 | tf_op jit(solution)/shard_map/ppermute | solution.py:446
  138.7 4.6 %collective-permute-start.26 = (bf16[1920,128]{1,0:T(8,128)(2,1)S(1)}, bf16[1920,128]{1,0:T(8,128)(2,1)S(1)}, u32[]{:S(2)}, u32[]{:S(2)}) collective-permute-start(bf16[1920,128]{1,0:T(8,128)(2,1)S(1)} %collective-permute-done.13.refs_8_), channel_id=1, source_target_pairs={{0,4},{4,0},{8,12},{12,8},{16,20},{20,16},{24,28},{28,24},{1,5},{5... | collective-permute-start | bytes 1474568 | tf_op jit(solution)/shard_map/ppermute | solution.py:446
  139.2 2.3 %collective-permute-start.24 = (bf16[768,128]{1,0:T(8,128)(2,1)S(1)}, bf16[768,128]{1,0:T(8,128)(2,1)S(1)}, u32[]{:S(2)}, u32[]{:S(2)}) collective-permute-start(bf16[768,128]{1,0:T(8,128)(2,1)S(1)} %collective-permute-done.9.refs_6_), channel_id=1, source_target_pairs={{0,4},{4,0},{8,12},{12,8},{16,20},{20,16},{24,28},{28,24},{1,5},{5... | collective-permute-start | bytes 589832 | tf_op jit(solution)/shard_map/ppermute | solution.py:446
  139.2 2.6 %collective-permute-start.25 = (bf16[768,128]{1,0:T(8,128)(2,1)S(1)}, bf16[768,128]{1,0:T(8,128)(2,1)S(1)}, u32[]{:S(2)}, u32[]{:S(2)}) collective-permute-start(bf16[768,128]{1,0:T(8,128)(2,1)S(1)} %collective-permute-done.10.refs_7_), channel_id=1, source_target_pairs={{0,4},{4,0},{8,12},{12,8},{16,20},{20,16},{24,28},{28,24},{1,5},{5... | collective-permute-start | bytes 589832 | tf_op jit(solution)/shard_map/ppermute | solution.py:446
  141.5 1.4 collective-permute-start.21
  141.8 1.4 collective-permute-start.22
  158.7 2.4 %collective-permute-start.27 = (bf16[3456,128]{1,0:T(8,128)(2,1)S(1)}, bf16[3456,128]{1,0:T(8,128)(2,1)S(1)}, u32[]{:S(2)}, u32[]{:S(2)}) collective-permute-start(bf16[3456,128]{1,0:T(8,128)(2,1)S(1)} %collective-permute-done.20.refs_0_), channel_id=1, source_target_pairs={{0,4},{4,0},{8,12},{12,8},{16,20},{20,16},{24,28},{28,24},{1,5},{5... | collective-permute-start | bytes 2654216 | tf_op jit(solution)/shard_map/ppermute | solution.py:446
  166.7 10.1 %collective-permute-start.30 = (bf16[1024,128]{1,0:T(8,128)(2,1)S(1)}, bf16[1024,128]{1,0:T(8,128)(2,1)S(1)}, u32[]{:S(2)}, u32[]{:S(2)}) collective-permute-start(bf16[1024,128]{1,0:T(8,128)(2,1)S(1)} %get-tuple-element.73.refs_1_.refs_2_), channel_id=1, source_target_pairs={{0,1},{1,2},{2,3},{3,0},{4,5},{5,6},{6,7},{7,4},{8,9},{9,10},{10,1... | collective-permute-start | bytes 786440 | tf_op jit(solution)/shard_map/ppermute | solution.py:570
  168.2 15.2 %collective-permute-start.31 = (bf16[1024,128]{1,0:T(8,128)(2,1)S(1)}, bf16[1024,128]{1,0:T(8,128)(2,1)S(1)}, u32[]{:S(2)}, u32[]{:S(2)}) collective-permute-start(bf16[1024,128]{1,0:T(8,128)(2,1)S(1)} %get-tuple-element.72.refs_0_.refs_1_), channel_id=1, source_target_pairs={{1,0},{2,1},{3,2},{0,3},{5,4},{6,5},{7,6},{4,7},{9,8},{10,9},{11,1... | collective-permute-start | bytes 786440 | tf_op jit(solution)/shard_map/ppermute | solution.py:571
  177.0 6.4 %collective-permute-start.32 = (f32[1,8,16]{2,1,0:T(8,128)S(1)}, f32[1,8,16]{2,1,0:T(8,128)S(1)}, u32[]{:S(2)}, u32[]{:S(2)}) collective-permute-start(f32[1,8,16]{2,1,0:T(8,128)S(1)} %reshape.31), channel_id=1, source_target_pairs={{0,1},{1,2},{2,3},{3,0},{4,5},{5,6},{6,7},{7,4},{8,9},{9,10},{10,1... | collective-permute-start | bytes 1544 | tf_op jit(solution)/shard_map/ppermute | solution.py:534
  177.8 5.6 %collective-permute-start.33 = (f32[1,8,16]{2,1,0:T(8,128)S(1)}, f32[1,8,16]{2,1,0:T(8,128)S(1)}, u32[]{:S(2)}, u32[]{:S(2)}) collective-permute-start(f32[1,8,16]{2,1,0:T(8,128)S(1)} %reshape.32), channel_id=1, source_target_pairs={{1,0},{2,1},{3,2},{0,3},{5,4},{6,5},{7,6},{4,7},{9,8},{10,9},{11,1... | collective-permute-start | bytes 1544 | tf_op jit(solution)/shard_map/ppermute | solution.py:535
  180.2 8.8 %collective-permute-start.28 = (bf16[768,128]{1,0:T(8,128)(2,1)S(1)}, bf16[768,128]{1,0:T(8,128)(2,1)S(1)}, u32[]{:S(2)}, u32[]{:S(2)}) collective-permute-start(bf16[768,128]{1,0:T(8,128)(2,1)S(1)} %get-tuple-element.76.refs_3_.refs_2_), channel_id=1, source_target_pairs={{0,1},{1,2},{2,3},{3,0},{4,5},{5,6},{6,7},{7,4},{8,9},{9,10},{10,1... | collective-permute-start | bytes 589832 | tf_op jit(solution)/shard_map/ppermute | solution.py:570
  180.2 9.3 %collective-permute-start.29 = (bf16[768,128]{1,0:T(8,128)(2,1)S(1)}, bf16[768,128]{1,0:T(8,128)(2,1)S(1)}, u32[]{:S(2)}, u32[]{:S(2)}) collective-permute-start(bf16[768,128]{1,0:T(8,128)(2,1)S(1)} %get-tuple-element.75.refs_2_.refs_1_), channel_id=1, source_target_pairs={{1,0},{2,1},{3,2},{0,3},{5,4},{6,5},{7,6},{4,7},{9,8},{10,9},{11,1... | collective-permute-start | bytes 589832 | tf_op jit(solution)/shard_map/ppermute | solution.py:571
  183.4 1.2 collective-permute-start.34
  184.6 6.7 %collective-permute-start.35 = (f32[2,8,16]{2,1,0:T(8,128)S(1)}, f32[2,8,16]{2,1,0:T(8,128)S(1)}, u32[]{:S(2)}, u32[]{:S(2)}) collective-permute-start(f32[2,8,16]{2,1,0:T(8,128)S(1)} %add.51), channel_id=1, source_target_pairs={{0,8},{4,12},{8,0},{12,4},{16,24},{20,28},{24,16},{28,20},{1,9},{5... | collective-permute-start | bytes 3080 | tf_op jit(solution)/shard_map/ppermute | solution.py:442
  186.2 5.2 %collective-permute-start.36 = (f32[2,8,16]{2,1,0:T(8,128)S(1)}, f32[2,8,16]{2,1,0:T(8,128)S(1)}, u32[]{:S(2)}, u32[]{:S(2)}) collective-permute-start(f32[2,8,16]{2,1,0:T(8,128)S(1)} %add.51), channel_id=1, source_target_pairs={{0,16},{4,20},{16,0},{20,4},{8,24},{12,28},{24,8},{28,12},{1,17},{... | collective-permute-start | bytes 3080 | tf_op jit(solution)/shard_map/ppermute | solution.py:442
  187.9 5.4 %collective-permute-start.37 = (f32[2,8,16]{2,1,0:T(8,128)S(1)}, f32[2,8,16]{2,1,0:T(8,128)S(1)}, u32[]{:S(2)}, u32[]{:S(2)}) collective-permute-start(f32[2,8,16]{2,1,0:T(8,128)S(1)} %add.51), channel_id=1, source_target_pairs={{0,24},{4,28},{24,0},{28,4},{8,16},{12,20},{16,8},{20,12},{1,25},{... | collective-permute-start | bytes 3080 | tf_op jit(solution)/shard_map/ppermute | solution.py:442

commit v4 on v3

--- a/solution.py
+++ b/solution.py
@@ -174,7 +174,7 @@
     count, pieces, cells, local, part, planes, has_acc, has_token, buffers, chips_ref, core_ref, *refs
 ):
     refs = list(refs)
-    given = [[refs.pop(0) for _ in range(pieces)] for _ in range(2 * count)]
+    given = [[refs.pop(0) for _ in range(n)] for n in pieces]
     collision_ref = refs.pop(0)
     acc_ref = refs.pop(0) if has_acc else None
     state_ref = refs.pop(0) if part else None
@@ -202,12 +202,14 @@
             sems.at[n % buffers],
         )
 
+    most = max(pieces)
+
     def load(sources, target, number):
         copies, start = [], 0
         for i, source in enumerate(sources):
             here = pl.ds(start, source.shape[0])
             copies.append(
-                pltpu.make_async_copy(source, target.at[here], load_sems.at[number * pieces + i])
+                pltpu.make_async_copy(source, target.at[here], load_sems.at[number * most + i])
             )
             start += source.shape[0]
         for one in copies:
@@ -296,7 +298,7 @@
         height = min(part[1] * LANES, local) - part[0] * LANES
     rows = row_block(height)
     buffers = BUFFERS
-    count, pieces = len(pairs), len(pairs[0][0])
+    count, pieces = len(pairs), tuple(len(block) for pair in pairs for block in pair)
     padded = -(-cells // LANES) * LANES
     given = [a for pair in pairs for block in pair for a in block]
     operands = given + [collision] + [a for a in (acc, state, token) if a is not None]
@@ -330,7 +332,7 @@
             pltpu.SemaphoreType.DMA((buffers,)),
             pltpu.VMEM((count, padded, 2 * local), jnp.bfloat16),
             pltpu.VMEM((height, padded) if part else small, jnp.float32),
-            pltpu.SemaphoreType.DMA(((2 * count + 2) * pieces,)),
+            pltpu.SemaphoreType.DMA(((2 * count + 2) * max(pieces),)),
             pltpu.VMEM(state.shape if part else small, jnp.bfloat16),
         ]
         + [pltpu.VMEM(block, jnp.bfloat16)] * (2 * count),
@@ -354,9 +356,13 @@
     half = cells // 2
 
     def tile(t, tail, out_ref, begin):
+        @functools.lru_cache
+        def cell(x, y):
+            at = t * size + y * depth
+            return plane_refs[x + 1][rows_at(at, depth), :].astype(jnp.float32)
+
         def plane(x, y):
-            at = t * size + y % height * depth
-            return plane_refs[x + 1][rows_at(at, depth), :].astype(jnp.float32)
+            return cell(x, y % height)
 
         speed = [speed_ref[first + t, d : d + 1, :] for d in range(3)]
         fast = [jnp.abs(s) for s in speed]
@@ -407,6 +413,11 @@
         lax.fori_loop(begin - first, min(stop, full) - first, body, 0)
         if stop > full:
             tile(full - first, True, out_ref, begin)
+    if not final and len(blocks) > 1:
+        at = 0
+        for ref in out_refs:
+            refs[1][at : at + ref.shape[0], :] = ref[...]
+            at += ref.shape[0]
 
 
 def stream(part, planes, speed, inflow, code, shape, final, done, token):
@@ -420,6 +431,9 @@
             jax.ShapeDtypeStruct((packed_rows(*span, cells, local), LANES), jnp.bfloat16)
             for span in blocks_of(part, local)
         ] + [jax.ShapeDtypeStruct((8, LANES), jnp.float32)]
+        if len(out_shape) > 2:
+            rows = packed_rows(*part, cells, local)
+            out_shape.append(jax.ShapeDtypeStruct((rows, LANES), jnp.bfloat16))
     return pl.pallas_call(
         functools.partial(stream_kernel, part, shape, final),
         out_shape=out_shape,
@@ -575,13 +589,13 @@
         return blocks, [other_core(block) for block in blocks]
 
     start, speed, inflow, code = tied(chip, speed, inflow, code)
-    state = pack(deviation)
+    blocks = state = pack(deviation)
     for step in range(ITERS):
         final = step == ITERS - 1
-        sent = [(along(block, FAR), along(block, NEAR)) for block in state]
-        far, near = [f for f, _ in sent], [n for _, n in sent]
+        far = [along(block, FAR) for block in blocks]
+        near = [along(block, NEAR) for block in state]
         parts = spans(PARTS[step], local)
-        early = len(state) - 1
+        early = len(blocks) - 1
         if early:
             *far[:early], start = tied(*far[:early], start)
         acc = matmul([pair(state)], [start], core, collision, cells)[0]
@@ -602,14 +616,17 @@
             chunks.append(halo(relaxed))
         if final:
             token, *sums = totals(chunks, speed, inflow, code, shape, parts)
-        state, done, firsts = [], (), []
+        blocks, state, done, firsts = [], [], (), []
         for part, chunk in zip(parts, chunks):
-            *blocks, last = stream(part, chunk, speed, inflow, code, shape, final, done, token)
-            state += blocks
-            firsts.append(last)
-            done = (last,)
+            result = list(stream(part, chunk, speed, inflow, code, shape, final, done, token))
+            if not final:
+                mine = [result.pop(0) for _ in blocks_of(part, local)]
+                blocks += mine
+                state.append(result[-1] if len(mine) > 1 else mine[0])
+            firsts.append(result[0])
+            done = (result[0],)
     density = density_of(*sums, code, shape, chunks[0][0], firsts[0])
-    return last.reshape(shape), density
+    return done[0].reshape(shape), density
 
 
 def shards(deviation, collision, *rest):

time: 194 us -> 194 us (level)
  waiting for transfers between devices: 54.3 us -> 56.6 us
    ppermute x13 -> x12, waiting for transfers between devices: 36.8 us -> 39.9 us  [along(): return lax.ppermute(block, 'vel', perm)]
    ppermute x15 -> x13, waiting for transfers between devices: 10.1 us -> 9.24 us  [other_core(): return lax.ppermute(block, 'vel', [(i, i ^ 1) for i in range(8)])]
    ppermute x13 -> x12, starting transfers between devices: 36.1 us -> 35.8 us  [along(): return lax.ppermute(block, 'vel', perm)]
    unnamed x22 -> x21, local copies, waits for them, and re-layouts: 7.21 us -> 7.19 us
  transfers between devices with their start and end apart: 38 -> 35, of which waited for: 18 -> 15; matrix products, arithmetic and copies ran while one was open for 4% -> 4% of each run, Pallas kernels for 30% -> 29%
where the time goes in v4:
time: 194 us
  Pallas kernels  67.3 us (35%)
  waiting for transfers between devices  56.6 us (29%)
  starting transfers between devices  53.2 us (27%)
  local copies, waits for them, and re-layouts  10.9 us (6%)
  other arithmetic  5.04 us (3%)
    pallas_call x8, Pallas kernels, matmul(): pl.pallas_call(functools.partial(matmul_kernel, count, pieces, cells, loc...  59.2 us
    ppermute x12, waiting for transfers between devices, along(): return lax.ppermute(block, 'vel', perm)  39.9 us
    ppermute x12, starting transfers between devices, along(): return lax.ppermute(block, 'vel', perm)  35.8 us
    ppermute x13, waiting for transfers between devices, other_core(): return lax.ppermute(block, 'vel', [(i, i ^ 1) for i in range(8)])  9.24 us
    ppermute x4, starting transfers between devices, halo(): high = lax.ppermute(relaxed[0], 'space', backward)  8.18 us
    unnamed x21, local copies, waits for them, and re-layouts  7.19 us
    pallas_call x4, Pallas kernels, stream(): pl.pallas_call(functools.partial(stream_kernel, part, shape, final), out_...  6.6 us
    ppermute x4, waiting for transfers between devices, halo(): high = lax.ppermute(relaxed[0], 'space', backward)  6.59 us
  transfers between devices with their start and end apart: 35, of which 15 were waited for; matrix products, arithmetic and copies ran while one was open for 4% of the time, Pallas kernels for 29%

profile of v4, /device:TPU:0, one launch (start us, length us, event | category | flops | bytes accessed | tf_op | source)
XLA Modules:
  0.0 193.9 jit_solution(1074036488831740435)
XLA Ops:
  0.6 1.2 copy-done.3
  2.0 0.5 collective-permute-start.2
  2.5 4.7 %collective-permute-start = (bf16[3456,128]{1,0:T(8,128)(2,1)S(1)}, bf16[3456,128]{1,0:T(8,128)(2,1)S(1)}, u32[]{:S(2)}, u32[]{:S(2)}) collective-permute-start(bf16[3456,128]{1,0:T(8,128)(2,1)S(1)} %pack.1.refs_0_), channel_id=1, source_target_pairs={{0,24},{4,28},{24,0},{28,4},{8,16},{12,20},{16,8},{20,12},{1,25},{... | collective-permute-start | bytes 2654216 | tf_op jit(solution)/shard_map/ppermute | solution.py:456
  7.2 0.6 stack.37
  7.8 0.6 stack.38
  8.4 1.3 convert_element_type.20
  9.7 0.7 compare_select_fusion
  10.4 0.6 reshape.28
  11.0 0.7 bitcast_convert_fusion.inflow_ref
  11.7 1.3 fusion.speed_ref
  13.1 6.5 %collide.8.refs_5_ = f32[1728,256]{1,0:T(8,128)S(1)} custom-call(s32[1]{0:T(128)} %bitcast.5.chips_ref, s32[1]{0:T(128)} %bitcast.4.core_ref, bf16[3456,128]{1,0:T(8,128)(2,1)S(1)} %pack.1.refs_0_, bf16[3456,128]{1,0:T(8,128)(2,1)S(1)} %collective-permute-done.2.refs_1_, bf16[1728,13824]{1,0:T(8,128)(2,1)} %refs_2_.9), custom_call_target="tpu_custom_call" | custom-call | flops 1024 | bytes 1024 | tf_op jit(solution)/shard_map/collide/pallas_call | solution.py:314
  19.6 1.2 copy-done
  20.8 7.0 %collective-permute-done.refs_2_ = bf16[3456,128]{1,0:T(8,128)(2,1)S(1)} collective-permute-done((bf16[3456,128]{1,0:T(8,128)(2,1)S(1)}, bf16[3456,128]{1,0:T(8,128)(2,1)S(1)}, u32[]{:S(2)}, u32[]{:S(2)}) %collective-permute-start) | collective-permute-done | bytes 884768 | tf_op jit(solution)/shard_map/ppermute | solution.py:456
  27.8 18.7 %collective-permute-done.1.refs_0_ = bf16[3456,128]{1,0:T(8,128)(2,1)S(1)} collective-permute-done((bf16[3456,128]{1,0:T(8,128)(2,1)S(1)}, bf16[3456,128]{1,0:T(8,128)(2,1)S(1)}, u32[]{:S(2)}, u32[]{:S(2)}) %collective-permute-start.1) | collective-permute-done | bytes 884768 | tf_op jit(solution)/shard_map/ppermute | solution.py:456
  47.0 1.0 broadcast_select_fusion
  48.0 0.6 collective-permute-start.3
  48.7 1.1 collective-permute-done.4.refs_1_
  49.8 0.9 copy-done.6
  50.7 1.5 copy-done.1
  52.2 1.2 copy-done.5
  53.4 1.2 copy-done.7
  54.5 11.2 %collide.9.refs_3_ = f32[1728,256]{1,0:T(8,128)S(1)} custom-call(s32[2]{0:T(128)S(1)} %pad_add_fusion.chips_ref, s32[1]{0:T(128)} %bitcast.4.core_ref, bf16[3456,128]{1,0:T(8,128)(2,1)S(1)} %copy-done.5, bf16[3456,128]{1,0:T(8,128)(2,1)S(1)} %copy-done.7, bf16[3456,128]{1,0:T(8,128)(2,1)S(1)} %collective-permute-done.refs_2_, ...), custom_call_target="tpu_custom_call" | custom-call | flops 1024 | bytes 1024 | tf_op jit(solution)/shard_map/collide/pallas_call | solution.py:314
  65.8 4.1 %collective-permute-done.3.refs_0_ = bf16[3456,128]{1,0:T(8,128)(2,1)} collective-permute-done((bf16[3456,128]{1,0:T(8,128)(2,1)}, bf16[3456,128]{1,0:T(8,128)(2,1)}, u32[]{:S(2)}, u32[]{:S(2)}) %collective-permute-start.3) | collective-permute-done | bytes 884768 | tf_op jit(solution)/shard_map/ppermute | solution.py:456
  69.9 2.6 %collective-permute-done.6.refs_1_ = bf16[3456,128]{1,0:T(8,128)(2,1)S(1)} collective-permute-done((bf16[3456,128]{1,0:T(8,128)(2,1)}, bf16[3456,128]{1,0:T(8,128)(2,1)S(1)}, u32[]{:S(2)}, u32[]{:S(2)}) %collective-permute-start.6) | collective-permute-done | bytes 884768 | tf_op jit(solution)/shard_map/ppermute | solution.py:460
  72.5 5.3 %collide.10 = (bf16[768,128]{1,0:T(8,128)(2,1)}, bf16[768,128]{1,0:T(8,128)(2,1)}, f32[8,128]{1,0:T(8,128)S(1)}) custom-call(s32[1]{0:T(128)} %bitcast.3.chips_ref, s32[1]{0:T(128)} %bitcast.4.core_ref, bf16[3456,128]{1,0:T(8,128)(2,1)} %collective-permute-done.3.refs_0_, bf16[3456,128]{1,0:T(8,128)(2,1)S(1)} %collective-permute-done.6.refs_1_, ...), custom_call_target="tpu_custom_call" | custom-call | flops 1024 | bytes 1024 | tf_op jit(solution)/shard_map/collide/pallas_call | solution.py:314
  77.9 1.5 collective-permute-start.7
  79.4 1.4 collective-permute-start.8
  80.9 5.4 %collide.11 = (bf16[1024,128]{1,0:T(8,128)(2,1)S(1)}, bf16[1024,128]{1,0:T(8,128)(2,1)S(1)}, f32[8,128]{1,0:T(8,128)S(1)}) custom-call(s32[1]{0:T(128)} %bitcast.3.chips_ref, s32[1]{0:T(128)} %bitcast.4.core_ref, bf16[3456,128]{1,0:T(8,128)(2,1)} %collective-permute-done.3.refs_0_, bf16[3456,128]{1,0:T(8,128)(2,1)S(1)} %collective-permute-done.6.refs_1_, ...), custom_call_target="tpu_custom_call" | custom-call | flops 1024 | bytes 1024 | tf_op jit(solution)/shard_map/collide/pallas_call | solution.py:314
  86.3 0.6 collective-permute-start.11
  86.9 2.3 %collective-permute-start.12 = (bf16[1024,128]{1,0:T(8,128)(2,1)S(1)}, bf16[1024,128]{1,0:T(8,128)(2,1)S(1)}, u32[]{:S(2)}, u32[]{:S(2)}) collective-permute-start(bf16[1024,128]{1,0:T(8,128)(2,1)S(1)} %get-tuple-element.61.refs_1_), channel_id=1, source_target_pairs={{1,0},{2,1},{3,2},{0,3},{5,4},{6,5},{7,6},{4,7},{9,8},{10,9},{11,1... | collective-permute-start | bytes 786440 | tf_op jit(solution)/shard_map/ppermute | solution.py:585
  89.4 1.7 collective-permute-done.8.refs_3_
  91.1 2.1 %stream.4 = (bf16[768,128]{1,0:T(8,128)(2,1)S(1)}, bf16[768,128]{1,0:T(8,128)(2,1)S(1)}, f32[8,128]{1,0:T(8,128)S(1)}, bf16[1536,128]{1,0:T(8,128)(2,1)S(1)}) custom-call(f32[8,128]{1,0:T(8,128)S(1)} %get-tuple-element.53._, f32[14,3,128]{2,1,0:T(4,128)S(1)} %copy-done.2, f32[14,1,128]{2,1,0:T(1,128)S(1)} %bitcast_convert_fusion.inflow_ref, ...), custom_call_target="tpu_custom_call" | custom-call | flops 1024 | bytes 1024 | tf_op jit(solution)/shard_map/stream/pallas_call | solution.py:437
  93.1 1.7 collective-permute-start.10
  94.8 2.2 %collective-permute-start.9 = (bf16[768,128]{1,0:T(8,128)(2,1)S(1)}, bf16[768,128]{1,0:T(8,128)(2,1)S(1)}, u32[]{:S(2)}, u32[]{:S(2)}) collective-permute-start(bf16[768,128]{1,0:T(8,128)(2,1)S(1)} %get-tuple-element.56), channel_id=1, source_target_pairs={{0,24},{4,28},{24,0},{28,4},{8,16},{12,20},{16,8},{20,12},{1,25},{... | collective-permute-start | bytes 589832 | tf_op jit(solution)/shard_map/ppermute | solution.py:456
  97.0 4.4 %collective-permute-done.12.refs_3_ = bf16[1024,128]{1,0:T(8,128)(2,1)S(1)} collective-permute-done((bf16[1024,128]{1,0:T(8,128)(2,1)S(1)}, bf16[1024,128]{1,0:T(8,128)(2,1)S(1)}, u32[]{:S(2)}, u32[]{:S(2)}) %collective-permute-start.12) | collective-permute-done | bytes 262176 | tf_op jit(solution)/shard_map/ppermute | solution.py:585
  101.5 1.7 stream.5
  103.2 1.6 collective-permute-start.13
  104.8 1.0 collective-permute-start.15
  106.0 18.3 %collective-permute-start.14 = (bf16[1536,128]{1,0:T(8,128)(2,1)S(1)}, bf16[1536,128]{1,0:T(8,128)(2,1)S(1)}, u32[]{:S(2)}, u32[]{:S(2)}) collective-permute-start(bf16[1536,128]{1,0:T(8,128)(2,1)S(1)} %get-tuple-element.64.refs_0_), channel_id=1, source_target_pairs={{0,8},{4,12},{8,0},{12,4},{16,24},{20,28},{24,16},{28,20},{1,9},{5... | collective-permute-start | bytes 1179656 | tf_op jit(solution)/shard_map/ppermute | solution.py:456
  124.4 7.2 %collide.12.refs_11_ = f32[1728,256]{1,0:T(8,128)S(1)} custom-call(s32[1]{0:T(128)} %bitcast.8.chips_ref, s32[1]{0:T(128)} %bitcast.4.core_ref, bf16[1536,128]{1,0:T(8,128)(2,1)S(1)} %get-tuple-element.64.refs_0_, bf16[1920,128]{1,0:T(8,128)(2,1)S(1)} %get-tuple-element.63.refs_1_, bf16[1536,128]{1,0:T(8,128)(2,1)S(1)} %collective-permute-done.16.refs_2_, ...), custom_call_target="tpu_custom_call" | custom-call | flops 1024 | bytes 1024 | tf_op jit(solution)/shard_map/collide/pallas_call | solution.py:314
  131.5 5.5 %collective-permute-done.14.refs_0_ = bf16[1536,128]{1,0:T(8,128)(2,1)S(1)} collective-permute-done((bf16[1536,128]{1,0:T(8,128)(2,1)S(1)}, bf16[1536,128]{1,0:T(8,128)(2,1)S(1)}, u32[]{:S(2)}, u32[]{:S(2)}) %collective-permute-start.14) | collective-permute-done | bytes 393248 | tf_op jit(solution)/shard_map/ppermute | solution.py:456
  137.3 1.3 collective-permute-start.18
  139.2 0.5 collective-permute-start.19
  139.7 1.8 collective-permute-done.21.refs_7_
  141.6 1.3 collective-permute-done.22.refs_8_
  142.9 13.2 %collide.13.refs_3_ = f32[1728,256]{1,0:T(8,128)S(1)} custom-call(s32[2]{0:T(128)S(1)} %pad_add_fusion.chips_ref, s32[1]{0:T(128)} %bitcast.4.core_ref, bf16[1536,128]{1,0:T(8,128)(2,1)S(1)} %collective-permute-done.14.refs_0_, bf16[1920,128]{1,0:T(8,128)(2,1)S(1)} %collective-permute-done.15.refs_1_, bf16[1536,128]{1,0:T(8,128)(2,1)S(1)} %collective-permute-done.19.refs_2_, ...), custom_call_target="tpu_custom_call" | custom-call | flops 1024 | bytes 1024 | tf_op jit(solution)/shard_map/collide/pallas_call | solution.py:314
  156.1 2.6 %collective-permute-done.18.refs_0_ = bf16[3456,128]{1,0:T(8,128)(2,1)S(1)} collective-permute-done((bf16[3456,128]{1,0:T(8,128)(2,1)S(1)}, bf16[3456,128]{1,0:T(8,128)(2,1)S(1)}, u32[]{:S(2)}, u32[]{:S(2)}) %collective-permute-start.18) | collective-permute-done | bytes 884768 | tf_op jit(solution)/shard_map/ppermute | solution.py:456
  158.7 2.4 %collective-permute-done.24.refs_1_ = bf16[3456,128]{1,0:T(8,128)(2,1)S(1)} collective-permute-done((bf16[3456,128]{1,0:T(8,128)(2,1)S(1)}, bf16[3456,128]{1,0:T(8,128)(2,1)S(1)}, u32[]{:S(2)}, u32[]{:S(2)}) %collective-permute-start.24) | collective-permute-done | bytes 884768 | tf_op jit(solution)/shard_map/ppermute | solution.py:460
  161.1 5.6 %collide.14 = (bf16[1024,128]{1,0:T(8,128)(2,1)S(1)}, bf16[1024,128]{1,0:T(8,128)(2,1)S(1)}, f32[8,128]{1,0:T(8,128)S(1)}) custom-call(s32[1]{0:T(128)} %bitcast.3.chips_ref, s32[1]{0:T(128)} %bitcast.4.core_ref, bf16[3456,128]{1,0:T(8,128)(2,1)S(1)} %collective-permute-done.18.refs_0_, bf16[3456,128]{1,0:T(8,128)(2,1)S(1)} %collective-permute-done.24.refs_1_, ...), custom_call_target="tpu_custom_call" | custom-call | flops 1024 | bytes 1024 | tf_op jit(solution)/shard_map/collide/pallas_call | solution.py:314
  166.7 1.5 collective-permute-start.27
  168.2 1.5 collective-permute-start.28
  169.7 4.9 %collide.15 = (bf16[768,128]{1,0:T(8,128)(2,1)S(1)}, bf16[768,128]{1,0:T(8,128)(2,1)S(1)}, f32[8,128]{1,0:T(8,128)}) custom-call(s32[1]{0:T(128)} %bitcast.3.chips_ref, s32[1]{0:T(128)} %bitcast.4.core_ref, bf16[3456,128]{1,0:T(8,128)(2,1)S(1)} %collective-permute-done.18.refs_0_, bf16[3456,128]{1,0:T(8,128)(2,1)S(1)} %collective-permute-done.24.refs_1_, ...), custom_call_target="tpu_custom_call" | custom-call | flops 1024 | bytes 1024 | tf_op jit(solution)/shard_map/collide/pallas_call | solution.py:314
  174.7 1.3 totals.1
  176.0 0.8 collective-permute-done.27.refs_0_
  177.0 0.6 collective-permute-start.29
  177.8 2.3 %collective-permute-start.30 = (f32[1,8,16]{2,1,0:T(8,128)S(1)}, f32[1,8,16]{2,1,0:T(8,128)S(1)}, u32[]{:S(2)}, u32[]{:S(2)}) collective-permute-start(f32[1,8,16]{2,1,0:T(8,128)S(1)} %reshape.32), channel_id=1, source_target_pairs={{1,0},{2,1},{3,2},{0,3},{5,4},{6,5},{7,6},{4,7},{9,8},{10,9},{11,1... | collective-permute-start | bytes 1544 | tf_op jit(solution)/shard_map/ppermute | solution.py:549
  180.2 2.9 %collective-permute-start.26 = (bf16[768,128]{1,0:T(8,128)(2,1)S(1)}, bf16[768,128]{1,0:T(8,128)(2,1)S(1)}, u32[]{:S(2)}, u32[]{:S(2)}) collective-permute-start(bf16[768,128]{1,0:T(8,128)(2,1)S(1)} %get-tuple-element.75.refs_2_.refs_1_), channel_id=1, source_target_pairs={{1,0},{2,1},{3,2},{0,3},{5,4},{6,5},{7,6},{4,7},{9,8},{10,9},{11,1... | collective-permute-start | bytes 589832 | tf_op jit(solution)/shard_map/ppermute | solution.py:585
  183.5 1.1 stream.6.refs_4_
  184.6 1.5 collective-permute-start.32
  186.1 1.7 collective-permute-start.33
  187.9 1.2 collective-permute-start.34
  189.5 1.8 stream.7
  191.3 2.0 %collective-permute-done.34 = f32[2,8,16]{2,1,0:T(8,128)S(1)} collective-permute-done((f32[2,8,16]{2,1,0:T(8,128)S(1)}, f32[2,8,16]{2,1,0:T(8,128)S(1)}, u32[]{:S(2)}, u32[]{:S(2)}) %collective-permute-start.34) | collective-permute-done | bytes 1056 | tf_op jit(solution)/shard_map/ppermute | solution.py:456
  193.3 0.6 add_multiply_fusion
  (70 shorter events, 3.6 us)
Async XLA Ops:
  0.6 1.2 copy-start.3
  1.8 5.4 %copy-start.8 = (s32[1728]{0:T(1024)S(1)}, s32[1728]{0:T(1024)}, u32[]{:S(2)}) copy-start(s32[1728]{0:T(1024)} %param.8) | copy-start | bytes 20740
  2.0 11.1 %collective-permute-start.2 = (bf16[3456,128]{1,0:T(8,128)(2,1)S(1)}, bf16[3456,128]{1,0:T(8,128)(2,1)S(1)}, u32[]{:S(2)}, u32[]{:S(2)}) collective-permute-start(bf16[3456,128]{1,0:T(8,128)(2,1)S(1)} %pack.1.refs_0_), channel_id=1, source_target_pairs={{0,4},{4,0},{8,12},{12,8},{16,20},{20,16},{24,28},{28,24},{1,5},{5... | collective-permute-start | bytes 2654216 | tf_op jit(solution)/shard_map/ppermute | solution.py:460
  2.5 25.3 %collective-permute-start = (bf16[3456,128]{1,0:T(8,128)(2,1)S(1)}, bf16[3456,128]{1,0:T(8,128)(2,1)S(1)}, u32[]{:S(2)}, u32[]{:S(2)}) collective-permute-start(bf16[3456,128]{1,0:T(8,128)(2,1)S(1)} %pack.1.refs_0_), channel_id=1, source_target_pairs={{0,24},{4,28},{24,0},{28,4},{8,16},{12,20},{16,8},{20,12},{1,25},{... | collective-permute-start | bytes 2654216 | tf_op jit(solution)/shard_map/ppermute | solution.py:456
  7.2 39.3 %collective-permute-start.1 = (bf16[3456,128]{1,0:T(8,128)(2,1)S(1)}, bf16[3456,128]{1,0:T(8,128)(2,1)S(1)}, u32[]{:S(2)}, u32[]{:S(2)}) collective-permute-start(bf16[3456,128]{1,0:T(8,128)(2,1)S(1)} %pack.1.refs_0_), channel_id=1, source_target_pairs={{0,8},{4,12},{8,0},{12,4},{16,24},{20,28},{24,16},{28,20},{1,9},{5... | collective-permute-start | bytes 2654216 | tf_op jit(solution)/shard_map/ppermute | solution.py:456
  19.6 1.2 copy-start
  46.5 3.3 %copy-start.4 = (bf16[3456,128]{1,0:T(8,128)(2,1)}, bf16[3456,128]{1,0:T(8,128)(2,1)S(1)}, u32[]{:S(2)}) copy-start(bf16[3456,128]{1,0:T(8,128)(2,1)S(1)} %collective-permute-done.1.refs_0_) | copy-start | bytes 2654212
  46.5 3.3 %collective-permute-start.4 = (bf16[3456,128]{1,0:T(8,128)(2,1)S(1)}, bf16[3456,128]{1,0:T(8,128)(2,1)S(1)}, u32[]{:S(2)}, u32[]{:S(2)}) collective-permute-start(bf16[3456,128]{1,0:T(8,128)(2,1)S(1)} %collective-permute-done.1.refs_0_), channel_id=1, source_target_pairs={{0,4},{4,0},{8,12},{12,8},{16,20},{20,16},{24,28},{28,24},{1,5},{5... | collective-permute-start | bytes 2654216 | tf_op jit(solution)/shard_map/ppermute | solution.py:460
  46.5 4.2 %collective-permute-start.5 = (bf16[3456,128]{1,0:T(8,128)(2,1)S(1)}, bf16[3456,128]{1,0:T(8,128)(2,1)}, u32[]{:S(2)}, u32[]{:S(2)}) collective-permute-start(bf16[3456,128]{1,0:T(8,128)(2,1)S(1)} %collective-permute-done.refs_2_), channel_id=1, source_target_pairs={{0,4},{4,0},{8,12},{12,8},{16,20},{20,16},{24,28},{28,24},{1,5},{5... | collective-permute-start | bytes 2654216 | tf_op jit(solution)/shard_map/ppermute | solution.py:460
  48.0 21.9 %collective-permute-start.3 = (bf16[3456,128]{1,0:T(8,128)(2,1)}, bf16[3456,128]{1,0:T(8,128)(2,1)}, u32[]{:S(2)}, u32[]{:S(2)}) collective-permute-start(bf16[3456,128]{1,0:T(8,128)(2,1)} %broadcast_select_fusion), channel_id=1, source_target_pairs={{0,16},{4,20},{24,8},{28,12},{16,24},{20,28},{8,0},{12,4},{1,17},{... | collective-permute-start | bytes 2654216 | tf_op jit(solution)/shard_map/ppermute | solution.py:456
  49.8 0.9 copy-start.6
  50.7 1.5 copy-start.1
  52.2 1.2 copy-start.5
  53.4 1.2 copy-start.7
  69.9 2.6 %collective-permute-start.6 = (bf16[3456,128]{1,0:T(8,128)(2,1)}, bf16[3456,128]{1,0:T(8,128)(2,1)S(1)}, u32[]{:S(2)}, u32[]{:S(2)}) collective-permute-start(bf16[3456,128]{1,0:T(8,128)(2,1)} %collective-permute-done.3.refs_0_), channel_id=1, source_target_pairs={{0,4},{4,0},{8,12},{12,8},{16,20},{20,16},{24,28},{28,24},{1,5},{5... | collective-permute-start | bytes 2654216 | tf_op jit(solution)/shard_map/ppermute | solution.py:460
  77.9 11.5 %collective-permute-start.7 = (bf16[768,128]{1,0:T(8,128)(2,1)}, bf16[768,128]{1,0:T(8,128)(2,1)}, u32[]{:S(2)}, u32[]{:S(2)}) collective-permute-start(bf16[768,128]{1,0:T(8,128)(2,1)} %get-tuple-element.54.refs_2_), channel_id=1, source_target_pairs={{0,1},{1,2},{2,3},{3,0},{4,5},{5,6},{6,7},{7,4},{8,9},{9,10},{10,1... | collective-permute-start | bytes 589832 | tf_op jit(solution)/shard_map/ppermute | solution.py:584
  79.4 11.7 %collective-permute-start.8 = (bf16[768,128]{1,0:T(8,128)(2,1)}, bf16[768,128]{1,0:T(8,128)(2,1)}, u32[]{:S(2)}, u32[]{:S(2)}) collective-permute-start(bf16[768,128]{1,0:T(8,128)(2,1)} %get-tuple-element.55.refs_1_), channel_id=1, source_target_pairs={{1,0},{2,1},{3,2},{0,3},{5,4},{6,5},{7,6},{4,7},{9,8},{10,9},{11,1... | collective-permute-start | bytes 589832 | tf_op jit(solution)/shard_map/ppermute | solution.py:585
  80.9 8.4 %copy-start.9 = (s32[256,1]{0,1:T(1,128)S(1)}, s32[256,1]{0,1:T(1,128)}, u32[]{:S(2)}) copy-start(s32[256,1]{0,1:T(1,128)} %reshape.28) | copy-start | bytes 3076
  80.9 10.2 %copy-start.2 = (f32[14,3,128]{2,1,0:T(4,128)S(1)}, f32[14,3,128]{2,1,0:T(4,128)}, u32[]{:S(2)}) copy-start(f32[14,3,128]{2,1,0:T(4,128)} %fusion.speed_ref) | copy-start | bytes 64516
  86.3 10.7 %collective-permute-start.11 = (bf16[1024,128]{1,0:T(8,128)(2,1)S(1)}, bf16[1024,128]{1,0:T(8,128)(2,1)S(1)}, u32[]{:S(2)}, u32[]{:S(2)}) collective-permute-start(bf16[1024,128]{1,0:T(8,128)(2,1)S(1)} %get-tuple-element.60.refs_2_), channel_id=1, source_target_pairs={{0,1},{1,2},{2,3},{3,0},{4,5},{5,6},{6,7},{7,4},{8,9},{9,10},{10,1... | collective-permute-start | bytes 786440 | tf_op jit(solution)/shard_map/ppermute | solution.py:584
  86.9 14.6 %collective-permute-start.12 = (bf16[1024,128]{1,0:T(8,128)(2,1)S(1)}, bf16[1024,128]{1,0:T(8,128)(2,1)S(1)}, u32[]{:S(2)}, u32[]{:S(2)}) collective-permute-start(bf16[1024,128]{1,0:T(8,128)(2,1)S(1)} %get-tuple-element.61.refs_1_), channel_id=1, source_target_pairs={{1,0},{2,1},{3,2},{0,3},{5,4},{6,5},{7,6},{4,7},{9,8},{10,9},{11,1... | collective-permute-start | bytes 786440 | tf_op jit(solution)/shard_map/ppermute | solution.py:585
  93.1 12.6 %collective-permute-start.10 = (bf16[768,128]{1,0:T(8,128)(2,1)S(1)}, bf16[768,128]{1,0:T(8,128)(2,1)S(1)}, u32[]{:S(2)}, u32[]{:S(2)}) collective-permute-start(bf16[768,128]{1,0:T(8,128)(2,1)S(1)} %get-tuple-element.57), channel_id=1, source_target_pairs={{0,24},{4,28},{24,0},{28,4},{8,16},{12,20},{16,8},{20,12},{1,25},{... | collective-permute-start | bytes 589832 | tf_op jit(solution)/shard_map/ppermute | solution.py:456
  94.8 11.2 %collective-permute-start.9 = (bf16[768,128]{1,0:T(8,128)(2,1)S(1)}, bf16[768,128]{1,0:T(8,128)(2,1)S(1)}, u32[]{:S(2)}, u32[]{:S(2)}) collective-permute-start(bf16[768,128]{1,0:T(8,128)(2,1)S(1)} %get-tuple-element.56), channel_id=1, source_target_pairs={{0,24},{4,28},{24,0},{28,4},{8,16},{12,20},{16,8},{20,12},{1,25},{... | collective-permute-start | bytes 589832 | tf_op jit(solution)/shard_map/ppermute | solution.py:456
  103.2 21.2 %collective-permute-start.17 = (bf16[1920,128]{1,0:T(8,128)(2,1)S(1)}, bf16[1920,128]{1,0:T(8,128)(2,1)S(1)}, u32[]{:S(2)}, u32[]{:S(2)}) collective-permute-start(bf16[1920,128]{1,0:T(8,128)(2,1)S(1)} %get-tuple-element.63.refs_1_), channel_id=1, source_target_pairs={{0,4},{4,0},{8,12},{12,8},{16,20},{20,16},{24,28},{28,24},{1,5},{5... | collective-permute-start | bytes 1474568 | tf_op jit(solution)/shard_map/ppermute | solution.py:460
  103.2 33.9 %collective-permute-start.13 = (bf16[1920,128]{1,0:T(8,128)(2,1)S(1)}, bf16[1920,128]{1,0:T(8,128)(2,1)S(1)}, u32[]{:S(2)}, u32[]{:S(2)}) collective-permute-start(bf16[1920,128]{1,0:T(8,128)(2,1)S(1)} %get-tuple-element.63.refs_1_), channel_id=1, source_target_pairs={{0,24},{4,28},{24,0},{28,4},{8,16},{12,20},{16,8},{20,12},{1,25},{... | collective-permute-start | bytes 1474568 | tf_op jit(solution)/shard_map/ppermute | solution.py:456
  104.8 32.3 %collective-permute-start.15 = (bf16[1920,128]{1,0:T(8,128)(2,1)S(1)}, bf16[1920,128]{1,0:T(8,128)(2,1)S(1)}, u32[]{:S(2)}, u32[]{:S(2)}) collective-permute-start(bf16[1920,128]{1,0:T(8,128)(2,1)S(1)} %get-tuple-element.63.refs_1_), channel_id=1, source_target_pairs={{0,8},{4,12},{8,0},{12,4},{16,24},{20,28},{24,16},{28,20},{1,9},{5... | collective-permute-start | bytes 1474568 | tf_op jit(solution)/shard_map/ppermute | solution.py:456
  105.7 18.6 %collective-permute-start.16 = (bf16[1536,128]{1,0:T(8,128)(2,1)S(1)}, bf16[1536,128]{1,0:T(8,128)(2,1)S(1)}, u32[]{:S(2)}, u32[]{:S(2)}) collective-permute-start(bf16[1536,128]{1,0:T(8,128)(2,1)S(1)} %get-tuple-element.64.refs_0_), channel_id=1, source_target_pairs={{0,4},{4,0},{8,12},{12,8},{16,20},{20,16},{24,28},{28,24},{1,5},{5... | collective-permute-start | bytes 1179656 | tf_op jit(solution)/shard_map/ppermute | solution.py:460
  106.0 31.1 %collective-permute-start.14 = (bf16[1536,128]{1,0:T(8,128)(2,1)S(1)}, bf16[1536,128]{1,0:T(8,128)(2,1)S(1)}, u32[]{:S(2)}, u32[]{:S(2)}) collective-permute-start(bf16[1536,128]{1,0:T(8,128)(2,1)S(1)} %get-tuple-element.64.refs_0_), channel_id=1, source_target_pairs={{0,8},{4,12},{8,0},{12,4},{16,24},{20,28},{24,16},{28,20},{1,9},{5... | collective-permute-start | bytes 1179656 | tf_op jit(solution)/shard_map/ppermute | solution.py:456
  137.3 21.3 %collective-permute-start.18 = (bf16[3456,128]{1,0:T(8,128)(2,1)S(1)}, bf16[3456,128]{1,0:T(8,128)(2,1)S(1)}, u32[]{:S(2)}, u32[]{:S(2)}) collective-permute-start(bf16[3456,128]{1,0:T(8,128)(2,1)S(1)} %maximum_select_fusion), channel_id=1, source_target_pairs={{0,16},{4,20},{24,8},{28,12},{16,24},{20,28},{8,0},{12,4},{1,17},{... | collective-permute-start | bytes 2654216 | tf_op jit(solution)/shard_map/ppermute | solution.py:456
  138.6 4.3 %collective-permute-start.20 = (bf16[1920,128]{1,0:T(8,128)(2,1)S(1)}, bf16[1920,128]{1,0:T(8,128)(2,1)S(1)}, u32[]{:S(2)}, u32[]{:S(2)}) collective-permute-start(bf16[1920,128]{1,0:T(8,128)(2,1)S(1)} %collective-permute-done.15.refs_1_), channel_id=1, source_target_pairs={{0,4},{4,0},{8,12},{12,8},{16,20},{20,16},{24,28},{28,24},{1,5},{5... | collective-permute-start | bytes 1474568 | tf_op jit(solution)/shard_map/ppermute | solution.py:460
  138.6 4.3 %collective-permute-start.23 = (bf16[1920,128]{1,0:T(8,128)(2,1)S(1)}, bf16[1920,128]{1,0:T(8,128)(2,1)S(1)}, u32[]{:S(2)}, u32[]{:S(2)}) collective-permute-start(bf16[1920,128]{1,0:T(8,128)(2,1)S(1)} %collective-permute-done.13.refs_6_), channel_id=1, source_target_pairs={{0,4},{4,0},{8,12},{12,8},{16,20},{20,16},{24,28},{28,24},{1,5},{5... | collective-permute-start | bytes 1474568 | tf_op jit(solution)/shard_map/ppermute | solution.py:460
  139.2 2.3 %collective-permute-start.21 = (bf16[768,128]{1,0:T(8,128)(2,1)S(1)}, bf16[768,128]{1,0:T(8,128)(2,1)S(1)}, u32[]{:S(2)}, u32[]{:S(2)}) collective-permute-start(bf16[768,128]{1,0:T(8,128)(2,1)S(1)} %collective-permute-done.9.refs_4_), channel_id=1, source_target_pairs={{0,4},{4,0},{8,12},{12,8},{16,20},{20,16},{24,28},{28,24},{1,5},{5... | collective-permute-start | bytes 589832 | tf_op jit(solution)/shard_map/ppermute | solution.py:460
  139.2 3.8 %collective-permute-start.19 = (bf16[1536,128]{1,0:T(8,128)(2,1)S(1)}, bf16[1536,128]{1,0:T(8,128)(2,1)S(1)}, u32[]{:S(2)}, u32[]{:S(2)}) collective-permute-start(bf16[1536,128]{1,0:T(8,128)(2,1)S(1)} %collective-permute-done.14.refs_0_), channel_id=1, source_target_pairs={{0,4},{4,0},{8,12},{12,8},{16,20},{20,16},{24,28},{28,24},{1,5},{5... | collective-permute-start | bytes 1179656 | tf_op jit(solution)/shard_map/ppermute | solution.py:460
  141.5 1.4 collective-permute-start.22
  158.7 2.4 %collective-permute-start.24 = (bf16[3456,128]{1,0:T(8,128)(2,1)S(1)}, bf16[3456,128]{1,0:T(8,128)(2,1)S(1)}, u32[]{:S(2)}, u32[]{:S(2)}) collective-permute-start(bf16[3456,128]{1,0:T(8,128)(2,1)S(1)} %collective-permute-done.18.refs_0_), channel_id=1, source_target_pairs={{0,4},{4,0},{8,12},{12,8},{16,20},{20,16},{24,28},{28,24},{1,5},{5... | collective-permute-start | bytes 2654216 | tf_op jit(solution)/shard_map/ppermute | solution.py:460
  166.7 10.1 %collective-permute-start.27 = (bf16[1024,128]{1,0:T(8,128)(2,1)S(1)}, bf16[1024,128]{1,0:T(8,128)(2,1)S(1)}, u32[]{:S(2)}, u32[]{:S(2)}) collective-permute-start(bf16[1024,128]{1,0:T(8,128)(2,1)S(1)} %get-tuple-element.73.refs_1_.refs_2_), channel_id=1, source_target_pairs={{0,1},{1,2},{2,3},{3,0},{4,5},{5,6},{6,7},{7,4},{8,9},{9,10},{10,1... | collective-permute-start | bytes 786440 | tf_op jit(solution)/shard_map/ppermute | solution.py:584
  168.2 15.2 %collective-permute-start.28 = (bf16[1024,128]{1,0:T(8,128)(2,1)S(1)}, bf16[1024,128]{1,0:T(8,128)(2,1)S(1)}, u32[]{:S(2)}, u32[]{:S(2)}) collective-permute-start(bf16[1024,128]{1,0:T(8,128)(2,1)S(1)} %get-tuple-element.72.refs_0_.refs_1_), channel_id=1, source_target_pairs={{1,0},{2,1},{3,2},{0,3},{5,4},{6,5},{7,6},{4,7},{9,8},{10,9},{11,1... | collective-permute-start | bytes 786440 | tf_op jit(solution)/shard_map/ppermute | solution.py:585
  177.0 6.4 %collective-permute-start.29 = (f32[1,8,16]{2,1,0:T(8,128)S(1)}, f32[1,8,16]{2,1,0:T(8,128)S(1)}, u32[]{:S(2)}, u32[]{:S(2)}) collective-permute-start(f32[1,8,16]{2,1,0:T(8,128)S(1)} %reshape.31), channel_id=1, source_target_pairs={{0,1},{1,2},{2,3},{3,0},{4,5},{5,6},{6,7},{7,4},{8,9},{9,10},{10,1... | collective-permute-start | bytes 1544 | tf_op jit(solution)/shard_map/ppermute | solution.py:548
  177.8 5.6 %collective-permute-start.30 = (f32[1,8,16]{2,1,0:T(8,128)S(1)}, f32[1,8,16]{2,1,0:T(8,128)S(1)}, u32[]{:S(2)}, u32[]{:S(2)}) collective-permute-start(f32[1,8,16]{2,1,0:T(8,128)S(1)} %reshape.32), channel_id=1, source_target_pairs={{1,0},{2,1},{3,2},{0,3},{5,4},{6,5},{7,6},{4,7},{9,8},{10,9},{11,1... | collective-permute-start | bytes 1544 | tf_op jit(solution)/shard_map/ppermute | solution.py:549
  180.2 8.8 %collective-permute-start.25 = (bf16[768,128]{1,0:T(8,128)(2,1)S(1)}, bf16[768,128]{1,0:T(8,128)(2,1)S(1)}, u32[]{:S(2)}, u32[]{:S(2)}) collective-permute-start(bf16[768,128]{1,0:T(8,128)(2,1)S(1)} %get-tuple-element.76.refs_3_.refs_2_), channel_id=1, source_target_pairs={{0,1},{1,2},{2,3},{3,0},{4,5},{5,6},{6,7},{7,4},{8,9},{9,10},{10,1... | collective-permute-start | bytes 589832 | tf_op jit(solution)/shard_map/ppermute | solution.py:584
  180.2 9.3 %collective-permute-start.26 = (bf16[768,128]{1,0:T(8,128)(2,1)S(1)}, bf16[768,128]{1,0:T(8,128)(2,1)S(1)}, u32[]{:S(2)}, u32[]{:S(2)}) collective-permute-start(bf16[768,128]{1,0:T(8,128)(2,1)S(1)} %get-tuple-element.75.refs_2_.refs_1_), channel_id=1, source_target_pairs={{1,0},{2,1},{3,2},{0,3},{5,4},{6,5},{7,6},{4,7},{9,8},{10,9},{11,1... | collective-permute-start | bytes 589832 | tf_op jit(solution)/shard_map/ppermute | solution.py:585
  183.4 1.2 collective-permute-start.31
  184.6 6.7 %collective-permute-start.32 = (f32[2,8,16]{2,1,0:T(8,128)S(1)}, f32[2,8,16]{2,1,0:T(8,128)S(1)}, u32[]{:S(2)}, u32[]{:S(2)}) collective-permute-start(f32[2,8,16]{2,1,0:T(8,128)S(1)} %add.51), channel_id=1, source_target_pairs={{0,8},{4,12},{8,0},{12,4},{16,24},{20,28},{24,16},{28,20},{1,9},{5... | collective-permute-start | bytes 3080 | tf_op jit(solution)/shard_map/ppermute | solution.py:456
  186.1 5.2 %collective-permute-start.33 = (f32[2,8,16]{2,1,0:T(8,128)S(1)}, f32[2,8,16]{2,1,0:T(8,128)S(1)}, u32[]{:S(2)}, u32[]{:S(2)}) collective-permute-start(f32[2,8,16]{2,1,0:T(8,128)S(1)} %add.51), channel_id=1, source_target_pairs={{0,16},{4,20},{16,0},{20,4},{8,24},{12,28},{24,8},{28,12},{1,17},{... | collective-permute-start | bytes 3080 | tf_op jit(solution)/shard_map/ppermute | solution.py:456
  187.9 5.4 %collective-permute-start.34 = (f32[2,8,16]{2,1,0:T(8,128)S(1)}, f32[2,8,16]{2,1,0:T(8,128)S(1)}, u32[]{:S(2)}, u32[]{:S(2)}) collective-permute-start(f32[2,8,16]{2,1,0:T(8,128)S(1)} %add.51), channel_id=1, source_target_pairs={{0,24},{4,28},{24,0},{28,4},{8,16},{12,20},{16,8},{20,12},{1,25},{... | collective-permute-start | bytes 3080 | tf_op jit(solution)/shard_map/ppermute | solution.py:456

commit v5 on v3

--- a/solution.py
+++ b/solution.py
@@ -539,8 +539,8 @@
     part = part.reshape(planes, height, depth) + jnp.where(free, ends, 0.0)
     part = part + other_core(part)
     part, _ = tied(part, second)
-    others = [along(part, pairs) for pairs in (NEAR, TWO, FAR)]
-    part = part + (others[0] + (others[1] + others[2]))
+    for pairs in (NEAR, TWO):
+        part = part + along(part, pairs)
     return part / jnp.sqrt(jnp.float32(V))
 
 

time: 194 us -> 194 us (level)
    ppermute x13 -> x12, waiting for transfers between devices: 36.8 us -> 37.6 us  [along(): return lax.ppermute(block, 'vel', perm)]
    ppermute x13 -> x12, starting transfers between devices: 36.1 us -> 35.4 us  [along(): return lax.ppermute(block, 'vel', perm)]
  transfers between devices with their start and end apart: 38 -> 37, of which waited for: 18 -> 18; matrix products, arithmetic and copies ran while one was open for 4% -> 4% of each run, Pallas kernels for 30% -> 30%
where the time goes in v5:
time: 194 us; the launch traced here: 193 us
  Pallas kernels  68.6 us (35%)
  waiting for transfers between devices  54.6 us (28%)
  starting transfers between devices  53.2 us (27%)
  local copies, waits for them, and re-layouts  11 us (6%)
  other arithmetic  5.08 us (3%)
    pallas_call x8, Pallas kernels, matmul(): pl.pallas_call(functools.partial(matmul_kernel, count, pieces, cells, loc...  60.6 us
    ppermute x12, waiting for transfers between devices, along(): return lax.ppermute(block, 'vel', perm)  37.6 us
    ppermute x12, starting transfers between devices, along(): return lax.ppermute(block, 'vel', perm)  35.4 us
    ppermute x15, waiting for transfers between devices, other_core(): return lax.ppermute(block, 'vel', [(i, i ^ 1) for i in range(8)])  10.1 us
    ppermute x4, starting transfers between devices, halo(): high = lax.ppermute(relaxed[0], 'space', backward)  8.17 us
    unnamed x22, local copies, waits for them, and re-layouts  7.2 us
    pallas_call x4, Pallas kernels, stream(): pl.pallas_call(functools.partial(stream_kernel, part, shape, final), out_...  6.57 us
    ppermute x4, waiting for transfers between devices, halo(): high = lax.ppermute(relaxed[0], 'space', backward)  6.13 us
  transfers between devices with their start and end apart: 37, of which 18 were waited for; matrix products, arithmetic and copies ran while one was open for 4% of the time, Pallas kernels for 30%

profile of v5, /device:TPU:0, one launch (start us, length us, event | category | flops | bytes accessed | tf_op | source)
XLA Modules:
  0.0 193.5 jit_solution(1993135644404142873)
XLA Ops:
  0.6 1.2 copy-done.3
  2.5 4.7 %collective-permute-start = (bf16[3456,128]{1,0:T(8,128)(2,1)S(1)}, bf16[3456,128]{1,0:T(8,128)(2,1)S(1)}, u32[]{:S(2)}, u32[]{:S(2)}) collective-permute-start(bf16[3456,128]{1,0:T(8,128)(2,1)S(1)} %pack.1.refs_0_), channel_id=1, source_target_pairs={{0,24},{4,28},{24,0},{28,4},{8,16},{12,20},{16,8},{20,12},{1,25},{... | collective-permute-start | bytes 2654216 | tf_op jit(solution)/shard_map/ppermute | solution.py:442
  7.2 0.6 stack.37
  7.8 0.6 stack.38
  8.4 1.3 convert_element_type.20
  9.7 0.7 compare_select_fusion
  10.4 0.7 reshape.28
  11.1 0.7 bitcast_convert_fusion.inflow_ref
  11.8 1.3 fusion.speed_ref
  13.1 6.5 %collide.8.refs_5_ = f32[1728,256]{1,0:T(8,128)S(1)} custom-call(s32[1]{0:T(128)} %bitcast.5.chips_ref, s32[1]{0:T(128)} %bitcast.4.core_ref, bf16[3456,128]{1,0:T(8,128)(2,1)S(1)} %pack.1.refs_0_, bf16[3456,128]{1,0:T(8,128)(2,1)S(1)} %collective-permute-done.2.refs_1_, bf16[1728,13824]{1,0:T(8,128)(2,1)} %refs_2_.9), custom_call_target="tpu_custom_call" | custom-call | flops 1024 | bytes 1024 | tf_op jit(solution)/shard_map/collide/pallas_call | solution.py:312
  19.6 1.2 copy-done
  20.9 6.9 %collective-permute-done.refs_2_ = bf16[3456,128]{1,0:T(8,128)(2,1)S(1)} collective-permute-done((bf16[3456,128]{1,0:T(8,128)(2,1)S(1)}, bf16[3456,128]{1,0:T(8,128)(2,1)S(1)}, u32[]{:S(2)}, u32[]{:S(2)}) %collective-permute-start) | collective-permute-done | bytes 884768 | tf_op jit(solution)/shard_map/ppermute | solution.py:442
  27.8 18.7 %collective-permute-done.1.refs_0_ = bf16[3456,128]{1,0:T(8,128)(2,1)S(1)} collective-permute-done((bf16[3456,128]{1,0:T(8,128)(2,1)S(1)}, bf16[3456,128]{1,0:T(8,128)(2,1)S(1)}, u32[]{:S(2)}, u32[]{:S(2)}) %collective-permute-start.1) | collective-permute-done | bytes 884768 | tf_op jit(solution)/shard_map/ppermute | solution.py:442
  47.0 1.0 broadcast_select_fusion
  48.0 0.6 collective-permute-start.3
  48.7 1.1 collective-permute-done.4.refs_1_
  49.8 0.9 copy-done.6
  50.7 1.5 copy-done.1
  52.2 1.2 copy-done.5
  53.4 1.2 copy-done.7
  54.5 11.2 %collide.9.refs_3_ = f32[1728,256]{1,0:T(8,128)S(1)} custom-call(s32[2]{0:T(128)S(1)} %pad_add_fusion.chips_ref, s32[1]{0:T(128)} %bitcast.4.core_ref, bf16[3456,128]{1,0:T(8,128)(2,1)S(1)} %copy-done.5, bf16[3456,128]{1,0:T(8,128)(2,1)S(1)} %copy-done.7, bf16[3456,128]{1,0:T(8,128)(2,1)S(1)} %collective-permute-done.refs_2_, ...), custom_call_target="tpu_custom_call" | custom-call | flops 1024 | bytes 1024 | tf_op jit(solution)/shard_map/collide/pallas_call | solution.py:312
  65.8 4.1 %collective-permute-done.3.refs_0_ = bf16[3456,128]{1,0:T(8,128)(2,1)} collective-permute-done((bf16[3456,128]{1,0:T(8,128)(2,1)}, bf16[3456,128]{1,0:T(8,128)(2,1)}, u32[]{:S(2)}, u32[]{:S(2)}) %collective-permute-start.3) | collective-permute-done | bytes 884768 | tf_op jit(solution)/shard_map/ppermute | solution.py:442
  69.9 2.6 %collective-permute-done.6.refs_1_ = bf16[3456,128]{1,0:T(8,128)(2,1)S(1)} collective-permute-done((bf16[3456,128]{1,0:T(8,128)(2,1)}, bf16[3456,128]{1,0:T(8,128)(2,1)S(1)}, u32[]{:S(2)}, u32[]{:S(2)}) %collective-permute-start.6) | collective-permute-done | bytes 884768 | tf_op jit(solution)/shard_map/ppermute | solution.py:446
  72.5 5.3 %collide.10 = (bf16[768,128]{1,0:T(8,128)(2,1)}, bf16[768,128]{1,0:T(8,128)(2,1)}, f32[8,128]{1,0:T(8,128)S(1)}) custom-call(s32[1]{0:T(128)} %bitcast.3.chips_ref, s32[1]{0:T(128)} %bitcast.4.core_ref, bf16[3456,128]{1,0:T(8,128)(2,1)} %collective-permute-done.3.refs_0_, bf16[3456,128]{1,0:T(8,128)(2,1)S(1)} %collective-permute-done.6.refs_1_, ...), custom_call_target="tpu_custom_call" | custom-call | flops 1024 | bytes 1024 | tf_op jit(solution)/shard_map/collide/pallas_call | solution.py:312
  77.9 1.5 collective-permute-start.7
  79.4 1.4 collective-permute-start.8
  80.9 5.4 %collide.11 = (bf16[1024,128]{1,0:T(8,128)(2,1)S(1)}, bf16[1024,128]{1,0:T(8,128)(2,1)S(1)}, f32[8,128]{1,0:T(8,128)S(1)}) custom-call(s32[1]{0:T(128)} %bitcast.3.chips_ref, s32[1]{0:T(128)} %bitcast.4.core_ref, bf16[3456,128]{1,0:T(8,128)(2,1)} %collective-permute-done.3.refs_0_, bf16[3456,128]{1,0:T(8,128)(2,1)S(1)} %collective-permute-done.6.refs_1_, ...), custom_call_target="tpu_custom_call" | custom-call | flops 1024 | bytes 1024 | tf_op jit(solution)/shard_map/collide/pallas_call | solution.py:312
  86.3 0.6 collective-permute-start.11
  86.9 2.3 %collective-permute-start.12 = (bf16[1024,128]{1,0:T(8,128)(2,1)S(1)}, bf16[1024,128]{1,0:T(8,128)(2,1)S(1)}, u32[]{:S(2)}, u32[]{:S(2)}) collective-permute-start(bf16[1024,128]{1,0:T(8,128)(2,1)S(1)} %get-tuple-element.61.refs_1_), channel_id=1, source_target_pairs={{1,0},{2,1},{3,2},{0,3},{5,4},{6,5},{7,6},{4,7},{9,8},{10,9},{11,1... | collective-permute-start | bytes 786440 | tf_op jit(solution)/shard_map/ppermute | solution.py:571
  89.4 1.7 collective-permute-done.8.refs_3_
  91.1 2.0 %stream.4 = (bf16[768,128]{1,0:T(8,128)(2,1)S(1)}, bf16[768,128]{1,0:T(8,128)(2,1)S(1)}, f32[8,128]{1,0:T(8,128)S(1)}) custom-call(f32[8,128]{1,0:T(8,128)S(1)} %get-tuple-element.53._, f32[14,3,128]{2,1,0:T(4,128)S(1)} %copy-done.2, f32[14,1,128]{2,1,0:T(1,128)S(1)} %bitcast_convert_fusion.inflow_ref, s32[256,1]{1,0:T(8,128)S(1)} %copy.10.code_ref, ...), custom_call_target="tpu_custom_call" | custom-call | flops 1024 | bytes 1024 | tf_op jit(solution)/shard_map/stream/pallas_call | solution.py:423
  93.1 1.7 collective-permute-start.10
  94.8 2.2 %collective-permute-start.9 = (bf16[768,128]{1,0:T(8,128)(2,1)S(1)}, bf16[768,128]{1,0:T(8,128)(2,1)S(1)}, u32[]{:S(2)}, u32[]{:S(2)}) collective-permute-start(bf16[768,128]{1,0:T(8,128)(2,1)S(1)} %get-tuple-element.56.refs_0_), channel_id=1, source_target_pairs={{0,24},{4,28},{24,0},{28,4},{8,16},{12,20},{16,8},{20,12},{1,25},{... | collective-permute-start | bytes 589832 | tf_op jit(solution)/shard_map/ppermute | solution.py:442
  97.0 4.5 %collective-permute-done.12.refs_3_ = bf16[1024,128]{1,0:T(8,128)(2,1)S(1)} collective-permute-done((bf16[1024,128]{1,0:T(8,128)(2,1)S(1)}, bf16[1024,128]{1,0:T(8,128)(2,1)S(1)}, u32[]{:S(2)}, u32[]{:S(2)}) %collective-permute-start.12) | collective-permute-done | bytes 262176 | tf_op jit(solution)/shard_map/ppermute | solution.py:571
  101.5 1.6 stream.5
  103.1 1.6 collective-permute-start.13
  104.7 1.0 collective-permute-start.16
  106.3 0.9 collective-permute-done.17.refs_3_
  107.1 17.2 %collective-permute-start.14 = (bf16[768,128]{1,0:T(8,128)(2,1)S(1)}, bf16[768,128]{1,0:T(8,128)(2,1)S(1)}, u32[]{:S(2)}, u32[]{:S(2)}) collective-permute-start(bf16[768,128]{1,0:T(8,128)(2,1)S(1)} %get-tuple-element.56.refs_0_), channel_id=1, source_target_pairs={{0,8},{4,12},{8,0},{12,4},{16,24},{20,28},{24,16},{28,20},{1,9},{5... | collective-permute-start | bytes 589832 | tf_op jit(solution)/shard_map/ppermute | solution.py:442
  124.4 1.3 collective-permute-start.15
  125.8 7.8 %collide.12.refs_13_ = f32[1728,256]{1,0:T(8,128)S(1)} custom-call(s32[1]{0:T(128)} %bitcast.8.chips_ref, s32[1]{0:T(128)} %bitcast.4.core_ref, bf16[768,128]{1,0:T(8,128)(2,1)S(1)} %get-tuple-element.56.refs_0_, bf16[768,128]{1,0:T(8,128)(2,1)S(1)} %get-tuple-element.57.refs_1_, bf16[1920,128]{1,0:T(8,128)(2,1)S(1)} %get-tuple-element.63.refs_2_, ...), custom_call_target="tpu_custom_call" | custom-call | flops 1024 | bytes 1024 | tf_op jit(solution)/shard_map/collide/pallas_call | solution.py:312
  133.6 3.4 %collective-permute-done.15.refs_1_ = bf16[768,128]{1,0:T(8,128)(2,1)S(1)} collective-permute-done((bf16[768,128]{1,0:T(8,128)(2,1)S(1)}, bf16[768,128]{1,0:T(8,128)(2,1)S(1)}, u32[]{:S(2)}, u32[]{:S(2)}) %collective-permute-start.15) | collective-permute-done | bytes 196640 | tf_op jit(solution)/shard_map/ppermute | solution.py:442
  137.3 1.3 collective-permute-start.20
  139.7 1.8 collective-permute-done.24.refs_9_
  142.0 0.9 collective-permute-done.21.refs_3_
  143.2 13.8 %collide.13.refs_3_ = f32[1728,256]{1,0:T(8,128)S(1)} custom-call(s32[2]{0:T(128)S(1)} %pad_add_fusion.chips_ref, s32[1]{0:T(128)} %bitcast.4.core_ref, bf16[768,128]{1,0:T(8,128)(2,1)S(1)} %collective-permute-done.14.refs_0_, bf16[768,128]{1,0:T(8,128)(2,1)S(1)} %collective-permute-done.15.refs_1_, bf16[1920,128]{1,0:T(8,128)(2,1)S(1)} %collective-permute-done.16.refs_2_, ...), custom_call_target="tpu_custom_call" | custom-call | flops 1024 | bytes 1024 | tf_op jit(solution)/shard_map/collide/pallas_call | solution.py:312
  157.0 1.6 collective-permute-done.20.refs_0_
  158.7 2.4 %collective-permute-done.27.refs_1_ = bf16[3456,128]{1,0:T(8,128)(2,1)S(1)} collective-permute-done((bf16[3456,128]{1,0:T(8,128)(2,1)S(1)}, bf16[3456,128]{1,0:T(8,128)(2,1)S(1)}, u32[]{:S(2)}, u32[]{:S(2)}) %collective-permute-start.27) | collective-permute-done | bytes 884768 | tf_op jit(solution)/shard_map/ppermute | solution.py:446
  161.1 5.6 %collide.14 = (bf16[1024,128]{1,0:T(8,128)(2,1)S(1)}, bf16[1024,128]{1,0:T(8,128)(2,1)S(1)}, f32[8,128]{1,0:T(8,128)S(1)}) custom-call(s32[1]{0:T(128)} %bitcast.3.chips_ref, s32[1]{0:T(128)} %bitcast.4.core_ref, bf16[3456,128]{1,0:T(8,128)(2,1)S(1)} %collective-permute-done.20.refs_0_, bf16[3456,128]{1,0:T(8,128)(2,1)S(1)} %collective-permute-done.27.refs_1_, ...), custom_call_target="tpu_custom_call" | custom-call | flops 1024 | bytes 1024 | tf_op jit(solution)/shard_map/collide/pallas_call | solution.py:312
  166.7 1.5 collective-permute-start.30
  168.2 1.5 collective-permute-start.31
  169.7 4.9 %collide.15 = (bf16[768,128]{1,0:T(8,128)(2,1)S(1)}, bf16[768,128]{1,0:T(8,128)(2,1)S(1)}, f32[8,128]{1,0:T(8,128)}) custom-call(s32[1]{0:T(128)} %bitcast.3.chips_ref, s32[1]{0:T(128)} %bitcast.4.core_ref, bf16[3456,128]{1,0:T(8,128)(2,1)S(1)} %collective-permute-done.20.refs_0_, bf16[3456,128]{1,0:T(8,128)(2,1)S(1)} %collective-permute-done.27.refs_1_, ...), custom_call_target="tpu_custom_call" | custom-call | flops 1024 | bytes 1024 | tf_op jit(solution)/shard_map/collide/pallas_call | solution.py:312
  174.7 1.3 totals.1
  176.0 0.7 collective-permute-done.30.refs_0_
  177.0 0.6 collective-permute-start.32
  177.8 2.3 %collective-permute-start.33 = (f32[1,8,16]{2,1,0:T(8,128)S(1)}, f32[1,8,16]{2,1,0:T(8,128)S(1)}, u32[]{:S(2)}, u32[]{:S(2)}) collective-permute-start(f32[1,8,16]{2,1,0:T(8,128)S(1)} %reshape.32), channel_id=1, source_target_pairs={{1,0},{2,1},{3,2},{0,3},{5,4},{6,5},{7,6},{4,7},{9,8},{10,9},{11,1... | collective-permute-start | bytes 1544 | tf_op jit(solution)/shard_map/ppermute | solution.py:535
  180.2 2.9 %collective-permute-start.29 = (bf16[768,128]{1,0:T(8,128)(2,1)S(1)}, bf16[768,128]{1,0:T(8,128)(2,1)S(1)}, u32[]{:S(2)}, u32[]{:S(2)}) collective-permute-start(bf16[768,128]{1,0:T(8,128)(2,1)S(1)} %get-tuple-element.75.refs_2_.refs_1_), channel_id=1, source_target_pairs={{1,0},{2,1},{3,2},{0,3},{5,4},{6,5},{7,6},{4,7},{9,8},{10,9},{11,1... | collective-permute-start | bytes 589832 | tf_op jit(solution)/shard_map/ppermute | solution.py:571
  183.5 1.1 stream.6.refs_4_
  184.6 1.5 collective-permute-start.35
  186.2 2.2 %collective-permute-done.35 = f32[2,8,16]{2,1,0:T(8,128)S(1)} collective-permute-done((f32[2,8,16]{2,1,0:T(8,128)S(1)}, f32[2,8,16]{2,1,0:T(8,128)S(1)}, u32[]{:S(2)}, u32[]{:S(2)}) %collective-permute-start.35) | collective-permute-done | bytes 1056 | tf_op jit(solution)/shard_map/ppermute | solution.py:442
  188.3 2.2 %collective-permute-start.36 = (f32[2,8,16]{2,1,0:T(8,128)S(1)}, f32[2,8,16]{2,1,0:T(8,128)S(1)}, u32[]{:S(2)}, u32[]{:S(2)}) collective-permute-start(f32[2,8,16]{2,1,0:T(8,128)S(1)} %add.49), channel_id=1, source_target_pairs={{0,16},{4,20},{16,0},{20,4},{8,24},{12,28},{24,8},{28,12},{1,17},{... | collective-permute-start | bytes 3080 | tf_op jit(solution)/shard_map/ppermute | solution.py:442
  190.5 1.8 stream.7
  192.3 0.6 collective-permute-done.36
  192.9 0.6 add_multiply_fusion
  (76 shorter events, 5.1 us)
Async XLA Ops:
  0.6 1.2 copy-start.3
  1.8 5.4 %copy-start.8 = (s32[1728]{0:T(1024)S(1)}, s32[1728]{0:T(1024)}, u32[]{:S(2)}) copy-start(s32[1728]{0:T(1024)} %param.8) | copy-start | bytes 20740
  2.0 11.2 %collective-permute-start.2 = (bf16[3456,128]{1,0:T(8,128)(2,1)S(1)}, bf16[3456,128]{1,0:T(8,128)(2,1)S(1)}, u32[]{:S(2)}, u32[]{:S(2)}) collective-permute-start(bf16[3456,128]{1,0:T(8,128)(2,1)S(1)} %pack.1.refs_0_), channel_id=1, source_target_pairs={{0,4},{4,0},{8,12},{12,8},{16,20},{20,16},{24,28},{28,24},{1,5},{5... | collective-permute-start | bytes 2654216 | tf_op jit(solution)/shard_map/ppermute | solution.py:446
  2.5 25.3 %collective-permute-start = (bf16[3456,128]{1,0:T(8,128)(2,1)S(1)}, bf16[3456,128]{1,0:T(8,128)(2,1)S(1)}, u32[]{:S(2)}, u32[]{:S(2)}) collective-permute-start(bf16[3456,128]{1,0:T(8,128)(2,1)S(1)} %pack.1.refs_0_), channel_id=1, source_target_pairs={{0,24},{4,28},{24,0},{28,4},{8,16},{12,20},{16,8},{20,12},{1,25},{... | collective-permute-start | bytes 2654216 | tf_op jit(solution)/shard_map/ppermute | solution.py:442
  7.2 39.3 %collective-permute-start.1 = (bf16[3456,128]{1,0:T(8,128)(2,1)S(1)}, bf16[3456,128]{1,0:T(8,128)(2,1)S(1)}, u32[]{:S(2)}, u32[]{:S(2)}) collective-permute-start(bf16[3456,128]{1,0:T(8,128)(2,1)S(1)} %pack.1.refs_0_), channel_id=1, source_target_pairs={{0,8},{4,12},{8,0},{12,4},{16,24},{20,28},{24,16},{28,20},{1,9},{5... | collective-permute-start | bytes 2654216 | tf_op jit(solution)/shard_map/ppermute | solution.py:442
  19.6 1.2 copy-start
  46.5 3.3 %copy-start.4 = (bf16[3456,128]{1,0:T(8,128)(2,1)}, bf16[3456,128]{1,0:T(8,128)(2,1)S(1)}, u32[]{:S(2)}) copy-start(bf16[3456,128]{1,0:T(8,128)(2,1)S(1)} %collective-permute-done.1.refs_0_) | copy-start | bytes 2654212
  46.5 3.3 %collective-permute-start.4 = (bf16[3456,128]{1,0:T(8,128)(2,1)S(1)}, bf16[3456,128]{1,0:T(8,128)(2,1)S(1)}, u32[]{:S(2)}, u32[]{:S(2)}) collective-permute-start(bf16[3456,128]{1,0:T(8,128)(2,1)S(1)} %collective-permute-done.1.refs_0_), channel_id=1, source_target_pairs={{0,4},{4,0},{8,12},{12,8},{16,20},{20,16},{24,28},{28,24},{1,5},{5... | collective-permute-start | bytes 2654216 | tf_op jit(solution)/shard_map/ppermute | solution.py:446
  46.5 4.2 %collective-permute-start.5 = (bf16[3456,128]{1,0:T(8,128)(2,1)S(1)}, bf16[3456,128]{1,0:T(8,128)(2,1)}, u32[]{:S(2)}, u32[]{:S(2)}) collective-permute-start(bf16[3456,128]{1,0:T(8,128)(2,1)S(1)} %collective-permute-done.refs_2_), channel_id=1, source_target_pairs={{0,4},{4,0},{8,12},{12,8},{16,20},{20,16},{24,28},{28,24},{1,5},{5... | collective-permute-start | bytes 2654216 | tf_op jit(solution)/shard_map/ppermute | solution.py:446
  48.0 21.9 %collective-permute-start.3 = (bf16[3456,128]{1,0:T(8,128)(2,1)}, bf16[3456,128]{1,0:T(8,128)(2,1)}, u32[]{:S(2)}, u32[]{:S(2)}) collective-permute-start(bf16[3456,128]{1,0:T(8,128)(2,1)} %broadcast_select_fusion), channel_id=1, source_target_pairs={{0,16},{4,20},{24,8},{28,12},{16,24},{20,28},{8,0},{12,4},{1,17},{... | collective-permute-start | bytes 2654216 | tf_op jit(solution)/shard_map/ppermute | solution.py:442
  49.8 0.9 copy-start.6
  50.7 1.5 copy-start.1
  52.2 1.2 copy-start.5
  53.4 1.2 copy-start.7
  69.9 2.6 %collective-permute-start.6 = (bf16[3456,128]{1,0:T(8,128)(2,1)}, bf16[3456,128]{1,0:T(8,128)(2,1)S(1)}, u32[]{:S(2)}, u32[]{:S(2)}) collective-permute-start(bf16[3456,128]{1,0:T(8,128)(2,1)} %collective-permute-done.3.refs_0_), channel_id=1, source_target_pairs={{0,4},{4,0},{8,12},{12,8},{16,20},{20,16},{24,28},{28,24},{1,5},{5... | collective-permute-start | bytes 2654216 | tf_op jit(solution)/shard_map/ppermute | solution.py:446
  77.9 11.5 %collective-permute-start.7 = (bf16[768,128]{1,0:T(8,128)(2,1)}, bf16[768,128]{1,0:T(8,128)(2,1)}, u32[]{:S(2)}, u32[]{:S(2)}) collective-permute-start(bf16[768,128]{1,0:T(8,128)(2,1)} %get-tuple-element.54.refs_2_), channel_id=1, source_target_pairs={{0,1},{1,2},{2,3},{3,0},{4,5},{5,6},{6,7},{7,4},{8,9},{9,10},{10,1... | collective-permute-start | bytes 589832 | tf_op jit(solution)/shard_map/ppermute | solution.py:570
  79.4 11.7 %collective-permute-start.8 = (bf16[768,128]{1,0:T(8,128)(2,1)}, bf16[768,128]{1,0:T(8,128)(2,1)}, u32[]{:S(2)}, u32[]{:S(2)}) collective-permute-start(bf16[768,128]{1,0:T(8,128)(2,1)} %get-tuple-element.55.refs_1_), channel_id=1, source_target_pairs={{1,0},{2,1},{3,2},{0,3},{5,4},{6,5},{7,6},{4,7},{9,8},{10,9},{11,1... | collective-permute-start | bytes 589832 | tf_op jit(solution)/shard_map/ppermute | solution.py:571
  80.9 8.4 %copy-start.9 = (s32[256,1]{0,1:T(1,128)S(1)}, s32[256,1]{0,1:T(1,128)}, u32[]{:S(2)}) copy-start(s32[256,1]{0,1:T(1,128)} %reshape.28) | copy-start | bytes 3076
  80.9 10.2 %copy-start.2 = (f32[14,3,128]{2,1,0:T(4,128)S(1)}, f32[14,3,128]{2,1,0:T(4,128)}, u32[]{:S(2)}) copy-start(f32[14,3,128]{2,1,0:T(4,128)} %fusion.speed_ref) | copy-start | bytes 64516
  86.3 10.7 %collective-permute-start.11 = (bf16[1024,128]{1,0:T(8,128)(2,1)S(1)}, bf16[1024,128]{1,0:T(8,128)(2,1)S(1)}, u32[]{:S(2)}, u32[]{:S(2)}) collective-permute-start(bf16[1024,128]{1,0:T(8,128)(2,1)S(1)} %get-tuple-element.60.refs_2_), channel_id=1, source_target_pairs={{0,1},{1,2},{2,3},{3,0},{4,5},{5,6},{6,7},{7,4},{8,9},{9,10},{10,1... | collective-permute-start | bytes 786440 | tf_op jit(solution)/shard_map/ppermute | solution.py:570
  86.9 14.6 %collective-permute-start.12 = (bf16[1024,128]{1,0:T(8,128)(2,1)S(1)}, bf16[1024,128]{1,0:T(8,128)(2,1)S(1)}, u32[]{:S(2)}, u32[]{:S(2)}) collective-permute-start(bf16[1024,128]{1,0:T(8,128)(2,1)S(1)} %get-tuple-element.61.refs_1_), channel_id=1, source_target_pairs={{1,0},{2,1},{3,2},{0,3},{5,4},{6,5},{7,6},{4,7},{9,8},{10,9},{11,1... | collective-permute-start | bytes 786440 | tf_op jit(solution)/shard_map/ppermute | solution.py:571
  93.1 12.6 %collective-permute-start.10 = (bf16[768,128]{1,0:T(8,128)(2,1)S(1)}, bf16[768,128]{1,0:T(8,128)(2,1)S(1)}, u32[]{:S(2)}, u32[]{:S(2)}) collective-permute-start(bf16[768,128]{1,0:T(8,128)(2,1)S(1)} %get-tuple-element.57.refs_1_), channel_id=1, source_target_pairs={{0,24},{4,28},{24,0},{28,4},{8,16},{12,20},{16,8},{20,12},{1,25},{... | collective-permute-start | bytes 589832 | tf_op jit(solution)/shard_map/ppermute | solution.py:442
  94.8 11.1 %collective-permute-start.9 = (bf16[768,128]{1,0:T(8,128)(2,1)S(1)}, bf16[768,128]{1,0:T(8,128)(2,1)S(1)}, u32[]{:S(2)}, u32[]{:S(2)}) collective-permute-start(bf16[768,128]{1,0:T(8,128)(2,1)S(1)} %get-tuple-element.56.refs_0_), channel_id=1, source_target_pairs={{0,24},{4,28},{24,0},{28,4},{8,16},{12,20},{16,8},{20,12},{1,25},{... | collective-permute-start | bytes 589832 | tf_op jit(solution)/shard_map/ppermute | solution.py:442
  103.1 22.6 %collective-permute-start.19 = (bf16[1920,128]{1,0:T(8,128)(2,1)S(1)}, bf16[1920,128]{1,0:T(8,128)(2,1)S(1)}, u32[]{:S(2)}, u32[]{:S(2)}) collective-permute-start(bf16[1920,128]{1,0:T(8,128)(2,1)S(1)} %get-tuple-element.63.refs_2_), channel_id=1, source_target_pairs={{0,4},{4,0},{8,12},{12,8},{16,20},{20,16},{24,28},{28,24},{1,5},{5... | collective-permute-start | bytes 1474568 | tf_op jit(solution)/shard_map/ppermute | solution.py:446
  103.1 33.9 %collective-permute-start.13 = (bf16[1920,128]{1,0:T(8,128)(2,1)S(1)}, bf16[1920,128]{1,0:T(8,128)(2,1)S(1)}, u32[]{:S(2)}, u32[]{:S(2)}) collective-permute-start(bf16[1920,128]{1,0:T(8,128)(2,1)S(1)} %get-tuple-element.63.refs_2_), channel_id=1, source_target_pairs={{0,24},{4,28},{24,0},{28,4},{8,16},{12,20},{16,8},{20,12},{1,25},{... | collective-permute-start | bytes 1474568 | tf_op jit(solution)/shard_map/ppermute | solution.py:442
  104.7 32.3 %collective-permute-start.16 = (bf16[1920,128]{1,0:T(8,128)(2,1)S(1)}, bf16[1920,128]{1,0:T(8,128)(2,1)S(1)}, u32[]{:S(2)}, u32[]{:S(2)}) collective-permute-start(bf16[1920,128]{1,0:T(8,128)(2,1)S(1)} %get-tuple-element.63.refs_2_), channel_id=1, source_target_pairs={{0,8},{4,12},{8,0},{12,4},{16,24},{20,28},{24,16},{28,20},{1,9},{5... | collective-permute-start | bytes 1474568 | tf_op jit(solution)/shard_map/ppermute | solution.py:442
  105.7 1.4 collective-permute-start.17
  105.9 18.5 %collective-permute-start.18 = (bf16[768,128]{1,0:T(8,128)(2,1)S(1)}, bf16[768,128]{1,0:T(8,128)(2,1)S(1)}, u32[]{:S(2)}, u32[]{:S(2)}) collective-permute-start(bf16[768,128]{1,0:T(8,128)(2,1)S(1)} %get-tuple-element.57.refs_1_), channel_id=1, source_target_pairs={{0,4},{4,0},{8,12},{12,8},{16,20},{20,16},{24,28},{28,24},{1,5},{5... | collective-permute-start | bytes 589832 | tf_op jit(solution)/shard_map/ppermute | solution.py:446
  107.1 26.5 %collective-permute-start.14 = (bf16[768,128]{1,0:T(8,128)(2,1)S(1)}, bf16[768,128]{1,0:T(8,128)(2,1)S(1)}, u32[]{:S(2)}, u32[]{:S(2)}) collective-permute-start(bf16[768,128]{1,0:T(8,128)(2,1)S(1)} %get-tuple-element.56.refs_0_), channel_id=1, source_target_pairs={{0,8},{4,12},{8,0},{12,4},{16,24},{20,28},{24,16},{28,20},{1,9},{5... | collective-permute-start | bytes 589832 | tf_op jit(solution)/shard_map/ppermute | solution.py:442
  124.4 12.7 %collective-permute-start.15 = (bf16[768,128]{1,0:T(8,128)(2,1)S(1)}, bf16[768,128]{1,0:T(8,128)(2,1)S(1)}, u32[]{:S(2)}, u32[]{:S(2)}) collective-permute-start(bf16[768,128]{1,0:T(8,128)(2,1)S(1)} %get-tuple-element.57.refs_1_), channel_id=1, source_target_pairs={{0,8},{4,12},{8,0},{12,4},{16,24},{20,28},{24,16},{28,20},{1,9},{5... | collective-permute-start | bytes 589832 | tf_op jit(solution)/shard_map/ppermute | solution.py:442
  137.3 21.3 %collective-permute-start.20 = (bf16[3456,128]{1,0:T(8,128)(2,1)S(1)}, bf16[3456,128]{1,0:T(8,128)(2,1)S(1)}, u32[]{:S(2)}, u32[]{:S(2)}) collective-permute-start(bf16[3456,128]{1,0:T(8,128)(2,1)S(1)} %maximum_select_fusion), channel_id=1, source_target_pairs={{0,16},{4,20},{24,8},{28,12},{16,24},{20,28},{8,0},{12,4},{1,17},{... | collective-permute-start | bytes 2654216 | tf_op jit(solution)/shard_map/ppermute | solution.py:442
  138.6 4.6 %collective-permute-start.23 = (bf16[1920,128]{1,0:T(8,128)(2,1)S(1)}, bf16[1920,128]{1,0:T(8,128)(2,1)S(1)}, u32[]{:S(2)}, u32[]{:S(2)}) collective-permute-start(bf16[1920,128]{1,0:T(8,128)(2,1)S(1)} %collective-permute-done.16.refs_2_), channel_id=1, source_target_pairs={{0,4},{4,0},{8,12},{12,8},{16,20},{20,16},{24,28},{28,24},{1,5},{5... | collective-permute-start | bytes 1474568 | tf_op jit(solution)/shard_map/ppermute | solution.py:446
  138.6 4.6 %collective-permute-start.26 = (bf16[1920,128]{1,0:T(8,128)(2,1)S(1)}, bf16[1920,128]{1,0:T(8,128)(2,1)S(1)}, u32[]{:S(2)}, u32[]{:S(2)}) collective-permute-start(bf16[1920,128]{1,0:T(8,128)(2,1)S(1)} %collective-permute-done.13.refs_8_), channel_id=1, source_target_pairs={{0,4},{4,0},{8,12},{12,8},{16,20},{20,16},{24,28},{28,24},{1,5},{5... | collective-permute-start | bytes 1474568 | tf_op jit(solution)/shard_map/ppermute | solution.py:446
  139.2 2.3 %collective-permute-start.24 = (bf16[768,128]{1,0:T(8,128)(2,1)S(1)}, bf16[768,128]{1,0:T(8,128)(2,1)S(1)}, u32[]{:S(2)}, u32[]{:S(2)}) collective-permute-start(bf16[768,128]{1,0:T(8,128)(2,1)S(1)} %collective-permute-done.9.refs_6_), channel_id=1, source_target_pairs={{0,4},{4,0},{8,12},{12,8},{16,20},{20,16},{24,28},{28,24},{1,5},{5... | collective-permute-start | bytes 589832 | tf_op jit(solution)/shard_map/ppermute | solution.py:446
  139.2 2.6 %collective-permute-start.25 = (bf16[768,128]{1,0:T(8,128)(2,1)S(1)}, bf16[768,128]{1,0:T(8,128)(2,1)S(1)}, u32[]{:S(2)}, u32[]{:S(2)}) collective-permute-start(bf16[768,128]{1,0:T(8,128)(2,1)S(1)} %collective-permute-done.10.refs_7_), channel_id=1, source_target_pairs={{0,4},{4,0},{8,12},{12,8},{16,20},{20,16},{24,28},{28,24},{1,5},{5... | collective-permute-start | bytes 589832 | tf_op jit(solution)/shard_map/ppermute | solution.py:446
  141.5 1.4 collective-permute-start.21
  141.8 1.4 collective-permute-start.22
  158.7 2.4 %collective-permute-start.27 = (bf16[3456,128]{1,0:T(8,128)(2,1)S(1)}, bf16[3456,128]{1,0:T(8,128)(2,1)S(1)}, u32[]{:S(2)}, u32[]{:S(2)}) collective-permute-start(bf16[3456,128]{1,0:T(8,128)(2,1)S(1)} %collective-permute-done.20.refs_0_), channel_id=1, source_target_pairs={{0,4},{4,0},{8,12},{12,8},{16,20},{20,16},{24,28},{28,24},{1,5},{5... | collective-permute-start | bytes 2654216 | tf_op jit(solution)/shard_map/ppermute | solution.py:446
  166.7 10.1 %collective-permute-start.30 = (bf16[1024,128]{1,0:T(8,128)(2,1)S(1)}, bf16[1024,128]{1,0:T(8,128)(2,1)S(1)}, u32[]{:S(2)}, u32[]{:S(2)}) collective-permute-start(bf16[1024,128]{1,0:T(8,128)(2,1)S(1)} %get-tuple-element.73.refs_1_.refs_2_), channel_id=1, source_target_pairs={{0,1},{1,2},{2,3},{3,0},{4,5},{5,6},{6,7},{7,4},{8,9},{9,10},{10,1... | collective-permute-start | bytes 786440 | tf_op jit(solution)/shard_map/ppermute | solution.py:570
  168.2 15.2 %collective-permute-start.31 = (bf16[1024,128]{1,0:T(8,128)(2,1)S(1)}, bf16[1024,128]{1,0:T(8,128)(2,1)S(1)}, u32[]{:S(2)}, u32[]{:S(2)}) collective-permute-start(bf16[1024,128]{1,0:T(8,128)(2,1)S(1)} %get-tuple-element.72.refs_0_.refs_1_), channel_id=1, source_target_pairs={{1,0},{2,1},{3,2},{0,3},{5,4},{6,5},{7,6},{4,7},{9,8},{10,9},{11,1... | collective-permute-start | bytes 786440 | tf_op jit(solution)/shard_map/ppermute | solution.py:571
  177.0 6.4 %collective-permute-start.32 = (f32[1,8,16]{2,1,0:T(8,128)S(1)}, f32[1,8,16]{2,1,0:T(8,128)S(1)}, u32[]{:S(2)}, u32[]{:S(2)}) collective-permute-start(f32[1,8,16]{2,1,0:T(8,128)S(1)} %reshape.31), channel_id=1, source_target_pairs={{0,1},{1,2},{2,3},{3,0},{4,5},{5,6},{6,7},{7,4},{8,9},{9,10},{10,1... | collective-permute-start | bytes 1544 | tf_op jit(solution)/shard_map/ppermute | solution.py:534
  177.8 5.6 %collective-permute-start.33 = (f32[1,8,16]{2,1,0:T(8,128)S(1)}, f32[1,8,16]{2,1,0:T(8,128)S(1)}, u32[]{:S(2)}, u32[]{:S(2)}) collective-permute-start(f32[1,8,16]{2,1,0:T(8,128)S(1)} %reshape.32), channel_id=1, source_target_pairs={{1,0},{2,1},{3,2},{0,3},{5,4},{6,5},{7,6},{4,7},{9,8},{10,9},{11,1... | collective-permute-start | bytes 1544 | tf_op jit(solution)/shard_map/ppermute | solution.py:535
  180.2 10.3 %collective-permute-start.28 = (bf16[768,128]{1,0:T(8,128)(2,1)S(1)}, bf16[768,128]{1,0:T(8,128)(2,1)S(1)}, u32[]{:S(2)}, u32[]{:S(2)}) collective-permute-start(bf16[768,128]{1,0:T(8,128)(2,1)S(1)} %get-tuple-element.76.refs_3_.refs_2_), channel_id=1, source_target_pairs={{0,1},{1,2},{2,3},{3,0},{4,5},{5,6},{6,7},{7,4},{8,9},{9,10},{10,1... | collective-permute-start | bytes 589832 | tf_op jit(solution)/shard_map/ppermute | solution.py:570
  180.2 10.3 %collective-permute-start.29 = (bf16[768,128]{1,0:T(8,128)(2,1)S(1)}, bf16[768,128]{1,0:T(8,128)(2,1)S(1)}, u32[]{:S(2)}, u32[]{:S(2)}) collective-permute-start(bf16[768,128]{1,0:T(8,128)(2,1)S(1)} %get-tuple-element.75.refs_2_.refs_1_), channel_id=1, source_target_pairs={{1,0},{2,1},{3,2},{0,3},{5,4},{6,5},{7,6},{4,7},{9,8},{10,9},{11,1... | collective-permute-start | bytes 589832 | tf_op jit(solution)/shard_map/ppermute | solution.py:571
  183.4 1.2 collective-permute-start.34
  184.6 3.7 %collective-permute-start.35 = (f32[2,8,16]{2,1,0:T(8,128)S(1)}, f32[2,8,16]{2,1,0:T(8,128)S(1)}, u32[]{:S(2)}, u32[]{:S(2)}) collective-permute-start(f32[2,8,16]{2,1,0:T(8,128)S(1)} %add.48), channel_id=1, source_target_pairs={{0,8},{4,12},{8,0},{12,4},{16,24},{20,28},{24,16},{28,20},{1,9},{5... | collective-permute-start | bytes 3080 | tf_op jit(solution)/shard_map/ppermute | solution.py:442
  188.3 4.5 %collective-permute-start.36 = (f32[2,8,16]{2,1,0:T(8,128)S(1)}, f32[2,8,16]{2,1,0:T(8,128)S(1)}, u32[]{:S(2)}, u32[]{:S(2)}) collective-permute-start(f32[2,8,16]{2,1,0:T(8,128)S(1)} %add.49), channel_id=1, source_target_pairs={{0,16},{4,20},{16,0},{20,4},{8,24},{12,28},{24,8},{28,12},{1,17},{... | collective-permute-start | bytes 3080 | tf_op jit(solution)/shard_map/ppermute | solution.py:442
